TPU v7x, 512 devices: a whole 4x4x16 slice. The times are simulated.
512 devices in a mesh: gx: 8 (over y, core), gy: 4 (over x), gz: 16 (over z).
Axes of the slice: x: 4, y: 4, z: 16, core: 2. Of those that a mesh axis runs over, the one named last changes fastest.
Arguments:
- volume: bfloat16 [256, 512, 4096], P('gz', 'gx', 'gy'), may hold values from 0 to 1
- knot_bins: int32 [8], replicated, may hold values from 0 to 255, as said below
- tf_colour: float32 [3, 8], replicated, may hold values from 0 to 1
- tf_density: float32 [8], replicated, may hold values from 0.1 to 10
Outputs:
- image: float32 [3, 512, 4096], P(None, ('gx', 'gz'), 'gy')
- coverage: float32 [512, 4096], P(('gx', 'gz'), 'gy')
Inputs may be any that keep to these rules, and one draw needn't show every extreme that they name: `knot_bins`: strictly increasing; the first is 0 and the last is 255.
All inputs are finite; a program needn't handle non-finite values.
Results may differ from a plain program's by a relative error of at most 0.0003.
Values may be sent and summed in bfloat16 or wider, within the bound.
No kernel may reach another device: no remote copies, remote signals or barrier semaphores. Data moves between devices by JAX's collectives and lax.ppermute only.
A program may use at most 64 MiB of HBM per device.

v0:
```python
import jax
import jax.numpy as jnp
from jax import lax
from jax.sharding import PartitionSpec as P

BINS = 256


LIGHT_X = 1.0 / 3.0
LIGHT_Y = 2.0 / 3.0
LIGHT_Z = 2.0 / 3.0
AMBIENT = 0.2


def padded_2(x, sides, width):
    for axis, dim in sides:
        count, length = (lax.axis_size(axis), x.shape[dim])
        up = [(i, (i + 1) % count) for i in range(count - 1)]
        down = [(j, i) for i, j in up]
        last = lax.slice_in_dim(x, length - width, length, axis=dim)
        initial = lax.slice_in_dim(x, 0, width, axis=dim)
        before = lax.ppermute(last, axis, up)
        after = lax.ppermute(initial, axis, down)
        x = jnp.concatenate([before, x, after], axis=dim)
    return x


def classify(window, knot_bins, tf_colour, tf_density, depth_total):
    center = window[1:-1, 1:-1, 1:-1]
    grad_x = window[1:-1, 2:, 1:-1] - window[1:-1, :-2, 1:-1]
    grad_y = window[1:-1, 1:-1, 2:] - window[1:-1, 1:-1, :-2]
    grad_z = window[2:, 1:-1, 1:-1] - window[:-2, 1:-1, 1:-1]
    facing = jnp.abs(LIGHT_X * grad_x + LIGHT_Y * grad_y + LIGHT_Z * grad_z)
    shading = AMBIENT + (1.0 - AMBIENT) * facing / jnp.sqrt(
        grad_x * grad_x + grad_y * grad_y + grad_z * grad_z + 1.0
    )
    scalar = center * (BINS - 1.0)
    knots = knot_bins.astype(jnp.float32)
    spans = knots[1:] - knots[:-1]
    ramp_terms = jnp.clip(
        scalar[None] - knots[:-1, None, None, None], 0.0, spans[:, None, None, None]
    )
    table = jnp.concatenate([tf_colour, tf_density[None]], 0)
    slopes = (table[:, 1:] - table[:, :-1]) / spans[None]
    mapped = table[:, :1, None, None] + jnp.einsum(
        "kzxy,ck->czxy", ramp_terms, slopes, precision=lax.Precision.HIGHEST
    )
    opacity_step = 1.0 - jnp.exp(-mapped[3] / depth_total)
    emitted = mapped[:3] * shading[None]
    return (opacity_step, emitted)


def over_rule(front_part, rear_part):
    colour = front_part[:3] + front_part[3:4] * rear_part[:3]
    transmit = front_part[3:4] * rear_part[3:4]
    return jnp.concatenate([colour, transmit], 0)


def on_device(volume, knot_bins, tf_colour, tf_density):
    depth_cells, rows_x, rows_y = volume.shape
    depth_count = lax.axis_size("gz")
    depth_total = float(depth_cells * depth_count)
    padded = padded_2(volume, (("gx", 1), ("gy", 2), ("gz", 0)), 1)
    planes = 4
    slab_count = depth_cells // planes

    def advance(carry, slab_index):
        colour, transmit = carry
        offset = slab_index * planes
        window = lax.dynamic_slice_in_dim(padded, offset, planes + 2, 0).astype(jnp.float32)
        opacity_step, emitted = classify(window, knot_bins, tf_colour, tf_density, depth_total)
        for plane in range(planes):
            colour = colour + transmit[None] * opacity_step[plane][None] * emitted[:, plane]
            transmit = transmit * (1.0 - opacity_step[plane])
        return ((colour, transmit), None)

    start = (jnp.zeros((3, rows_x, rows_y), jnp.float32), jnp.ones((rows_x, rows_y), jnp.float32))
    (colour, transmit), _ = lax.scan(advance, start, jnp.arange(slab_count, dtype=jnp.int32))
    partial_image = jnp.concatenate([colour, transmit[None]], 0)
    band_rows = rows_x // depth_count
    received = lax.all_to_all(partial_image[None], "gz", split_axis=2, concat_axis=0, tiled=True)

    def compose(running, piece):
        return (over_rule(running, piece), None)

    initial = jnp.concatenate(
        [
            jnp.zeros((3, band_rows, rows_y), jnp.float32),
            jnp.ones((1, band_rows, rows_y), jnp.float32),
        ],
        0,
    )
    result, _ = lax.scan(compose, initial, received)
    return (result[:3], 1.0 - result[3])


def solution(mesh):
    placed = (P("gz", "gx", "gy"), P(), P(), P())
    return jax.shard_map(
        on_device,
        mesh=mesh,
        in_specs=placed,
        out_specs=(P(None, ("gx", "gz"), "gy"), P(("gx", "gz"), "gy")),
        check_vma=False,
    )
```

profile of v0, /device:TPU:16, one launch (start us, length us, event | category | flops | bytes accessed | tf_op | source)
XLA Modules:
  0.0 202.9 jit_solution(16948502057925717696)
XLA Ops:
  3.7 3.6 %collective-permute-start.1 = (bf16[16,1,1024]{2,1,0:T(2,128)(2,1)S(1)}, bf16[16,1,1024]{2,1,0:T(2,128)(2,1)S(1)}, u32[]{:S(2)}, u32[]{:S(2)}) collective-permute-start(bf16[16,1,1024]{2,1,0:T(2,128)(2,1)S(1)} %get-tuple-element.195), channel_id=1, source_target_pairs={{64,0},{128,64},{192,128},{256,192},{320,256},{384,320},{448,384},... | collective-permute-start | bytes 98312 | tf_op jit(solution)/shard_map/ppermute | solution.py:23
  9.2 2.8 %pad_maximum_fusion.2 = bf16[16,66,1024]{2,1,0:T(8,128)(2,1)S(1)} fusion(bf16[16,1,1024]{2,1,0:T(2,128)(2,1)S(1)} %collective-permute-done.1, bf16[16,64,1024]{2,1,0:T(8,128)(2,1)} %param.8, bf16[16,1,1024]{2,1,0:T(2,128)(2,1)S(1)} %collective-permute-done), kind=kLoop, calls=%fused_computation.61 | loop fusion | flops 6488064 | bytes 4325376 | tf_op jit(solution)/shard_map/concatenate | solution.py:24
  13.1 4.1 %collective-permute-start.2 = (bf16[16,66,1]{2,1,0:T(8,128)(2,1)}, bf16[16,66,1]{2,1,0:T(8,128)(2,1)}, u32[]{:S(2)}, u32[]{:S(2)}) collective-permute-start(bf16[16,66,1]{2,1,0:T(8,128)(2,1)} %get-tuple-element.193), channel_id=1, source_target_pairs={{0,16},{16,32},{32,48},{1,17},{17,33},{33,49},{2,18},{18,34},{34,5... | collective-permute-start | bytes 6344 | tf_op jit(solution)/shard_map/ppermute | solution.py:22
  18.7 5.1 %collective-permute-done.2 = bf16[16,66,1]{2,1,0:T(8,128)(2,1)} collective-permute-done((bf16[16,66,1]{2,1,0:T(8,128)(2,1)}, bf16[16,66,1]{2,1,0:T(8,128)(2,1)}, u32[]{:S(2)}, u32[]{:S(2)}) %collective-permute-start.2) | collective-permute-done | bytes 2144 | tf_op jit(solution)/shard_map/ppermute | solution.py:22
  23.8 5.3 %collective-permute-done.3 = bf16[16,66,1]{2,1,0:T(8,128)(2,1)} collective-permute-done((bf16[16,66,1]{2,1,0:T(8,128)(2,1)}, bf16[16,66,1]{2,1,0:T(8,128)(2,1)}, u32[]{:S(2)}, u32[]{:S(2)}) %collective-permute-start.3) | collective-permute-done | bytes 2144 | tf_op jit(solution)/shard_map/ppermute | solution.py:23
  29.1 5.4 %concatenate.22 = bf16[16,66,1026]{2,1,0:T(8,128)(2,1)} concatenate(bf16[16,66,1]{2,1,0:T(8,128)(2,1)} %collective-permute-done.2, bf16[16,66,1024]{2,1,0:T(8,128)(2,1)S(1)} %pad_maximum_fusion.2, bf16[16,66,1]{2,1,0:T(8,128)(2,1)} %collective-permute-done.3), dimensions={2} | concatenate | bytes 4333824 | tf_op jit(solution)/shard_map/concatenate | solution.py:24
  35.5 3.8 %collective-permute-start.4 = (bf16[1,66,1026]{2,1,0:T(8,128)(2,1)S(1)}, bf16[1,66,1026]{2,1,0:T(8,128)(2,1)S(1)}, u32[]{:S(2)}, u32[]{:S(2)}) collective-permute-start(bf16[1,66,1026]{2,1,0:T(8,128)(2,1)S(1)} %get-tuple-element.190), channel_id=1, source_target_pairs={{0,1},{1,2},{2,3},{3,4},{4,5},{5,6},{6,7},{7,8},{8,9},{9,10},{10,1... | collective-permute-start | bytes 406304 | tf_op jit(solution)/shard_map/ppermute | solution.py:22
  40.7 2.4 %collective-permute-done.4 = bf16[1,66,1026]{2,1,0:T(8,128)(2,1)S(1)} collective-permute-done((bf16[1,66,1026]{2,1,0:T(8,128)(2,1)S(1)}, bf16[1,66,1026]{2,1,0:T(8,128)(2,1)S(1)}, u32[]{:S(2)}, u32[]{:S(2)}) %collective-permute-start.4) | collective-permute-done | bytes 135464 | tf_op jit(solution)/shard_map/ppermute | solution.py:22
  43.1 4.3 %collective-permute-done.5 = bf16[1,66,1026]{2,1,0:T(8,128)(2,1)S(1)} collective-permute-done((bf16[1,66,1026]{2,1,0:T(8,128)(2,1)S(1)}, bf16[1,66,1026]{2,1,0:T(8,128)(2,1)S(1)}, u32[]{:S(2)}, u32[]{:S(2)}) %collective-permute-start.5) | collective-permute-done | bytes 135464 | tf_op jit(solution)/shard_map/ppermute | solution.py:23
  47.4 3.9 %pad_maximum_fusion.1 = bf16[18,66,1026]{2,1,0:T(8,128)(2,1)} fusion(bf16[1,66,1026]{2,1,0:T(8,128)(2,1)S(1)} %collective-permute-done.5, bf16[16,66,1026]{2,1,0:T(8,128)(2,1)} %concatenate.22, bf16[1,66,1026]{2,1,0:T(8,128)(2,1)S(1)} %collective-permute-done.4), kind=kLoop, calls=%fused_computation.60 | loop fusion | flops 2437776 | bytes 4875552 | tf_op jit(solution)/shard_map/concatenate | solution.py:24
  51.2 82.0 %while.26 = (s32[]{:T(128)}, f32[3,64,1024]{2,1,0:T(8,128)S(1)}, f32[64,1024]{1,0:T(8,128)S(1)}, f32[4,8]{0,1:T(8,128)S(1)}, f32[7]{0:T(128)S(1)}, /*index=5*/f3...) while((s32[]{:T(128)}, f32[3,64,1024]{2,1,0:T(8,128)S(1)}, ...), condition=%wide.region_1.2_spmd.clone, body=%wide.region_0.1_spmd.clone.sunk | while | flops 104543040 | bytes 79246440 | solution.py:78
  55.5 8.0 %fusion.44 = f32[4,4,64,1024]{3,0,2,1:T(4,128)S(1)} fusion(f32[7]{0:T(128)S(1)} %bitcast.191, f32[4,64,1024]{2,1,0:T(8,128)S(1)} %get-tuple-element.284, f32[7]{0:T(128)S(1)} %get-tuple-element.322, f32[4,7]{1,0:T(4,128)S(1)} %get-tuple-element.323), kind=kOutput, calls=%fused_computation.7.clone.1 | convolution fusion | flops 93585440 | bytes 5243048 | tf_op jit(solution)/shard_map/while/body/eval_jaxpr/kzxy,ck->czxy/dot_general | solution.py:45
  63.6 2.4 %copy_add_fusion.2 = f32[4,4,64,1024]{3,2,1,0:T(8,128)S(1)} fusion(f32[4,4,64,1024]{3,0,2,1:T(4,128)S(1)} %fusion.44, f32[4]{0:T(128)S(1)} %slice_bitcast_fusion.13), kind=kLoop, calls=%fused_computation.11.clone.1 | loop fusion | flops 1048576 | bytes 8388624 | tf_op jit(solution)/shard_map/while/body/eval_jaxpr/add | solution.py:45
  68.4 1.9 copy-done.1
  76.0 8.0 %fusion.44 = f32[4,4,64,1024]{3,0,2,1:T(4,128)S(1)} fusion(f32[7]{0:T(128)S(1)} %bitcast.191, f32[4,64,1024]{2,1,0:T(8,128)S(1)} %get-tuple-element.284, f32[7]{0:T(128)S(1)} %get-tuple-element.322, f32[4,7]{1,0:T(4,128)S(1)} %get-tuple-element.323), kind=kOutput, calls=%fused_computation.7.clone.1 | convolution fusion | flops 93585440 | bytes 5243048 | tf_op jit(solution)/shard_map/while/body/eval_jaxpr/kzxy,ck->czxy/dot_general | solution.py:45
  84.1 2.4 %copy_add_fusion.2 = f32[4,4,64,1024]{3,2,1,0:T(8,128)S(1)} fusion(f32[4,4,64,1024]{3,0,2,1:T(4,128)S(1)} %fusion.44, f32[4]{0:T(128)S(1)} %slice_bitcast_fusion.13), kind=kLoop, calls=%fused_computation.11.clone.1 | loop fusion | flops 1048576 | bytes 8388624 | tf_op jit(solution)/shard_map/while/body/eval_jaxpr/add | solution.py:45
  88.9 1.9 copy-done.1
  96.5 8.0 %fusion.44 = f32[4,4,64,1024]{3,0,2,1:T(4,128)S(1)} fusion(f32[7]{0:T(128)S(1)} %bitcast.191, f32[4,64,1024]{2,1,0:T(8,128)S(1)} %get-tuple-element.284, f32[7]{0:T(128)S(1)} %get-tuple-element.322, f32[4,7]{1,0:T(4,128)S(1)} %get-tuple-element.323), kind=kOutput, calls=%fused_computation.7.clone.1 | convolution fusion | flops 93585440 | bytes 5243048 | tf_op jit(solution)/shard_map/while/body/eval_jaxpr/kzxy,ck->czxy/dot_general | solution.py:45
  104.6 2.4 %copy_add_fusion.2 = f32[4,4,64,1024]{3,2,1,0:T(8,128)S(1)} fusion(f32[4,4,64,1024]{3,0,2,1:T(4,128)S(1)} %fusion.44, f32[4]{0:T(128)S(1)} %slice_bitcast_fusion.13), kind=kLoop, calls=%fused_computation.11.clone.1 | loop fusion | flops 1048576 | bytes 8388624 | tf_op jit(solution)/shard_map/while/body/eval_jaxpr/add | solution.py:45
  109.4 1.9 copy-done.1
  117.0 8.0 %fusion.44 = f32[4,4,64,1024]{3,0,2,1:T(4,128)S(1)} fusion(f32[7]{0:T(128)S(1)} %bitcast.191, f32[4,64,1024]{2,1,0:T(8,128)S(1)} %get-tuple-element.284, f32[7]{0:T(128)S(1)} %get-tuple-element.322, f32[4,7]{1,0:T(4,128)S(1)} %get-tuple-element.323), kind=kOutput, calls=%fused_computation.7.clone.1 | convolution fusion | flops 93585440 | bytes 5243048 | tf_op jit(solution)/shard_map/while/body/eval_jaxpr/kzxy,ck->czxy/dot_general | solution.py:45
  125.1 2.4 %copy_add_fusion.2 = f32[4,4,64,1024]{3,2,1,0:T(8,128)S(1)} fusion(f32[4,4,64,1024]{3,0,2,1:T(4,128)S(1)} %fusion.44, f32[4]{0:T(128)S(1)} %slice_bitcast_fusion.13), kind=kLoop, calls=%fused_computation.11.clone.1 | loop fusion | flops 1048576 | bytes 8388624 | tf_op jit(solution)/shard_map/while/body/eval_jaxpr/add | solution.py:45
  135.4 14.9 %all-to-all-start = ((f32[1,4,64,1024]{3,1,0,2:T(4,128)}), f32[1,4,64,1024]{3,1,0,2:T(4,128)S(1)}, u32[]{:S(2)}, u32[]{:S(2)}) async-start(f32[1,4,64,1024]{3,1,0,2:T(4,128)} %maximum_bitcast_fusion), calls=%async_computation | async-start | bytes 2097152 | tf_op jit(solution)/shard_map/all_to_all | solution.py:81
  150.3 49.2 %all-to-all-done = f32[1,4,64,1024]{3,1,0,2:T(4,128)S(1)} async-done(((f32[1,4,64,1024]{3,1,0,2:T(4,128)}), f32[1,4,64,1024]{3,1,0,2:T(4,128)S(1)}, u32[]{:S(2)}, u32[]{:S(2)}) %all-to-all-start) | async-done | bytes 1048608 | tf_op jit(solution)/shard_map/all_to_all | solution.py:81
  (132 shorter events, 47.4 us)
Async XLA Ops:
  0.6 18.1 %copy-start.3 = (s32[8]{0:T(128)S(1)}, s32[8]{0:T(128)}, u32[]{:S(2)}) copy-start(s32[8]{0:T(128)} %param.9) | copy-start | bytes 100
  1.8 7.1 %collective-permute-start = (bf16[16,1,1024]{2,1,0:T(2,128)(2,1)S(1)}, bf16[16,1,1024]{2,1,0:T(2,128)(2,1)S(1)}, u32[]{:S(2)}, u32[]{:S(2)}) collective-permute-start(bf16[16,1,1024]{2,1,0:T(2,128)(2,1)S(1)} %get-tuple-element.194), channel_id=1, source_target_pairs={{0,64},{64,128},{128,192},{192,256},{256,320},{320,384},{384,448},... | collective-permute-start | bytes 98312 | tf_op jit(solution)/shard_map/ppermute | solution.py:22
  3.7 5.5 %collective-permute-start.1 = (bf16[16,1,1024]{2,1,0:T(2,128)(2,1)S(1)}, bf16[16,1,1024]{2,1,0:T(2,128)(2,1)S(1)}, u32[]{:S(2)}, u32[]{:S(2)}) collective-permute-start(bf16[16,1,1024]{2,1,0:T(2,128)(2,1)S(1)} %get-tuple-element.195), channel_id=1, source_target_pairs={{64,0},{128,64},{192,128},{256,192},{320,256},{384,320},{448,384},... | collective-permute-start | bytes 98312 | tf_op jit(solution)/shard_map/ppermute | solution.py:23
  13.1 10.7 %collective-permute-start.2 = (bf16[16,66,1]{2,1,0:T(8,128)(2,1)}, bf16[16,66,1]{2,1,0:T(8,128)(2,1)}, u32[]{:S(2)}, u32[]{:S(2)}) collective-permute-start(bf16[16,66,1]{2,1,0:T(8,128)(2,1)} %get-tuple-element.193), channel_id=1, source_target_pairs={{0,16},{16,32},{32,48},{1,17},{17,33},{33,49},{2,18},{18,34},{34,5... | collective-permute-start | bytes 6344 | tf_op jit(solution)/shard_map/ppermute | solution.py:22
  17.2 11.9 %collective-permute-start.3 = (bf16[16,66,1]{2,1,0:T(8,128)(2,1)}, bf16[16,66,1]{2,1,0:T(8,128)(2,1)}, u32[]{:S(2)}, u32[]{:S(2)}) collective-permute-start(bf16[16,66,1]{2,1,0:T(8,128)(2,1)} %get-tuple-element.192), channel_id=1, source_target_pairs={{16,0},{32,16},{48,32},{17,1},{33,17},{49,33},{18,2},{34,18},{50,3... | collective-permute-start | bytes 6344 | tf_op jit(solution)/shard_map/ppermute | solution.py:23
  35.5 7.6 %collective-permute-start.4 = (bf16[1,66,1026]{2,1,0:T(8,128)(2,1)S(1)}, bf16[1,66,1026]{2,1,0:T(8,128)(2,1)S(1)}, u32[]{:S(2)}, u32[]{:S(2)}) collective-permute-start(bf16[1,66,1026]{2,1,0:T(8,128)(2,1)S(1)} %get-tuple-element.190), channel_id=1, source_target_pairs={{0,1},{1,2},{2,3},{3,4},{4,5},{5,6},{6,7},{7,8},{8,9},{9,10},{10,1... | collective-permute-start | bytes 406304 | tf_op jit(solution)/shard_map/ppermute | solution.py:22
  39.3 8.1 %collective-permute-start.5 = (bf16[1,66,1026]{2,1,0:T(8,128)(2,1)S(1)}, bf16[1,66,1026]{2,1,0:T(8,128)(2,1)S(1)}, u32[]{:S(2)}, u32[]{:S(2)}) collective-permute-start(bf16[1,66,1026]{2,1,0:T(8,128)(2,1)S(1)} %get-tuple-element.191), channel_id=1, source_target_pairs={{1,0},{2,1},{3,2},{4,3},{5,4},{6,5},{7,6},{8,7},{9,8},{10,9},{11,1... | collective-permute-start | bytes 406304 | tf_op jit(solution)/shard_map/ppermute | solution.py:23
  66.0 1.9 copy-start
  68.1 2.2 %copy-start.1 = (f32[4,4,64,1024]{3,2,1,0:T(8,128)S(1)}, f32[4,4,64,1024]{3,2,1,0:T(8,128)}, u32[]{:S(2)}) copy-start(f32[4,4,64,1024]{3,2,1,0:T(8,128)} %copy-done) | copy-start | bytes 12582916 | tf_op jit(solution)/shard_map/while
  86.5 1.9 copy-start
  88.6 2.2 %copy-start.1 = (f32[4,4,64,1024]{3,2,1,0:T(8,128)S(1)}, f32[4,4,64,1024]{3,2,1,0:T(8,128)}, u32[]{:S(2)}) copy-start(f32[4,4,64,1024]{3,2,1,0:T(8,128)} %copy-done) | copy-start | bytes 12582916 | tf_op jit(solution)/shard_map/while
  107.0 1.9 copy-start
  109.1 2.2 %copy-start.1 = (f32[4,4,64,1024]{3,2,1,0:T(8,128)S(1)}, f32[4,4,64,1024]{3,2,1,0:T(8,128)}, u32[]{:S(2)}) copy-start(f32[4,4,64,1024]{3,2,1,0:T(8,128)} %copy-done) | copy-start | bytes 12582916 | tf_op jit(solution)/shard_map/while
  127.5 1.9 copy-start
  129.6 2.2 %copy-start.1 = (f32[4,4,64,1024]{3,2,1,0:T(8,128)S(1)}, f32[4,4,64,1024]{3,2,1,0:T(8,128)}, u32[]{:S(2)}) copy-start(f32[4,4,64,1024]{3,2,1,0:T(8,128)} %copy-done) | copy-start | bytes 12582916 | tf_op jit(solution)/shard_map/while
  134.0 66.2 %copy-start.2 = (f32[4,4,1024]{2,1,0:T(4,128)S(1)}, f32[4,4,1024]{2,1,0:T(4,128)}, u32[]{:S(2)}) copy-start(f32[4,4,1024]{2,1,0:T(4,128)} %constant.69.clone.1) | copy-start | bytes 196612
  135.4 64.0 %all-to-all-start = ((f32[1,4,64,1024]{3,1,0,2:T(4,128)}), f32[1,4,64,1024]{3,1,0,2:T(4,128)S(1)}, u32[]{:S(2)}, u32[]{:S(2)}) async-start(f32[1,4,64,1024]{3,1,0,2:T(4,128)} %maximum_bitcast_fusion), calls=%async_computation | async-start | bytes 2097152 | tf_op jit(solution)/shard_map/all_to_all | solution.py:81
where the time goes:
time: 204 us; the launch traced here: 203 us
  waiting for transfers between devices  66.5 us (33%)
  other arithmetic  38.6 us (19%)
  matrix products  32.2 us (16%)
  starting transfers between devices  31 us (15%)
  local copies, waits for them, and re-layouts  30.2 us (15%)
  loops' own time  3.65 us (2%)
    all_to_all x1, waiting for transfers between devices, on_device(): lax.all_to_all(partial_image[None], 'gz', split_axis=2, concat_axis=0, ti...  49.2 us
    dot_general x4, matrix products, classify(): jnp.einsum('kzxy,ck->czxy', ramp_terms, slopes, precision=lax.Precision.H...  32.2 us
    while x20, local copies, waits for them, and re-layouts  15.6 us
    all_to_all x1, starting transfers between devices, on_device(): lax.all_to_all(partial_image[None], 'gz', split_axis=2, concat_axis=0, ti...  14.9 us
    ppermute x3, waiting for transfers between devices, padded_2(): after = lax.ppermute(initial, axis, down)  9.93 us
    ppermute x3, starting transfers between devices, padded_2(): before = lax.ppermute(last, axis, up)  9.87 us
    add x4, other arithmetic, classify(): table[:, :1, None, None]  9.73 us
    ppermute x3, waiting for transfers between devices, padded_2(): before = lax.ppermute(last, axis, up)  7.44 us
  transfers between devices with their start and end apart: 7, of which 6 were waited for; matrix products, arithmetic and copies ran while one was open for 1% of the time, Pallas kernels for 0%

commit v1 on v0

v1 whole, which is shorter than its diff:
```python
import functools
import math

import jax
import jax.numpy as jnp
import numpy as np
from jax import lax
from jax.experimental import pallas as pl
from jax.experimental.pallas import tpu as pltpu
from jax.sharding import PartitionSpec as P

BINS = 256
KNOTS = 8
SEGMENTS = KNOTS - 1
AMBIENT = 0.2
LANES = 128
SUB = 8
GROUPS = 8
PITCH = 9

COLOUR_SPAN = 26.0
COVER_SPAN = 9.0
CODES = 65534.0


def colour_scale(colour_ref, channel):
    largest = colour_ref[channel, 0]
    for k in range(1, KNOTS):
        largest = jnp.maximum(largest, colour_ref[channel, k])
    return jnp.maximum(largest, 1e-30)


def encode(value, span):
    position = (jnp.log2(jnp.maximum(value, 2.0 ** (-span - 1.0))) + span) * (CODES / span) + 1.5
    return jnp.clip(position, 0.0, 65535.0).astype(jnp.int32)


def opacity_terms(largest):
    half = 0.5 * largest
    nodes = [half + half * math.cos(math.pi * (2 * i + 1) / 8.0) for i in range(4)]
    values = [-math.expm1(-y) / y for y in nodes]
    return [float(c) for c in np.polynomial.polynomial.polyfit(nodes, values, 3)]


def full(x):
    return jnp.full((SUB, LANES), x, jnp.float32)


def lanes_of(t):
    return slice(t * LANES, (t + 1) * LANES)


def lane_index():
    return lax.broadcasted_iota(jnp.int32, (SUB, LANES), 1)


def edges_kernel(x_low, x_high, y_low, y_high, z_low, z_high, x_out, y_out, front, rear, rows_x):
    depth = x_low.shape[0]
    cols = x_low.shape[2]
    for z in range(depth):
        low = x_low[z].astype(jnp.float32)
        high = x_high[z].astype(jnp.float32)
        rows_x[0, z:z + 1, :] = low[:1]
        rows_x[1, z:z + 1, :] = high[15:]
    x_out[...] = rows_x[...].astype(x_out.dtype)
    lane = lane_index()
    for i in range(GROUPS // 2):
        sides = [jnp.zeros((SUB, LANES), jnp.float32)] * 2
        for z in range(depth):
            low = y_low[z, 16 * i:16 * i + 16, :].astype(jnp.float32)
            high = y_high[z, 16 * i:16 * i + 16, :].astype(jnp.float32)
            for part in range(2):
                at = slice(8 * part, 8 * part + 8)
                sides[part] = jnp.where(lane == z, low[at, :1], sides[part])
                sides[part] = jnp.where(lane == depth + z, high[at, LANES - 1:], sides[part])
        for part in range(2):
            y_out[pl.ds(2 * i + part, SUB, stride=GROUPS), :] = sides[part]
    front[...] = z_low[0]
    rear[...] = z_high[0]


def spread_kernel(vol_ref, cells, grads):
    depth, rows, cols = vol_ref.shape
    lane = lax.broadcasted_iota(jnp.int32, (16, LANES), 1)
    tiles = cols // LANES

    def step(z, carry):
        for c in range(rows // 16):
            plane = vol_ref[z, 16 * c:16 * c + 16, :].astype(jnp.float32)
            left = pltpu.roll(plane, 1, 1)
            right = pltpu.roll(plane, cols - 1, 1)
            for t in range(tiles):
                l, r = left[:, lanes_of(t)], right[:, lanes_of(t)]
                if t == 0:
                    l = jnp.where(lane == 0, 0.0, l)
                if t == tiles - 1:
                    r = jnp.where(lane == LANES - 1, 0.0, r)
                across = r - l
                own = plane[:, lanes_of(t)]
                for part in range(2):
                    i = 2 * c + part
                    at = slice(8 * part, 8 * part + 8)
                    cells[t, z, pl.ds(i, SUB, stride=PITCH), :] = own[at]
                    grads[t, z, pl.ds(i, SUB, stride=PITCH), :] = across[at]
        return carry

    lax.fori_loop(0, depth, step, 0)


def prepare(consts, knots_ref, colour_ref, density_ref, depth_total):
    top = BINS - 1.0
    spans = []
    for k in range(SEGMENTS):
        low = full(knots_ref[k].astype(jnp.float32))
        high = full(knots_ref[k + 1].astype(jnp.float32))
        spans.append((high - low) * (1.0 / top))
        if k:
            consts[k - 1] = low / top
    consts[6] = full(density_ref[0]) * (1.0 / depth_total)
    for k in range(SEGMENTS):
        step = full(density_ref[k + 1]) - full(density_ref[k])
        consts[7 + k] = step * (1.0 / depth_total) / spans[k]
    for c in range(3):
        scale = full(colour_scale(colour_ref, c))
        consts[14 + 8 * c] = full(colour_ref[c, 0]) / scale
        for k in range(SEGMENTS):
            step = full(colour_ref[c, k + 1]) - full(colour_ref[c, k])
            consts[15 + 8 * c + k] = step / scale / spans[k]


def composite(consts, cell, grad_x, grad_y, depth, depth_total):
    c0, c1, c2, c3 = opacity_terms(10.0 / depth_total)
    points = [consts[k] for k in range(6)]
    first = consts[6]
    slopes = [consts[7 + k] for k in range(SEGMENTS)]
    transmit = jnp.ones((SUB, LANES), jnp.float32)
    weight = None
    moments = None
    earlier, now = cell(-1), cell(0)
    for z in range(depth):
        later = cell(z + 1)
        gx, gy, gz = grad_x(z), grad_y(z), later - earlier
        across = gy + gz
        facing = jnp.abs(gx + (across + across))
        shading = AMBIENT + facing * (
            ((1.0 - AMBIENT) / 3.0) * lax.rsqrt(gx * gx + gy * gy + (gz * gz + 1.0))
        )
        capped = [jnp.minimum(now, p) for p in points] + [now]
        ramps = [capped[0]] + [capped[k + 1] - capped[k] for k in range(6)]
        y = first
        for k in range(SEGMENTS):
            y = y + ramps[k] * slopes[k]
        taken = transmit * (y * (c0 + y * (c1 + y * (c2 + y * c3))))
        transmit = transmit - taken
        shaded = taken * shading
        if z == 0:
            weight = shaded
            moments = [shaded * r for r in ramps]
        else:
            weight = weight + shaded
            moments = [m + shaded * r for m, r in zip(moments, ramps)]
        earlier, now = now, later
    codes = []
    for c in range(3):
        value = weight * consts[14 + 8 * c]
        for k in range(SEGMENTS):
            value = value + moments[k] * consts[15 + 8 * c + k]
        codes.append(encode(value, COLOUR_SPAN))
    codes.append(encode(1.0 - transmit, COVER_SPAN))
    return codes[0] | (codes[1] << 16), codes[2] | (codes[3] << 16)


def store_words(out_ref, words, t, r, tiles):
    base = (r // 4) * (tiles * SUB) + t * SUB + r % 4
    out_ref[pl.ds(base, SUB, stride=2 * tiles * SUB), :] = words[0]
    out_ref[pl.ds(base + 4, SUB, stride=2 * tiles * SUB), :] = words[1]


def inner_kernel(
    knots_ref, colour_ref, density_ref, cells, grads, bz_ref, az_ref, out_ref, sides, consts,
    *, depth_total,
):
    tiles, depth = cells.shape[:2]
    prepare(consts, knots_ref, colour_ref, density_ref, depth_total)
    for side, ref in enumerate((bz_ref, az_ref)):
        for c in range(ref.shape[0] // 16):
            plane = ref[16 * c:16 * c + 16, :].astype(jnp.float32)
            for t in range(tiles):
                for part in range(2):
                    at = slice(8 * part, 8 * part + 8)
                    sides[side, t, pl.ds(2 * c + part, SUB, stride=PITCH), :] = plane[at, lanes_of(t)]

    def tile_step(t, carry):
        def row_step(r, carry):
            at = pl.ds(PITCH * r, SUB)

            def cell(z):
                if z < 0:
                    return sides[0, t, at, :]
                if z == depth:
                    return sides[1, t, at, :]
                return cells[t, z, at, :]

            def grad_x(z):
                return cells[t, z, pl.ds(PITCH * r + PITCH, SUB), :] - cells[t, z, pl.ds(PITCH * r - PITCH, SUB), :]

            words = composite(
                consts, cell, grad_x, lambda z: grads[t, z, at, :], depth, depth_total
            )
            store_words(out_ref, words, t, r, tiles)
            return carry

        return lax.fori_loop(1, GROUPS - 1, row_step, carry, unroll=2)

    lax.fori_loop(1, tiles - 1, tile_step, 0)


def outer_kernel(
    knots_ref, colour_ref, density_ref, cells, grads, sides, x_ref, y_ref, _, out_ref, x_edges, y_edges,
    consts, *, depth_total,
):
    tiles, depth = cells.shape[:2]
    prepare(consts, knots_ref, colour_ref, density_ref, depth_total)
    gx, gy = lax.axis_index("gx"), lax.axis_index("gy")
    x_last, y_last = x_ref.shape[0] - 1, y_ref.shape[0] - 1
    x_edges[0] = jnp.where(gx > 0, x_ref[jnp.maximum(gx - 1, 0), 1].astype(jnp.float32), 0.0)
    x_edges[1] = jnp.where(gx < x_last, x_ref[jnp.minimum(gx + 1, x_last), 0].astype(jnp.float32), 0.0)
    y_edges[0] = jnp.where(gy > 0, -pltpu.roll(y_ref[jnp.maximum(gy - 1, 0)], LANES - depth, 1), 0.0)
    y_edges[1] = jnp.where(gy < y_last, y_ref[jnp.minimum(gy + 1, y_last)], 0.0)
    lane = lane_index()
    sublane = lax.broadcasted_iota(jnp.int32, (SUB, LANES), 0)

    def work(t, r, above_start, below_start):
        at = pl.ds(PITCH * r, SUB)
        edge_lane = lane == jnp.where(t == 0, 0, jnp.where(t == tiles - 1, LANES - 1, -1))
        columns = y_edges[jnp.where(t == 0, 0, 1), pl.ds(pl.multiple_of(SUB * r, SUB), SUB), :]
        at_lanes = pl.ds(pl.multiple_of(t * LANES, LANES), LANES)

        def cell(z):
            if z < 0:
                return sides[0, t, at, :]
            if z == depth:
                return sides[1, t, at, :]
            return cells[t, z, at, :]

        def grad_x(z):
            above = cells[t, z, pl.ds(above_start, SUB), :]
            below = cells[t, z, pl.ds(below_start, SUB), :]
            if isinstance(r, int) and r == 0:
                above = jnp.where(sublane == 0, x_edges[0, z:z + 1, at_lanes], above)
            if isinstance(r, int) and r == GROUPS - 1:
                below = jnp.where(sublane == SUB - 1, x_edges[1, z:z + 1, at_lanes], below)
            return below - above

        def grad_y(z):
            return grads[t, z, at, :] + jnp.where(edge_lane, columns[:, z:z + 1], 0.0)

        store_words(out_ref, composite(consts, cell, grad_x, grad_y, depth, depth_total), t, r, tiles)

    last = GROUPS - 1

    def rows_step(t, carry):
        work(t, 0, jnp.minimum(t, 0) + PITCH * last - 1, jnp.minimum(t, 0) + PITCH)
        work(t, last, jnp.minimum(t, 0) + PITCH * (last - 1), jnp.minimum(t, 0) + 1)
        return carry

    lax.fori_loop(0, tiles, rows_step, 0)

    def cols_step(r, carry):
        for t in (0, tiles - 1):
            work(t, r, PITCH * r - PITCH, PITCH * r + PITCH)
        return carry

    lax.fori_loop(1, last, cols_step, 0)


def compose_kernel(colour_ref, pieces_ref, image_ref, coverage_ref):
    count = pieces_ref.shape[0]
    low_rows = lax.broadcasted_iota(jnp.int32, (SUB, LANES), 0) < 4
    scales = [full(colour_scale(colour_ref, c)) for c in range(3)]
    step = COLOUR_SPAN / CODES
    steps_hi = jnp.where(low_rows, step, COVER_SPAN / CODES)
    start_hi = jnp.where(low_rows, -COLOUR_SPAN - step, -COVER_SPAN - COVER_SPAN / CODES)

    def decode(code, steps, start):
        value = jnp.exp2(code.astype(jnp.float32) * steps + start)
        return jnp.where(code > 0, value, 0.0)

    for t in range(pieces_ref.shape[1] // SUB):
        low = high = None
        transmit = None
        for piece in range(count):
            word = pieces_ref[piece, t * SUB:(t + 1) * SUB, :]
            red_blue = decode(word & 0xFFFF, step, -COLOUR_SPAN - step)
            green_cover = decode(lax.shift_right_logical(word, 16), steps_hi, start_hi)
            cover = jnp.where(low_rows, pltpu.roll(green_cover, 4, 0), green_cover)
            if piece == 0:
                low, high, transmit = red_blue, green_cover, 1.0 - cover
            else:
                low = low + transmit * red_blue
                high = high + transmit * green_cover
                transmit = transmit * (1.0 - cover)
        low = low * jnp.where(low_rows, scales[0], scales[2])
        high = high * jnp.where(low_rows, scales[1], 1.0)
        image_ref[0, :, lanes_of(t)] = low[:4]
        image_ref[1, :, lanes_of(t)] = high[:4]
        image_ref[2, :, lanes_of(t)] = low[4:]
        coverage_ref[:, lanes_of(t)] = high[4:]


def cost(flops, moved):
    return pl.CostEstimate(flops=flops, bytes_accessed=moved, transcendentals=0)


def on_device(volume, knot_bins, tf_colour, tf_density):
    depth, rows, cols = volume.shape
    count = lax.axis_size("gz")
    tiles = cols // LANES
    depth_total = float(depth * count)
    smem = pl.BlockSpec(memory_space=pltpu.SMEM)
    vmem = pl.BlockSpec(memory_space=pltpu.VMEM)
    params = pltpu.CompilerParams(vmem_limit_bytes=24 << 20)
    f32 = jnp.float32

    def whole(*shape):
        return pl.BlockSpec(shape, lambda n: (0,) * len(shape))

    x_edges, y_edges, front, rear = pl.pallas_call(
        edges_kernel,
        grid=(1,),
        out_shape=(
            jax.ShapeDtypeStruct((2, depth, cols), volume.dtype),
            jax.ShapeDtypeStruct((rows, LANES), f32),
            jax.ShapeDtypeStruct((rows, cols), volume.dtype),
            jax.ShapeDtypeStruct((rows, cols), volume.dtype),
        ),
        in_specs=[
            pl.BlockSpec((depth, 16, cols), lambda n: (0, 0, 0)),
            pl.BlockSpec((depth, 16, cols), lambda n: (0, rows // 16 - 1, 0)),
            pl.BlockSpec((depth, rows, LANES), lambda n: (0, 0, 0)),
            pl.BlockSpec((depth, rows, LANES), lambda n: (0, 0, tiles - 1)),
            pl.BlockSpec((1, rows, cols), lambda n: (0, 0, 0)),
            pl.BlockSpec((1, rows, cols), lambda n: (depth - 1, 0, 0)),
        ],
        out_specs=(whole(2, depth, cols), whole(rows, LANES), whole(rows, cols), whole(rows, cols)),
        scratch_shapes=[pltpu.VMEM((2, depth, cols), f32)],
        compiler_params=params,
        cost_estimate=cost(1 << 20, 2 << 20),
        name="edges",
    )(*[volume] * 6)
    x_all = lax.all_gather(x_edges, "gx")
    y_all = lax.all_gather(y_edges, "gy")
    up = [(i, i + 1) for i in range(count - 1)]
    down = [(j, i) for i, j in up]
    bz = lax.ppermute(rear, "gz", up)
    az = lax.ppermute(front, "gz", down)

    cells, grads = pl.pallas_call(
        spread_kernel,
        out_shape=(
            jax.ShapeDtypeStruct((tiles, depth, PITCH * GROUPS, LANES), f32),
            jax.ShapeDtypeStruct((tiles, depth, PITCH * GROUPS, LANES), f32),
        ),
        in_specs=[vmem],
        out_specs=(vmem, vmem),
        compiler_params=params,
        cost_estimate=cost(1 << 23, 2 << 20),
        name="spread",
    )(volume)

    tables = (knot_bins, tf_colour, tf_density)
    words = jax.ShapeDtypeStruct((count * tiles * SUB, LANES), jnp.int32)
    side_shape = (2, tiles, PITCH * GROUPS, LANES)
    inner, sides = pl.pallas_call(
        functools.partial(inner_kernel, depth_total=depth_total),
        out_shape=(words, jax.ShapeDtypeStruct(side_shape, f32)),
        in_specs=[smem] * 3 + [vmem] * 4,
        out_specs=(vmem, vmem),
        scratch_shapes=[pltpu.VMEM((40, SUB, LANES), f32)],
        compiler_params=params,
        cost_estimate=cost(1 << 26, 1 << 23),
        name="inner",
    )(*tables, cells, grads, bz, az)
    codes = pl.pallas_call(
        functools.partial(outer_kernel, depth_total=depth_total),
        out_shape=words,
        in_specs=[smem] * 3 + [vmem] * 6,
        out_specs=vmem,
        input_output_aliases={8: 0},
        scratch_shapes=[
            pltpu.VMEM((2, depth, cols), f32),
            pltpu.VMEM((2, rows, LANES), f32),
            pltpu.VMEM((40, SUB, LANES), f32),
        ],
        compiler_params=params,
        cost_estimate=cost(1 << 26, 1 << 23),
        name="outer",
    )(*tables, cells, grads, sides, x_all, y_all, inner)
    pieces = lax.all_to_all(
        codes.reshape(count, tiles * SUB, LANES), "gz", split_axis=0, concat_axis=0, tiled=True
    )
    band = rows // count
    return pl.pallas_call(
        compose_kernel,
        out_shape=(
            jax.ShapeDtypeStruct((3, band, cols), f32),
            jax.ShapeDtypeStruct((band, cols), f32),
        ),
        in_specs=[smem, vmem],
        out_specs=(vmem, vmem),
        name="compose",
    )(tf_colour, pieces)


def solution(mesh):
    placed = (P("gz", "gx", "gy"), P(), P(), P())
    return jax.shard_map(
        on_device,
        mesh=mesh,
        in_specs=placed,
        out_specs=(P(None, ("gx", "gz"), "gy"), P(("gx", "gz"), "gy")),
        check_vma=False,
    )
```

time: 204 us -> 94.3 us (0.46)
  the two profiles are of different devices: /device:TPU:16 before, /device:TPU:32 now
where the time goes in v1:
time: 94.3 us; the launch traced here: 94.1 us
  blocking collectives  65.9 us (70%)
  Pallas kernels  17.2 us (18%)
  starting transfers between devices  8.69 us (9%)
  local copies, waits for them, and re-layouts  1.6 us (2%)
    all_to_all x1, blocking collectives, on_device(): lax.all_to_all(codes.reshape(count, tiles * SUB, LANES), 'gz', split_axis...  40.8 us
    all_gather x1, blocking collectives, on_device(): x_all = lax.all_gather(x_edges, 'gx')  13.1 us
    all_gather x1, blocking collectives, on_device(): y_all = lax.all_gather(y_edges, 'gy')  12 us
    pallas_call x1, Pallas kernels, on_device(): pl.pallas_call(functools.partial(inner_kernel, depth_total=depth_total),...  6.76 us
    pallas_call x1, Pallas kernels, on_device(): pl.pallas_call(functools.partial(outer_kernel, depth_total=depth_total),...  5.66 us
    ppermute x1, starting transfers between devices, on_device(): az = lax.ppermute(front, 'gz', down)  4.86 us
    ppermute x1, starting transfers between devices, on_device(): bz = lax.ppermute(rear, 'gz', up)  3.83 us
    pallas_call x1, Pallas kernels, on_device(): pl.pallas_call(spread_kernel, out_shape=(jax.ShapeDtypeStruct((tiles, dep...  2.45 us
  transfers between devices with their start and end apart: 2, of which 0 were waited for; matrix products, arithmetic and copies ran while one was open for 0% of the time, Pallas kernels for 3%

profile of v1, /device:TPU:32, one launch (start us, length us, event | category | flops | bytes accessed | tf_op | source)
XLA Modules:
  0.0 94.1 jit_solution(15396274428096364194)
XLA Ops:
  0.6 0.0 copy-start
  0.6 1.6 %copy-done = bf16[16,64,1024]{2,1,0:T(8,128)(2,1)S(1)} copy-done((bf16[16,64,1024]{2,1,0:T(8,128)(2,1)S(1)}, bf16[16,64,1024]{2,1,0:T(8,128)(2,1)}, u32[]{:S(2)}) %copy-start) | copy-done | bytes 2097176
  2.2 0.0 copy-start.1
  2.2 0.0 copy-start.2
  2.2 0.0 copy-start.3
  2.2 0.3 edges.1
  2.5 3.8 %collective-permute-start = (bf16[64,1024]{1,0:T(8,128)(2,1)S(1)}, bf16[64,1024]{1,0:T(8,128)(2,1)S(1)}, u32[]{:S(2)}, u32[]{:S(2)}) collective-permute-start(bf16[64,1024]{1,0:T(8,128)(2,1)S(1)} %get-tuple-element.12), channel_id=1, source_target_pairs={{0,1},{1,2},{2,3},{3,4},{4,5},{5,6},{6,7},{7,8},{8,9},{9,10},{10,1... | collective-permute-start | bytes 393224 | tf_op jit(solution)/shard_map/ppermute | solution.py:355
  6.4 4.9 %collective-permute-start.1 = (bf16[64,1024]{1,0:T(8,128)(2,1)S(1)}, bf16[64,1024]{1,0:T(8,128)(2,1)S(1)}, u32[]{:S(2)}, u32[]{:S(2)}) collective-permute-start(bf16[64,1024]{1,0:T(8,128)(2,1)S(1)} %get-tuple-element.13), channel_id=1, source_target_pairs={{1,0},{2,1},{3,2},{4,3},{5,4},{6,5},{7,6},{8,7},{9,8},{10,9},{11,1... | collective-permute-start | bytes 393224 | tf_op jit(solution)/shard_map/ppermute | solution.py:356
  11.2 13.1 %all-gather = bf16[16,16,1024]{2,1,0:T(8,128)(2,1)S(1)} all-gather(bf16[2,16,1024]{2,1,0:T(8,128)(2,1)S(1)} %get-tuple-element.15), channel_id=2, replica_groups=mesh['gx'=8,'gy'=4,'gz'=16] {'gx'}, dimensions={0}, use_global_device_ids=true | all-gather | bytes 589824 | tf_op jit(solution)/shard_map/all_gather | solution.py:351
  24.4 2.5 %spread.1 = (f32[8,16,72,128]{3,2,1,0:T(8,128)S(1)}, f32[8,16,72,128]{3,2,1,0:T(8,128)S(1)}) custom-call(bf16[16,64,1024]{2,1,0:T(8,128)(2,1)S(1)} %copy-done), custom_call_target="tpu_custom_call" | custom-call | flops 8388608 | bytes 2097152 | tf_op jit(solution)/shard_map/spread/pallas_call | solution.py:358
  26.8 12.0 %all-gather.1 = f32[256,128]{1,0:T(8,128)S(1)} all-gather(f32[64,128]{1,0:T(8,128)S(1)} %get-tuple-element.16), channel_id=3, replica_groups=mesh['gx'=8,'gy'=4,'gz'=16] {'gy'}, dimensions={0}, use_global_device_ids=true | all-gather | bytes 163840 | tf_op jit(solution)/shard_map/all_gather | solution.py:352
  38.8 0.0 collective-permute-done.bz_ref
  38.8 0.0 collective-permute-done.1.az_ref
  38.8 0.0 copy-done.1
  38.8 0.0 copy-done.2
  38.8 0.0 copy-done.3
  38.8 6.8 %inner.1 = (s32[1024,128]{1,0:T(8,128)S(1)}, f32[2,8,72,128]{3,2,1,0:T(8,128)S(1)}) custom-call(s32[8]{0:T(128)S(1)} %copy-done.2, f32[3,8]{1,0:T(4,128)S(1)} %copy-done.1, f32[8]{0:T(128)S(1)} %copy-done.3, f32[8,16,72,128]{3,2,1,0:T(8,128)S(1)} %get-tuple-element.10.cells, f32[8,16,72,128]{3,2,1,0:T(8,128)S(1)} %get-tuple-element.11.grads, ...), custom_call_target="tpu_custom_call" | custom-call | flops 67108864 | bytes 8388608 | tf_op jit(solution)/shard_map/inner/pallas_call | solution.py:374
  45.6 5.7 %outer.1 = s32[1024,128]{1,0:T(8,128)S(1)} custom-call(s32[8]{0:T(128)S(1)} %copy-done.2, f32[3,8]{1,0:T(4,128)S(1)} %copy-done.1, f32[8]{0:T(128)S(1)} %copy-done.3, f32[8,16,72,128]{3,2,1,0:T(8,128)S(1)} %get-tuple-element.10.cells, f32[8,16,72,128]{3,2,1,0:T(8,128)S(1)} %get-tuple-element.11.grads, ...), custom_call_target="tpu_custom_call", output_to_operand_aliasing={{}: (8, {})} | custom-call | flops 67108864 | bytes 8388608 | tf_op jit(solution)/shard_map/outer/pallas_call | solution.py:384
  51.3 40.8 %all_to_all.5.pieces_ref = s32[16,64,128]{2,1,0:T(8,128)} all-to-all(s32[16,64,128]{2,1,0:T(8,128)S(1)} %bitcast.4), channel_id=1, replica_groups=mesh['gx'=8,'gy'=4,'gz'=16] {'gz'}, dimensions={0} | all-to-all | bytes 1048576 | tf_op jit(solution)/shard_map/all_to_all | solution.py:399
  92.0 2.0 %compose.1 = (f32[3,4,1024]{2,1,0:T(4,128)}, f32[4,1024]{1,0:T(4,128)}) custom-call(f32[3,8]{1,0:T(4,128)} %colour_ref.5, s32[16,64,128]{2,1,0:T(8,128)} %all_to_all.5.pieces_ref), custom_call_target="tpu_custom_call" | custom-call | tf_op jit(solution)/shard_map/compose/pallas_call | solution.py:403
Async XLA Ops:
  0.6 1.6 %copy-start = (bf16[16,64,1024]{2,1,0:T(8,128)(2,1)S(1)}, bf16[16,64,1024]{2,1,0:T(8,128)(2,1)}, u32[]{:S(2)}) copy-start(bf16[16,64,1024]{2,1,0:T(8,128)(2,1)} %z_high.1) | copy-start | bytes 6291460
  2.2 36.6 %copy-start.1 = (f32[3,8]{1,0:T(4,128)S(1)}, f32[3,8]{1,0:T(4,128)}, u32[]{:S(2)}) copy-start(f32[3,8]{1,0:T(4,128)} %colour_ref.5) | copy-start | bytes 292
  2.2 36.6 %copy-start.2 = (s32[8]{0:T(128)S(1)}, s32[8]{0:T(128)}, u32[]{:S(2)}) copy-start(s32[8]{0:T(128)} %knots_ref.3) | copy-start | bytes 100
  2.2 36.6 %copy-start.3 = (f32[8]{0:T(128)S(1)}, f32[8]{0:T(128)}, u32[]{:S(2)}) copy-start(f32[8]{0:T(128)} %density_ref.3) | copy-start | bytes 100
  2.5 36.3 %collective-permute-start = (bf16[64,1024]{1,0:T(8,128)(2,1)S(1)}, bf16[64,1024]{1,0:T(8,128)(2,1)S(1)}, u32[]{:S(2)}, u32[]{:S(2)}) collective-permute-start(bf16[64,1024]{1,0:T(8,128)(2,1)S(1)} %get-tuple-element.12), channel_id=1, source_target_pairs={{0,1},{1,2},{2,3},{3,4},{4,5},{5,6},{6,7},{7,8},{8,9},{9,10},{10,1... | collective-permute-start | bytes 393224 | tf_op jit(solution)/shard_map/ppermute | solution.py:355
  6.4 32.4 %collective-permute-start.1 = (bf16[64,1024]{1,0:T(8,128)(2,1)S(1)}, bf16[64,1024]{1,0:T(8,128)(2,1)S(1)}, u32[]{:S(2)}, u32[]{:S(2)}) collective-permute-start(bf16[64,1024]{1,0:T(8,128)(2,1)S(1)} %get-tuple-element.13), channel_id=1, source_target_pairs={{1,0},{2,1},{3,2},{4,3},{5,4},{6,5},{7,6},{8,7},{9,8},{10,9},{11,1... | collective-permute-start | bytes 393224 | tf_op jit(solution)/shard_map/ppermute | solution.py:356

commit v2 on v1

--- a/solution.py
+++ b/solution.py
@@ -54,7 +54,7 @@
     return lax.broadcasted_iota(jnp.int32, (SUB, LANES), 1)
 
 
-def edges_kernel(x_low, x_high, y_low, y_high, z_low, z_high, x_out, y_out, front, rear, rows_x):
+def edges_kernel(x_low, x_high, y_low, y_high, z_low, z_high, top, bottom, y_out, front, rear, rows_x):
     depth = x_low.shape[0]
     cols = x_low.shape[2]
     for z in range(depth):
@@ -62,7 +62,8 @@
         high = x_high[z].astype(jnp.float32)
         rows_x[0, z:z + 1, :] = low[:1]
         rows_x[1, z:z + 1, :] = high[15:]
-    x_out[...] = rows_x[...].astype(x_out.dtype)
+    top[...] = rows_x[0].astype(top.dtype)
+    bottom[...] = rows_x[1].astype(bottom.dtype)
     lane = lane_index()
     for i in range(GROUPS // 2):
         sides = [jnp.zeros((SUB, LANES), jnp.float32)] * 2
@@ -160,39 +161,56 @@
             weight = weight + shaded
             moments = [m + shaded * r for m, r in zip(moments, ramps)]
         earlier, now = now, later
-    codes = []
+    values = []
     for c in range(3):
         value = weight * consts[14 + 8 * c]
         for k in range(SEGMENTS):
             value = value + moments[k] * consts[15 + 8 * c + k]
-        codes.append(encode(value, COLOUR_SPAN))
-    codes.append(encode(1.0 - transmit, COVER_SPAN))
-    return codes[0] | (codes[1] << 16), codes[2] | (codes[3] << 16)
-
-
-def store_words(out_ref, words, t, r, tiles):
-    base = (r // 4) * (tiles * SUB) + t * SUB + r % 4
-    out_ref[pl.ds(base, SUB, stride=2 * tiles * SUB), :] = words[0]
-    out_ref[pl.ds(base + 4, SUB, stride=2 * tiles * SUB), :] = words[1]
-
-
-def inner_kernel(
-    knots_ref, colour_ref, density_ref, cells, grads, bz_ref, az_ref, out_ref, sides, consts,
-    *, depth_total,
-):
+        values.append(value)
+    return values + [1.0 - transmit]
+
+
+def spread_side(ref, sides, side):
+    for c in range(ref.shape[0] // 16):
+        plane = ref[16 * c:16 * c + 16, :].astype(jnp.float32)
+        for t in range(sides.shape[1]):
+            for part in range(2):
+                own = plane[8 * part:8 * part + 8, lanes_of(t)]
+                sides[side, t, pl.ds(2 * c + part, SUB, stride=PITCH), :] = own
+
+
+def place_edges(cells, grads, bx_ref, ax_ref, by_ref, ay_ref):
     tiles, depth = cells.shape[:2]
-    prepare(consts, knots_ref, colour_ref, density_ref, depth_total)
-    for side, ref in enumerate((bz_ref, az_ref)):
-        for c in range(ref.shape[0] // 16):
-            plane = ref[16 * c:16 * c + 16, :].astype(jnp.float32)
+    for slot, ref in ((PITCH * (GROUPS - 1) - 1, bx_ref), (GROUPS, ax_ref)):
+        edge = ref[...].astype(jnp.float32)
+        for z in range(depth):
             for t in range(tiles):
-                for part in range(2):
-                    at = slice(8 * part, 8 * part + 8)
-                    sides[side, t, pl.ds(2 * c + part, SUB, stride=PITCH), :] = plane[at, lanes_of(t)]
+                cells[t, z, slot:slot + 1, :] = edge[z:z + 1, lanes_of(t)]
+    lane = lane_index()
+
+    def step(r, carry):
+        rows = pl.ds(pl.multiple_of(SUB * r, SUB), SUB)
+        at = pl.ds(PITCH * r, SUB)
+        before, after = by_ref[rows, :], ay_ref[rows, :]
+        for z in range(depth):
+            first = jnp.where(lane == 0, before[:, depth + z:depth + z + 1], 0.0)
+            last = jnp.where(lane == LANES - 1, after[:, z:z + 1], 0.0)
+            grads[0, z, at, :] = grads[0, z, at, :] - first
+            grads[tiles - 1, z, at, :] = grads[tiles - 1, z, at, :] + last
+        return carry
+
+    lax.fori_loop(0, GROUPS, step, 0)
+
+
+def half_loop(consts, cells, grads, sides, parity, depth_total, store):
+    tiles, depth = cells.shape[:2]
 
     def tile_step(t, carry):
-        def row_step(r, carry):
+        def row_step(j, carry):
+            r = 4 * parity + j
             at = pl.ds(PITCH * r, SUB)
+            above = pl.ds(jnp.where(r == 0, PITCH * (GROUPS - 1) - 1, PITCH * r - PITCH), SUB)
+            below = pl.ds(jnp.where(r == GROUPS - 1, 1, PITCH * r + PITCH), SUB)
 
             def cell(z):
                 if z < 0:
@@ -201,77 +219,85 @@
                     return sides[1, t, at, :]
                 return cells[t, z, at, :]
 
-            def grad_x(z):
-                return cells[t, z, pl.ds(PITCH * r + PITCH, SUB), :] - cells[t, z, pl.ds(PITCH * r - PITCH, SUB), :]
-
-            words = composite(
-                consts, cell, grad_x, lambda z: grads[t, z, at, :], depth, depth_total
+            values = composite(
+                consts,
+                cell,
+                lambda z: cells[t, z, below, :] - cells[t, z, above, :],
+                lambda z: grads[t, z, at, :],
+                depth,
+                depth_total,
             )
-            store_words(out_ref, words, t, r, tiles)
+            store(t, j, values)
             return carry
 
-        return lax.fori_loop(1, GROUPS - 1, row_step, carry, unroll=2)
-
-    lax.fori_loop(1, tiles - 1, tile_step, 0)
-
-
-def outer_kernel(
-    knots_ref, colour_ref, density_ref, cells, grads, sides, x_ref, y_ref, _, out_ref, x_edges, y_edges,
-    consts, *, depth_total,
+        return lax.fori_loop(0, 4, row_step, carry, unroll=2)
+
+    lax.fori_loop(0, tiles, tile_step, 0)
+
+
+def pack(values):
+    codes = [encode(v, COLOUR_SPAN) for v in values[:3]] + [encode(values[3], COVER_SPAN)]
+    return codes[0] | (codes[1] << 16), codes[2] | (codes[3] << 16)
+
+
+def decode(code, span):
+    value = jnp.exp2(code.astype(jnp.float32) * (span / CODES) - (span + span / CODES))
+    return jnp.where(code > 0, value, 0.0)
+
+
+def theirs_kernel(
+    knots_ref, colour_ref, density_ref, cells_in, grads_in, bx_ref, ax_ref, by_ref, ay_ref, bz_ref, az_ref,
+    out_ref, cells, grads, sides, consts, *, depth_total,
 ):
-    tiles, depth = cells.shape[:2]
     prepare(consts, knots_ref, colour_ref, density_ref, depth_total)
-    gx, gy = lax.axis_index("gx"), lax.axis_index("gy")
-    x_last, y_last = x_ref.shape[0] - 1, y_ref.shape[0] - 1
-    x_edges[0] = jnp.where(gx > 0, x_ref[jnp.maximum(gx - 1, 0), 1].astype(jnp.float32), 0.0)
-    x_edges[1] = jnp.where(gx < x_last, x_ref[jnp.minimum(gx + 1, x_last), 0].astype(jnp.float32), 0.0)
-    y_edges[0] = jnp.where(gy > 0, -pltpu.roll(y_ref[jnp.maximum(gy - 1, 0)], LANES - depth, 1), 0.0)
-    y_edges[1] = jnp.where(gy < y_last, y_ref[jnp.minimum(gy + 1, y_last)], 0.0)
-    lane = lane_index()
-    sublane = lax.broadcasted_iota(jnp.int32, (SUB, LANES), 0)
-
-    def work(t, r, above_start, below_start):
-        at = pl.ds(PITCH * r, SUB)
-        edge_lane = lane == jnp.where(t == 0, 0, jnp.where(t == tiles - 1, LANES - 1, -1))
-        columns = y_edges[jnp.where(t == 0, 0, 1), pl.ds(pl.multiple_of(SUB * r, SUB), SUB), :]
-        at_lanes = pl.ds(pl.multiple_of(t * LANES, LANES), LANES)
-
-        def cell(z):
-            if z < 0:
-                return sides[0, t, at, :]
-            if z == depth:
-                return sides[1, t, at, :]
-            return cells[t, z, at, :]
-
-        def grad_x(z):
-            above = cells[t, z, pl.ds(above_start, SUB), :]
-            below = cells[t, z, pl.ds(below_start, SUB), :]
-            if isinstance(r, int) and r == 0:
-                above = jnp.where(sublane == 0, x_edges[0, z:z + 1, at_lanes], above)
-            if isinstance(r, int) and r == GROUPS - 1:
-                below = jnp.where(sublane == SUB - 1, x_edges[1, z:z + 1, at_lanes], below)
-            return below - above
-
-        def grad_y(z):
-            return grads[t, z, at, :] + jnp.where(edge_lane, columns[:, z:z + 1], 0.0)
-
-        store_words(out_ref, composite(consts, cell, grad_x, grad_y, depth, depth_total), t, r, tiles)
-
-    last = GROUPS - 1
-
-    def rows_step(t, carry):
-        work(t, 0, jnp.minimum(t, 0) + PITCH * last - 1, jnp.minimum(t, 0) + PITCH)
-        work(t, last, jnp.minimum(t, 0) + PITCH * (last - 1), jnp.minimum(t, 0) + 1)
+    spread_side(bz_ref, sides, 0)
+    spread_side(az_ref, sides, 1)
+    place_edges(cells, grads, bx_ref, ax_ref, by_ref, ay_ref)
+
+    def store(t, j, values):
+        first, second = pack(values)
+        out_ref[j, t] = first
+        out_ref[4 + j, t] = second
+
+    parity = 1 - lax.rem(lax.axis_index("gz"), 2)
+    half_loop(consts, cells, grads, sides, parity, depth_total, store)
+
+
+def ours_kernel(
+    knots_ref, colour_ref, density_ref, cells, grads, sides, out_ref, consts, *, depth_total,
+):
+    prepare(consts, knots_ref, colour_ref, density_ref, depth_total)
+
+    def store(t, j, values):
+        for c in range(4):
+            out_ref[4 * c + j, t] = values[c]
+
+    parity = lax.rem(lax.axis_index("gz"), 2)
+    half_loop(consts, cells, grads, sides, parity, depth_total, store)
+
+
+def pair_kernel(ours_ref, theirs_ref, out_ref):
+    tiles = ours_ref.shape[1]
+    front = lax.rem(lax.axis_index("gz"), 2) == 0
+
+    def step(t, carry):
+        for j in range(4):
+            ours = [ours_ref[4 * c + j, t] for c in range(4)]
+            first, second = theirs_ref[j, t], theirs_ref[4 + j, t]
+            theirs = [
+                decode(first & 0xFFFF, COLOUR_SPAN),
+                decode(lax.shift_right_logical(first, 16), COLOUR_SPAN),
+                decode(second & 0xFFFF, COLOUR_SPAN),
+                decode(lax.shift_right_logical(second, 16), COVER_SPAN),
+            ]
+            keep_ours = jnp.where(front, 1.0, 1.0 - theirs[3])
+            keep_theirs = jnp.where(front, 1.0 - ours[3], 1.0)
+            words = pack([o * keep_ours + p * keep_theirs for o, p in zip(ours, theirs)])
+            for w in range(2):
+                out_ref[pl.ds(t * SUB + 4 * w + j, SUB, stride=tiles * SUB), :] = words[w]
         return carry
 
-    lax.fori_loop(0, tiles, rows_step, 0)
-
-    def cols_step(r, carry):
-        for t in (0, tiles - 1):
-            work(t, r, PITCH * r - PITCH, PITCH * r + PITCH)
-        return carry
-
-    lax.fori_loop(1, last, cols_step, 0)
+    lax.fori_loop(0, tiles, step, 0)
 
 
 def compose_kernel(colour_ref, pieces_ref, image_ref, coverage_ref):
@@ -282,7 +308,7 @@
     steps_hi = jnp.where(low_rows, step, COVER_SPAN / CODES)
     start_hi = jnp.where(low_rows, -COLOUR_SPAN - step, -COVER_SPAN - COVER_SPAN / CODES)
 
-    def decode(code, steps, start):
+    def level(code, steps, start):
         value = jnp.exp2(code.astype(jnp.float32) * steps + start)
         return jnp.where(code > 0, value, 0.0)
 
@@ -291,8 +317,8 @@
         transmit = None
         for piece in range(count):
             word = pieces_ref[piece, t * SUB:(t + 1) * SUB, :]
-            red_blue = decode(word & 0xFFFF, step, -COLOUR_SPAN - step)
-            green_cover = decode(lax.shift_right_logical(word, 16), steps_hi, start_hi)
+            red_blue = level(word & 0xFFFF, step, -COLOUR_SPAN - step)
+            green_cover = level(lax.shift_right_logical(word, 16), steps_hi, start_hi)
             cover = jnp.where(low_rows, pltpu.roll(green_cover, 4, 0), green_cover)
             if piece == 0:
                 low, high, transmit = red_blue, green_cover, 1.0 - cover
@@ -308,6 +334,13 @@
         coverage_ref[:, lanes_of(t)] = high[4:]
 
 
+def neighbours(last, initial, axis):
+    count = lax.axis_size(axis)
+    up = [(i, i + 1) for i in range(count - 1)]
+    down = [(j, i) for i, j in up]
+    return lax.ppermute(last, axis, up), lax.ppermute(initial, axis, down)
+
+
 def cost(flops, moved):
     return pl.CostEstimate(flops=flops, bytes_accessed=moved, transcendentals=0)
 
@@ -325,11 +358,12 @@
     def whole(*shape):
         return pl.BlockSpec(shape, lambda n: (0,) * len(shape))
 
-    x_edges, y_edges, front, rear = pl.pallas_call(
+    top, bottom, y_edges, front, rear = pl.pallas_call(
         edges_kernel,
         grid=(1,),
         out_shape=(
-            jax.ShapeDtypeStruct((2, depth, cols), volume.dtype),
+            jax.ShapeDtypeStruct((depth, cols), volume.dtype),
+            jax.ShapeDtypeStruct((depth, cols), volume.dtype),
             jax.ShapeDtypeStruct((rows, LANES), f32),
             jax.ShapeDtypeStruct((rows, cols), volume.dtype),
             jax.ShapeDtypeStruct((rows, cols), volume.dtype),
@@ -342,62 +376,71 @@
             pl.BlockSpec((1, rows, cols), lambda n: (0, 0, 0)),
             pl.BlockSpec((1, rows, cols), lambda n: (depth - 1, 0, 0)),
         ],
-        out_specs=(whole(2, depth, cols), whole(rows, LANES), whole(rows, cols), whole(rows, cols)),
+        out_specs=(whole(depth, cols), whole(depth, cols), whole(rows, LANES), whole(rows, cols), whole(rows, cols)),
         scratch_shapes=[pltpu.VMEM((2, depth, cols), f32)],
         compiler_params=params,
         cost_estimate=cost(1 << 20, 2 << 20),
         name="edges",
     )(*[volume] * 6)
-    x_all = lax.all_gather(x_edges, "gx")
-    y_all = lax.all_gather(y_edges, "gy")
-    up = [(i, i + 1) for i in range(count - 1)]
-    down = [(j, i) for i, j in up]
-    bz = lax.ppermute(rear, "gz", up)
-    az = lax.ppermute(front, "gz", down)
-
+    bz, az = neighbours(rear, front, "gz")
+    by, ay = neighbours(y_edges, y_edges, "gy")
+    bx, ax = neighbours(bottom, top, "gx")
+    spread_shape = jax.ShapeDtypeStruct((tiles, depth, PITCH * GROUPS, LANES), f32)
     cells, grads = pl.pallas_call(
         spread_kernel,
-        out_shape=(
-            jax.ShapeDtypeStruct((tiles, depth, PITCH * GROUPS, LANES), f32),
-            jax.ShapeDtypeStruct((tiles, depth, PITCH * GROUPS, LANES), f32),
-        ),
+        out_shape=(spread_shape, spread_shape),
         in_specs=[vmem],
         out_specs=(vmem, vmem),
         compiler_params=params,
         cost_estimate=cost(1 << 23, 2 << 20),
         name="spread",
     )(volume)
-
     tables = (knot_bins, tf_colour, tf_density)
-    words = jax.ShapeDtypeStruct((count * tiles * SUB, LANES), jnp.int32)
-    side_shape = (2, tiles, PITCH * GROUPS, LANES)
-    inner, sides = pl.pallas_call(
-        functools.partial(inner_kernel, depth_total=depth_total),
-        out_shape=(words, jax.ShapeDtypeStruct(side_shape, f32)),
-        in_specs=[smem] * 3 + [vmem] * 4,
-        out_specs=(vmem, vmem),
-        scratch_shapes=[pltpu.VMEM((40, SUB, LANES), f32)],
+    consts = [pltpu.VMEM((40, SUB, LANES), f32)]
+    theirs, cells, grads, sides = pl.pallas_call(
+        functools.partial(theirs_kernel, depth_total=depth_total),
+        out_shape=(
+            jax.ShapeDtypeStruct((8, tiles, SUB, LANES), jnp.int32),
+            spread_shape,
+            spread_shape,
+            jax.ShapeDtypeStruct((2, tiles, PITCH * GROUPS, LANES), f32),
+        ),
+        in_specs=[smem] * 3 + [vmem] * 8,
+        out_specs=(vmem,) * 4,
+        input_output_aliases={3: 1, 4: 2},
+        scratch_shapes=consts,
         compiler_params=params,
         cost_estimate=cost(1 << 26, 1 << 23),
-        name="inner",
-    )(*tables, cells, grads, bz, az)
-    codes = pl.pallas_call(
-        functools.partial(outer_kernel, depth_total=depth_total),
-        out_shape=words,
-        in_specs=[smem] * 3 + [vmem] * 6,
+        name="theirs",
+    )(*tables, cells, grads, bx, ax, by, ay, bz, az)
+    pairs = [(i, i ^ 1) for i in range(count)]
+    arrived = lax.ppermute(theirs, "gz", pairs)
+    ours = pl.pallas_call(
+        functools.partial(ours_kernel, depth_total=depth_total),
+        out_shape=jax.ShapeDtypeStruct((16, tiles, SUB, LANES), f32),
+        in_specs=[smem] * 3 + [vmem] * 3,
         out_specs=vmem,
-        input_output_aliases={8: 0},
-        scratch_shapes=[
-            pltpu.VMEM((2, depth, cols), f32),
-            pltpu.VMEM((2, rows, LANES), f32),
-            pltpu.VMEM((40, SUB, LANES), f32),
-        ],
+        scratch_shapes=consts,
         compiler_params=params,
         cost_estimate=cost(1 << 26, 1 << 23),
-        name="outer",
-    )(*tables, cells, grads, sides, x_all, y_all, inner)
+        name="ours",
+    )(*tables, cells, grads, sides)
+    half = count // 2
+    codes = pl.pallas_call(
+        pair_kernel,
+        out_shape=jax.ShapeDtypeStruct((half * tiles * SUB, LANES), jnp.int32),
+        in_specs=[vmem] * 2,
+        out_specs=vmem,
+        compiler_params=params,
+        name="pair",
+    )(ours, arrived)
     pieces = lax.all_to_all(
-        codes.reshape(count, tiles * SUB, LANES), "gz", split_axis=0, concat_axis=0, tiled=True
+        codes.reshape(half, tiles * SUB, LANES),
+        "gz",
+        split_axis=0,
+        concat_axis=0,
+        tiled=True,
+        axis_index_groups=[[2 * i + e for i in range(half)] for e in range(2)],
     )
     band = rows // count
     return pl.pallas_call(

time: 94.3 us -> 78.1 us (0.83)
  the two profiles are of different devices: /device:TPU:32 before, /device:TPU:10 now
where the time goes in v2:
time: 78.1 us; the launch traced here: 77.7 us
  blocking collectives  36.2 us (46%)
  starting transfers between devices  21 us (27%)
  Pallas kernels  17.9 us (23%)
  local copies, waits for them, and re-layouts  1.6 us (2%)
  between operations  0.8 us (1%)
    all_to_all x1, blocking collectives, on_device(): lax.all_to_all(codes.reshape(half, tiles * SUB, LANES), 'gz', split_axis=...  36.2 us
    ppermute x6, starting transfers between devices, neighbours(): return (lax.ppermute(last, axis, up), lax.ppermute(initial, axis, down))  16.5 us
    pallas_call x1, Pallas kernels, on_device(): pl.pallas_call(functools.partial(theirs_kernel, depth_total=depth_total),...  7.09 us
    pallas_call x1, Pallas kernels, on_device(): pl.pallas_call(functools.partial(ours_kernel, depth_total=depth_total), o...  5.66 us
    ppermute x1, starting transfers between devices, on_device(): arrived = lax.ppermute(theirs, 'gz', pairs)  4.5 us
    pallas_call x1, Pallas kernels, on_device(): pl.pallas_call(spread_kernel, out_shape=(spread_shape, spread_shape), in_...  2.45 us
    pallas_call x1, Pallas kernels, on_device(): pl.pallas_call(compose_kernel, out_shape=(jax.ShapeDtypeStruct((3, band,...  1.77 us
    unnamed x8, local copies, waits for them, and re-layouts  1.6 us
  transfers between devices with their start and end apart: 7, of which 1 were waited for; matrix products, arithmetic and copies ran while one was open for 0% of the time, Pallas kernels for 10%

profile of v2, /device:TPU:10, one launch (start us, length us, event | category | flops | bytes accessed | tf_op | source)
XLA Modules:
  0.0 77.7 jit_solution(15590617846957837198)
XLA Ops:
  0.6 0.0 copy-start
  0.6 1.6 %copy-done = bf16[16,64,1024]{2,1,0:T(8,128)(2,1)S(1)} copy-done((bf16[16,64,1024]{2,1,0:T(8,128)(2,1)S(1)}, bf16[16,64,1024]{2,1,0:T(8,128)(2,1)}, u32[]{:S(2)}) %copy-start) | copy-done | bytes 2097176
  2.2 0.3 edges.1
  2.5 3.8 %collective-permute-start.4 = (bf16[64,1024]{1,0:T(8,128)(2,1)S(1)}, bf16[64,1024]{1,0:T(8,128)(2,1)S(1)}, u32[]{:S(2)}, u32[]{:S(2)}) collective-permute-start(bf16[64,1024]{1,0:T(8,128)(2,1)S(1)} %get-tuple-element.18), channel_id=1, source_target_pairs={{0,1},{1,2},{2,3},{3,4},{4,5},{5,6},{6,7},{7,8},{8,9},{9,10},{10,1... | collective-permute-start | bytes 393224 | tf_op jit(solution)/shard_map/ppermute | solution.py:341
  6.4 1.3 %collective-permute-start.5 = (bf16[64,1024]{1,0:T(8,128)(2,1)S(1)}, bf16[64,1024]{1,0:T(8,128)(2,1)S(1)}, u32[]{:S(2)}, u32[]{:S(2)}) collective-permute-start(bf16[64,1024]{1,0:T(8,128)(2,1)S(1)} %get-tuple-element.19), channel_id=1, source_target_pairs={{1,0},{2,1},{3,2},{4,3},{5,4},{6,5},{7,6},{8,7},{9,8},{10,9},{11,1... | collective-permute-start | bytes 393224 | tf_op jit(solution)/shard_map/ppermute | solution.py:341
  7.7 1.9 %collective-permute-start = (bf16[16,1024]{1,0:T(8,128)(2,1)S(1)}, bf16[16,1024]{1,0:T(8,128)(2,1)S(1)}, u32[]{:S(2)}, u32[]{:S(2)}) collective-permute-start(bf16[16,1024]{1,0:T(8,128)(2,1)S(1)} %get-tuple-element.15), channel_id=1, source_target_pairs={{0,64},{64,128},{128,192},{192,256},{256,320},{320,384},{384,448},... | collective-permute-start | bytes 98312 | tf_op jit(solution)/shard_map/ppermute | solution.py:341
  9.6 3.6 %collective-permute-start.1 = (bf16[16,1024]{1,0:T(8,128)(2,1)S(1)}, bf16[16,1024]{1,0:T(8,128)(2,1)S(1)}, u32[]{:S(2)}, u32[]{:S(2)}) collective-permute-start(bf16[16,1024]{1,0:T(8,128)(2,1)S(1)} %get-tuple-element.16), channel_id=1, source_target_pairs={{64,0},{128,64},{192,128},{256,192},{320,256},{384,320},{448,384},... | collective-permute-start | bytes 98312 | tf_op jit(solution)/shard_map/ppermute | solution.py:341
  13.3 2.4 %collective-permute-start.3 = (f32[64,128]{1,0:T(8,128)S(1)}, f32[64,128]{1,0:T(8,128)S(1)}, u32[]{:S(2)}, u32[]{:S(2)}) collective-permute-start(f32[64,128]{1,0:T(8,128)S(1)} %get-tuple-element.17), channel_id=1, source_target_pairs={{16,0},{32,16},{48,32},{17,1},{33,17},{49,33},{18,2},{34,18},{50,3... | collective-permute-start | bytes 98312 | tf_op jit(solution)/shard_map/ppermute | solution.py:341
  15.7 0.0 collective-permute-done.bx_ref
  15.7 3.4 %collective-permute-start.2 = (f32[64,128]{1,0:T(8,128)S(1)}, f32[64,128]{1,0:T(8,128)S(1)}, u32[]{:S(2)}, u32[]{:S(2)}) collective-permute-start(f32[64,128]{1,0:T(8,128)S(1)} %get-tuple-element.17), channel_id=1, source_target_pairs={{0,16},{16,32},{32,48},{1,17},{17,33},{33,49},{2,18},{18,34},{34,5... | collective-permute-start | bytes 98312 | tf_op jit(solution)/shard_map/ppermute | solution.py:341
  19.1 2.5 %spread.1 = (f32[8,16,72,128]{3,2,1,0:T(8,128)S(1)}, f32[8,16,72,128]{3,2,1,0:T(8,128)S(1)}) custom-call(bf16[16,64,1024]{2,1,0:T(8,128)(2,1)S(1)} %copy-done), custom_call_target="tpu_custom_call" | custom-call | flops 8388608 | bytes 2097152 | tf_op jit(solution)/shard_map/spread/pallas_call | solution.py:389
  21.6 0.0 collective-permute-done.1.ax_ref
  21.6 0.0 collective-permute-done.3.ay_ref
  21.6 0.0 collective-permute-done.2.by_ref
  21.6 0.0 collective-permute-done.4.bz_ref
  21.6 0.0 collective-permute-done.5.az_ref
  21.6 0.0 copy-done.1
  21.7 7.1 %theirs.1 = (s32[8,8,8,128]{3,2,1,0:T(8,128)S(1)}, f32[8,16,72,128]{3,2,1,0:T(8,128)S(1)}, f32[8,16,72,128]{3,2,1,0:T(8,128)S(1)}, f32[2,8,72,128]{3,2,1,0:T(8,128)S(1)}) custom-call(s32[8]{0:T(128)S(1)} %copy-done.2, f32[3,8]{1,0:T(4,128)S(1)} %copy-done.1, f32[8]{0:T(128)S(1)} %copy-done.3, ...), custom_call_target="tpu_custom_call", output_to_operand_aliasing={{1}: (3, {}), {2}: (4, {})} | custom-call | flops 67108864 | bytes 8388608 | tf_op jit(solution)/shard_map/theirs/pallas_call | solution.py:400
  28.8 4.5 %collective-permute-start.6 = (s32[8,8,8,128]{3,2,1,0:T(8,128)S(1)}, s32[8,8,8,128]{3,2,1,0:T(8,128)S(1)}, u32[]{:S(2)}, u32[]{:S(2)}) collective-permute-start(s32[8,8,8,128]{3,2,1,0:T(8,128)S(1)} %get-tuple-element.23), channel_id=1, source_target_pairs={{0,1},{1,0},{2,3},{3,2},{4,5},{5,4},{6,7},{7,6},{8,9},{9,8},{10,11... | collective-permute-start | bytes 786440 | tf_op jit(solution)/shard_map/ppermute | solution.py:417
  33.3 5.7 %ours.1.ours_ref = f32[16,8,8,128]{3,2,1,0:T(8,128)S(1)} custom-call(s32[8]{0:T(128)S(1)} %copy-done.2, f32[3,8]{1,0:T(4,128)S(1)} %copy-done.1, f32[8]{0:T(128)S(1)} %copy-done.3, f32[8,16,72,128]{3,2,1,0:T(8,128)S(1)} %get-tuple-element.20.cells, f32[8,16,72,128]{3,2,1,0:T(8,128)S(1)} %get-tuple-element.21.grads, f32[2,8,72,128]{3,2,1,0:T(8,128)S(1)} %get-tuple-element.22.sides), custom_call_target="tpu_custom_call" | custom-call | flops 67108864 | bytes 8388608 | tf_op jit(solution)/shard_map/ours/pallas_call | solution.py:418
  38.9 0.2 collective-permute-done.6.theirs_ref
  39.1 0.6 pair.1
  39.7 36.2 %all_to_all.5.pieces_ref = s32[8,64,128]{2,1,0:T(8,128)} all-to-all(s32[8,64,128]{2,1,0:T(8,128)S(1)} %bitcast.1), channel_id=1, replica_groups={{0,2,4,6,8,10,12,14},{1,3,5,7,9,11,13,15},{16,18,20,22,24,26,28,30},{17..., dimensions={0} | all-to-all | bytes 524288 | tf_op jit(solution)/shard_map/all_to_all | solution.py:437
  76.0 1.8 %compose.1 = (f32[3,4,1024]{2,1,0:T(4,128)}, f32[4,1024]{1,0:T(4,128)}) custom-call(f32[3,8]{1,0:T(4,128)} %colour_ref.5, s32[8,64,128]{2,1,0:T(8,128)} %all_to_all.5.pieces_ref), custom_call_target="tpu_custom_call" | custom-call | tf_op jit(solution)/shard_map/compose/pallas_call | solution.py:446
  (5 shorter events, 0.0 us)
Async XLA Ops:
  0.6 1.6 %copy-start = (bf16[16,64,1024]{2,1,0:T(8,128)(2,1)S(1)}, bf16[16,64,1024]{2,1,0:T(8,128)(2,1)}, u32[]{:S(2)}) copy-start(bf16[16,64,1024]{2,1,0:T(8,128)(2,1)} %z_high.1) | copy-start | bytes 6291460
  2.2 19.4 %copy-start.1 = (f32[3,8]{1,0:T(4,128)S(1)}, f32[3,8]{1,0:T(4,128)}, u32[]{:S(2)}) copy-start(f32[3,8]{1,0:T(4,128)} %colour_ref.5) | copy-start | bytes 292
  2.2 19.4 %copy-start.2 = (s32[8]{0:T(128)S(1)}, s32[8]{0:T(128)}, u32[]{:S(2)}) copy-start(s32[8]{0:T(128)} %knots_ref.3) | copy-start | bytes 100
  2.2 19.4 %copy-start.3 = (f32[8]{0:T(128)S(1)}, f32[8]{0:T(128)}, u32[]{:S(2)}) copy-start(f32[8]{0:T(128)} %density_ref.3) | copy-start | bytes 100
  2.5 19.1 %collective-permute-start.4 = (bf16[64,1024]{1,0:T(8,128)(2,1)S(1)}, bf16[64,1024]{1,0:T(8,128)(2,1)S(1)}, u32[]{:S(2)}, u32[]{:S(2)}) collective-permute-start(bf16[64,1024]{1,0:T(8,128)(2,1)S(1)} %get-tuple-element.18), channel_id=1, source_target_pairs={{0,1},{1,2},{2,3},{3,4},{4,5},{5,6},{6,7},{7,8},{8,9},{9,10},{10,1... | collective-permute-start | bytes 393224 | tf_op jit(solution)/shard_map/ppermute | solution.py:341
  6.4 15.3 %collective-permute-start.5 = (bf16[64,1024]{1,0:T(8,128)(2,1)S(1)}, bf16[64,1024]{1,0:T(8,128)(2,1)S(1)}, u32[]{:S(2)}, u32[]{:S(2)}) collective-permute-start(bf16[64,1024]{1,0:T(8,128)(2,1)S(1)} %get-tuple-element.19), channel_id=1, source_target_pairs={{1,0},{2,1},{3,2},{4,3},{5,4},{6,5},{7,6},{8,7},{9,8},{10,9},{11,1... | collective-permute-start | bytes 393224 | tf_op jit(solution)/shard_map/ppermute | solution.py:341
  7.7 8.0 %collective-permute-start = (bf16[16,1024]{1,0:T(8,128)(2,1)S(1)}, bf16[16,1024]{1,0:T(8,128)(2,1)S(1)}, u32[]{:S(2)}, u32[]{:S(2)}) collective-permute-start(bf16[16,1024]{1,0:T(8,128)(2,1)S(1)} %get-tuple-element.15), channel_id=1, source_target_pairs={{0,64},{64,128},{128,192},{192,256},{256,320},{320,384},{384,448},... | collective-permute-start | bytes 98312 | tf_op jit(solution)/shard_map/ppermute | solution.py:341
  9.6 12.0 %collective-permute-start.1 = (bf16[16,1024]{1,0:T(8,128)(2,1)S(1)}, bf16[16,1024]{1,0:T(8,128)(2,1)S(1)}, u32[]{:S(2)}, u32[]{:S(2)}) collective-permute-start(bf16[16,1024]{1,0:T(8,128)(2,1)S(1)} %get-tuple-element.16), channel_id=1, source_target_pairs={{64,0},{128,64},{192,128},{256,192},{320,256},{384,320},{448,384},... | collective-permute-start | bytes 98312 | tf_op jit(solution)/shard_map/ppermute | solution.py:341
  13.3 8.3 %collective-permute-start.3 = (f32[64,128]{1,0:T(8,128)S(1)}, f32[64,128]{1,0:T(8,128)S(1)}, u32[]{:S(2)}, u32[]{:S(2)}) collective-permute-start(f32[64,128]{1,0:T(8,128)S(1)} %get-tuple-element.17), channel_id=1, source_target_pairs={{16,0},{32,16},{48,32},{17,1},{33,17},{49,33},{18,2},{34,18},{50,3... | collective-permute-start | bytes 98312 | tf_op jit(solution)/shard_map/ppermute | solution.py:341
  15.7 5.9 %collective-permute-start.2 = (f32[64,128]{1,0:T(8,128)S(1)}, f32[64,128]{1,0:T(8,128)S(1)}, u32[]{:S(2)}, u32[]{:S(2)}) collective-permute-start(f32[64,128]{1,0:T(8,128)S(1)} %get-tuple-element.17), channel_id=1, source_target_pairs={{0,16},{16,32},{32,48},{1,17},{17,33},{33,49},{2,18},{18,34},{34,5... | collective-permute-start | bytes 98312 | tf_op jit(solution)/shard_map/ppermute | solution.py:341
  28.8 10.4 %collective-permute-start.6 = (s32[8,8,8,128]{3,2,1,0:T(8,128)S(1)}, s32[8,8,8,128]{3,2,1,0:T(8,128)S(1)}, u32[]{:S(2)}, u32[]{:S(2)}) collective-permute-start(s32[8,8,8,128]{3,2,1,0:T(8,128)S(1)} %get-tuple-element.23), channel_id=1, source_target_pairs={{0,1},{1,0},{2,3},{3,2},{4,5},{5,4},{6,7},{7,6},{8,9},{9,8},{10,11... | collective-permute-start | bytes 786440 | tf_op jit(solution)/shard_map/ppermute | solution.py:417

commit v3 on v2

--- a/solution.py
+++ b/solution.py
@@ -15,8 +15,10 @@
 AMBIENT = 0.2
 LANES = 128
 SUB = 8
-GROUPS = 8
-PITCH = 9
+QUAD = 4
+STEP = 4
+MARGIN = 4
+SCALES = 38
 
 COLOUR_SPAN = 26.0
 COVER_SPAN = 9.0
@@ -37,9 +39,12 @@
 
 def opacity_terms(largest):
     half = 0.5 * largest
-    nodes = [half + half * math.cos(math.pi * (2 * i + 1) / 8.0) for i in range(4)]
+    nodes = [half + half * math.cos(math.pi * (2 * i + 1) / 6.0) for i in range(3)]
     values = [-math.expm1(-y) / y for y in nodes]
-    return [float(c) for c in np.polynomial.polynomial.polyfit(nodes, values, 3)]
+    c0, c1, c2 = (float(c) for c in np.polynomial.polynomial.polyfit(nodes, values, 2))
+    k = c2 ** (1.0 / 3.0)
+    a = c1 / (2.0 * k * k)
+    return k, a, c0 / k - a * a
 
 
 def full(x):
@@ -65,7 +70,7 @@
     top[...] = rows_x[0].astype(top.dtype)
     bottom[...] = rows_x[1].astype(bottom.dtype)
     lane = lane_index()
-    for i in range(GROUPS // 2):
+    for i in range(y_low.shape[1] // 16):
         sides = [jnp.zeros((SUB, LANES), jnp.float32)] * 2
         for z in range(depth):
             low = y_low[z, 16 * i:16 * i + 16, :].astype(jnp.float32)
@@ -75,15 +80,20 @@
                 sides[part] = jnp.where(lane == z, low[at, :1], sides[part])
                 sides[part] = jnp.where(lane == depth + z, high[at, LANES - 1:], sides[part])
         for part in range(2):
-            y_out[pl.ds(2 * i + part, SUB, stride=GROUPS), :] = sides[part]
+            y_out[pl.ds(SUB * STEP * part + i, SUB, stride=STEP), :] = sides[part]
     front[...] = z_low[0]
     rear[...] = z_high[0]
 
 
-def spread_kernel(vol_ref, cells, grads):
+def slots_of(i):
+    return pl.ds(MARGIN + SUB * STEP * (i % 2) + i // 2, SUB, stride=STEP)
+
+
+def spread_kernel(knots_ref, colour_ref, density_ref, vol_ref, cells, grads, consts, *, depth_total):
     depth, rows, cols = vol_ref.shape
     lane = lax.broadcasted_iota(jnp.int32, (16, LANES), 1)
     tiles = cols // LANES
+    prepare(consts, knots_ref, colour_ref, density_ref, depth_total)
 
     def step(z, carry):
         for c in range(rows // 16):
@@ -99,10 +109,14 @@
                 across = r - l
                 own = plane[:, lanes_of(t)]
                 for part in range(2):
-                    i = 2 * c + part
                     at = slice(8 * part, 8 * part + 8)
-                    cells[t, z, pl.ds(i, SUB, stride=PITCH), :] = own[at]
-                    grads[t, z, pl.ds(i, SUB, stride=PITCH), :] = across[at]
+                    cells[t, z, slots_of(2 * c + part), :] = own[at]
+                    grads[t, z, slots_of(2 * c + part), :] = across[at]
+                if c:
+                    slot = MARGIN + rows + c - 1
+                    cells[t, z, slot:slot + 1, :] = own[:1]
+                if c < rows // 16 - 1:
+                    cells[t, z, c + 1:c + 2, :] = own[15:]
         return carry
 
     lax.fori_loop(0, depth, step, 0)
@@ -117,12 +131,14 @@
         spans.append((high - low) * (1.0 / top))
         if k:
             consts[k - 1] = low / top
-    consts[6] = full(density_ref[0]) * (1.0 / depth_total)
+    unit = opacity_terms(10.0 / depth_total)[0] / depth_total
+    consts[6] = full(density_ref[0]) * unit
     for k in range(SEGMENTS):
         step = full(density_ref[k + 1]) - full(density_ref[k])
-        consts[7 + k] = step * (1.0 / depth_total) / spans[k]
+        consts[7 + k] = step * unit / spans[k]
     for c in range(3):
         scale = full(colour_scale(colour_ref, c))
+        consts[SCALES + c] = scale
         consts[14 + 8 * c] = full(colour_ref[c, 0]) / scale
         for k in range(SEGMENTS):
             step = full(colour_ref[c, k + 1]) - full(colour_ref[c, k])
@@ -130,7 +146,7 @@
 
 
 def composite(consts, cell, grad_x, grad_y, depth, depth_total):
-    c0, c1, c2, c3 = opacity_terms(10.0 / depth_total)
+    _, shift, rest = opacity_terms(10.0 / depth_total)
     points = [consts[k] for k in range(6)]
     first = consts[6]
     slopes = [consts[7 + k] for k in range(SEGMENTS)]
@@ -151,7 +167,8 @@
         y = first
         for k in range(SEGMENTS):
             y = y + ramps[k] * slopes[k]
-        taken = transmit * (y * (c0 + y * (c1 + y * (c2 + y * c3))))
+        shifted = y + shift
+        taken = transmit * (y * (shifted * shifted + rest))
         transmit = transmit - taken
         shaded = taken * shading
         if z == 0:
@@ -175,22 +192,21 @@
         plane = ref[16 * c:16 * c + 16, :].astype(jnp.float32)
         for t in range(sides.shape[1]):
             for part in range(2):
-                own = plane[8 * part:8 * part + 8, lanes_of(t)]
-                sides[side, t, pl.ds(2 * c + part, SUB, stride=PITCH), :] = own
+                sides[side, t, slots_of(2 * c + part), :] = plane[8 * part:8 * part + 8, lanes_of(t)]
 
 
 def place_edges(cells, grads, bx_ref, ax_ref, by_ref, ay_ref):
-    tiles, depth = cells.shape[:2]
-    for slot, ref in ((PITCH * (GROUPS - 1) - 1, bx_ref), (GROUPS, ax_ref)):
+    tiles, depth, slots = cells.shape[:3]
+    for slot, ref in ((0, bx_ref), (slots - 1, ax_ref)):
         edge = ref[...].astype(jnp.float32)
         for z in range(depth):
             for t in range(tiles):
                 cells[t, z, slot:slot + 1, :] = edge[z:z + 1, lanes_of(t)]
     lane = lane_index()
 
-    def step(r, carry):
-        rows = pl.ds(pl.multiple_of(SUB * r, SUB), SUB)
-        at = pl.ds(PITCH * r, SUB)
+    def step(g, carry):
+        rows = pl.ds(pl.multiple_of(SUB * g, SUB), SUB)
+        at = pl.ds(SUB * g + MARGIN, SUB)
         before, after = by_ref[rows, :], ay_ref[rows, :]
         for z in range(depth):
             first = jnp.where(lane == 0, before[:, depth + z:depth + z + 1], 0.0)
@@ -199,18 +215,16 @@
             grads[tiles - 1, z, at, :] = grads[tiles - 1, z, at, :] + last
         return carry
 
-    lax.fori_loop(0, GROUPS, step, 0)
-
-
-def half_loop(consts, cells, grads, sides, parity, depth_total, store):
+    lax.fori_loop(0, by_ref.shape[0] // SUB, step, 0)
+
+
+def quarter_loop(consts, cells, grads, sides, owner, depth_total, store):
     tiles, depth = cells.shape[:2]
 
-    def tile_step(t, carry):
-        def row_step(j, carry):
-            r = 4 * parity + j
-            at = pl.ds(PITCH * r, SUB)
-            above = pl.ds(jnp.where(r == 0, PITCH * (GROUPS - 1) - 1, PITCH * r - PITCH), SUB)
-            below = pl.ds(jnp.where(r == GROUPS - 1, 1, PITCH * r + PITCH), SUB)
+    def step(t, carry):
+        for p in range(2):
+            start = MARGIN + STEP * (4 * owner + 2 * p)
+            at, above, below = (pl.ds(start + shift, SUB) for shift in (0, -STEP, STEP))
 
             def cell(z):
                 if z < 0:
@@ -227,12 +241,10 @@
                 depth,
                 depth_total,
             )
-            store(t, j, values)
-            return carry
-
-        return lax.fori_loop(0, 4, row_step, carry, unroll=2)
-
-    lax.fori_loop(0, tiles, tile_step, 0)
+            store(t, p, values)
+        return carry
+
+    lax.fori_loop(0, tiles, step, 0)
 
 
 def pack(values):
@@ -245,65 +257,80 @@
     return jnp.where(code > 0, value, 0.0)
 
 
-def theirs_kernel(
-    knots_ref, colour_ref, density_ref, cells_in, grads_in, bx_ref, ax_ref, by_ref, ay_ref, bz_ref, az_ref,
-    out_ref, cells, grads, sides, consts, *, depth_total,
+def place_in_quad():
+    return lax.rem(lax.axis_index("gz"), QUAD)
+
+
+def send_quarter(consts, cells, grads, sides, out_ref, mate, depth_total):
+    def store(t, p, values):
+        first, second = pack(values)
+        out_ref[p, t] = first
+        out_ref[2 + p, t] = second
+
+    quarter_loop(consts, cells, grads, sides, place_in_quad() ^ mate, depth_total, store)
+
+
+def first_kernel(
+    consts, cells_in, grads_in, bx_ref, ax_ref, by_ref, ay_ref, bz_ref, az_ref,
+    out_ref, cells, grads, sides, *, mate, depth_total,
 ):
-    prepare(consts, knots_ref, colour_ref, density_ref, depth_total)
     spread_side(bz_ref, sides, 0)
     spread_side(az_ref, sides, 1)
     place_edges(cells, grads, bx_ref, ax_ref, by_ref, ay_ref)
-
-    def store(t, j, values):
-        first, second = pack(values)
-        out_ref[j, t] = first
-        out_ref[4 + j, t] = second
-
-    parity = 1 - lax.rem(lax.axis_index("gz"), 2)
-    half_loop(consts, cells, grads, sides, parity, depth_total, store)
-
-
-def ours_kernel(
-    knots_ref, colour_ref, density_ref, cells, grads, sides, out_ref, consts, *, depth_total,
-):
-    prepare(consts, knots_ref, colour_ref, density_ref, depth_total)
-
-    def store(t, j, values):
+    send_quarter(consts, cells, grads, sides, out_ref, mate, depth_total)
+
+
+def later_kernel(consts, cells, grads, sides, _, out_ref, *, mate, depth_total):
+    send_quarter(consts, cells, grads, sides, out_ref, mate, depth_total)
+
+
+def ours_kernel(consts, cells, grads, sides, _, out_ref, *, depth_total):
+    def store(t, p, values):
         for c in range(4):
-            out_ref[4 * c + j, t] = values[c]
-
-    parity = lax.rem(lax.axis_index("gz"), 2)
-    half_loop(consts, cells, grads, sides, parity, depth_total, store)
-
-
-def pair_kernel(ours_ref, theirs_ref, out_ref):
+            out_ref[2 * c + p, t] = values[c]
+
+    quarter_loop(consts, cells, grads, sides, place_in_quad(), depth_total, store)
+
+
+def quad_kernel(ours_ref, mate1_ref, mate2_ref, mate3_ref, out_ref):
     tiles = ours_ref.shape[1]
-    front = lax.rem(lax.axis_index("gz"), 2) == 0
-
-    def step(t, carry):
-        for j in range(4):
-            ours = [ours_ref[4 * c + j, t] for c in range(4)]
-            first, second = theirs_ref[j, t], theirs_ref[4 + j, t]
-            theirs = [
-                decode(first & 0xFFFF, COLOUR_SPAN),
-                decode(lax.shift_right_logical(first, 16), COLOUR_SPAN),
-                decode(second & 0xFFFF, COLOUR_SPAN),
-                decode(lax.shift_right_logical(second, 16), COVER_SPAN),
-            ]
-            keep_ours = jnp.where(front, 1.0, 1.0 - theirs[3])
-            keep_theirs = jnp.where(front, 1.0 - ours[3], 1.0)
-            words = pack([o * keep_ours + p * keep_theirs for o, p in zip(ours, theirs)])
-            for w in range(2):
-                out_ref[pl.ds(t * SUB + 4 * w + j, SUB, stride=tiles * SUB), :] = words[w]
-        return carry
-
-    lax.fori_loop(0, tiles, step, 0)
-
-
-def compose_kernel(colour_ref, pieces_ref, image_ref, coverage_ref):
+    mates = (ours_ref, mate1_ref, mate2_ref, mate3_ref)
+
+    def piece(k, t, p):
+        if k == 0:
+            return [ours_ref[2 * c + p, t] for c in range(4)]
+        first, second = mates[k][p, t], mates[k][2 + p, t]
+        return [
+            decode(first & 0xFFFF, COLOUR_SPAN),
+            decode(lax.shift_right_logical(first, 16), COLOUR_SPAN),
+            decode(second & 0xFFFF, COLOUR_SPAN),
+            decode(lax.shift_right_logical(second, 16), COVER_SPAN),
+        ]
+
+    for place in range(QUAD):
+
+        @pl.when(place_in_quad() == place)
+        def _():
+            def step(t, carry):
+                for p in range(2):
+                    total = piece(place, t, p)
+                    for other in range(1, QUAD):
+                        rear = piece(place ^ other, t, p)
+                        keep = 1.0 - total[3]
+                        total = [a + keep * b for a, b in zip(total, rear)]
+                    for w, word in enumerate(pack(total)):
+                        for q in range(2):
+                            row = t * SUB + 4 * w + 2 * p + q
+                            out_ref[pl.ds(row, 4, stride=tiles * SUB), :] = word[4 * q:4 * q + 4]
+                return carry
+
+            lax.fori_loop(0, tiles, step, 0)
+
+
+def compose_kernel(consts, pieces_ref, image_ref, coverage_ref):
     count = pieces_ref.shape[0]
     low_rows = lax.broadcasted_iota(jnp.int32, (SUB, LANES), 0) < 4
-    scales = [full(colour_scale(colour_ref, c)) for c in range(3)]
+    scales = [consts[SCALES + c] for c in range(3)]
     step = COLOUR_SPAN / CODES
     steps_hi = jnp.where(low_rows, step, COVER_SPAN / CODES)
     start_hi = jnp.where(low_rows, -COLOUR_SPAN - step, -COVER_SPAN - COVER_SPAN / CODES)
@@ -385,62 +412,77 @@
     bz, az = neighbours(rear, front, "gz")
     by, ay = neighbours(y_edges, y_edges, "gy")
     bx, ax = neighbours(bottom, top, "gx")
-    spread_shape = jax.ShapeDtypeStruct((tiles, depth, PITCH * GROUPS, LANES), f32)
-    cells, grads = pl.pallas_call(
-        spread_kernel,
-        out_shape=(spread_shape, spread_shape),
-        in_specs=[vmem],
-        out_specs=(vmem, vmem),
+    spread_shape = jax.ShapeDtypeStruct((tiles, depth, rows + 2 * MARGIN, LANES), f32)
+    consts_shape = jax.ShapeDtypeStruct((SCALES + 3, SUB, LANES), f32)
+    cells, grads, consts = pl.pallas_call(
+        functools.partial(spread_kernel, depth_total=depth_total),
+        out_shape=(spread_shape, spread_shape, consts_shape),
+        in_specs=[smem] * 3 + [vmem],
+        out_specs=(vmem,) * 3,
         compiler_params=params,
         cost_estimate=cost(1 << 23, 2 << 20),
         name="spread",
-    )(volume)
-    tables = (knot_bins, tf_colour, tf_density)
-    consts = [pltpu.VMEM((40, SUB, LANES), f32)]
-    theirs, cells, grads, sides = pl.pallas_call(
-        functools.partial(theirs_kernel, depth_total=depth_total),
+    )(knot_bins, tf_colour, tf_density, volume)
+    sent = jax.ShapeDtypeStruct((4, tiles, SUB, LANES), jnp.int32)
+    work = cost(1 << 26, 1 << 22)
+    arrived = {}
+
+    def send(words, mate):
+        arrived[mate] = lax.ppermute(words, "gz", [(i, i ^ mate) for i in range(count)])
+
+    words, cells, grads, sides = pl.pallas_call(
+        functools.partial(first_kernel, mate=2, depth_total=depth_total),
         out_shape=(
-            jax.ShapeDtypeStruct((8, tiles, SUB, LANES), jnp.int32),
+            sent,
             spread_shape,
             spread_shape,
-            jax.ShapeDtypeStruct((2, tiles, PITCH * GROUPS, LANES), f32),
+            jax.ShapeDtypeStruct((2, tiles, rows + 2 * MARGIN, LANES), f32),
         ),
-        in_specs=[smem] * 3 + [vmem] * 8,
+        in_specs=[vmem] * 9,
         out_specs=(vmem,) * 4,
-        input_output_aliases={3: 1, 4: 2},
-        scratch_shapes=consts,
+        input_output_aliases={1: 1, 2: 2},
         compiler_params=params,
-        cost_estimate=cost(1 << 26, 1 << 23),
-        name="theirs",
-    )(*tables, cells, grads, bx, ax, by, ay, bz, az)
-    pairs = [(i, i ^ 1) for i in range(count)]
-    arrived = lax.ppermute(theirs, "gz", pairs)
+        cost_estimate=work,
+        name="first",
+    )(consts, cells, grads, bx, ax, by, ay, bz, az)
+    send(words, 2)
+    later_specs = [vmem] * 4 + [pl.BlockSpec(memory_space=pl.ANY)]
+    for mate, behind in ((3, words), (1, arrived[2])):
+        words = pl.pallas_call(
+            functools.partial(later_kernel, mate=mate, depth_total=depth_total),
+            out_shape=sent,
+            in_specs=later_specs,
+            out_specs=vmem,
+            compiler_params=params,
+            cost_estimate=work,
+            name="later",
+        )(consts, cells, grads, sides, behind)
+        send(words, mate)
     ours = pl.pallas_call(
         functools.partial(ours_kernel, depth_total=depth_total),
-        out_shape=jax.ShapeDtypeStruct((16, tiles, SUB, LANES), f32),
-        in_specs=[smem] * 3 + [vmem] * 3,
-        out_specs=vmem,
-        scratch_shapes=consts,
-        compiler_params=params,
-        cost_estimate=cost(1 << 26, 1 << 23),
-        name="ours",
-    )(*tables, cells, grads, sides)
-    half = count // 2
-    codes = pl.pallas_call(
-        pair_kernel,
-        out_shape=jax.ShapeDtypeStruct((half * tiles * SUB, LANES), jnp.int32),
-        in_specs=[vmem] * 2,
+        out_shape=jax.ShapeDtypeStruct((8, tiles, SUB, LANES), f32),
+        in_specs=later_specs,
         out_specs=vmem,
         compiler_params=params,
-        name="pair",
-    )(ours, arrived)
+        cost_estimate=work,
+        name="ours",
+    )(consts, cells, grads, sides, arrived[3])
+    quads = count // QUAD
+    codes = pl.pallas_call(
+        quad_kernel,
+        out_shape=jax.ShapeDtypeStruct((quads * tiles * SUB, LANES), jnp.int32),
+        in_specs=[vmem] * 4,
+        out_specs=vmem,
+        compiler_params=params,
+        name="quad",
+    )(ours, arrived[1], arrived[2], arrived[3])
     pieces = lax.all_to_all(
-        codes.reshape(half, tiles * SUB, LANES),
+        codes.reshape(quads, tiles * SUB, LANES),
         "gz",
         split_axis=0,
         concat_axis=0,
         tiled=True,
-        axis_index_groups=[[2 * i + e for i in range(half)] for e in range(2)],
+        axis_index_groups=[[QUAD * i + e for i in range(quads)] for e in range(QUAD)],
     )
     band = rows // count
     return pl.pallas_call(
@@ -449,10 +491,10 @@
             jax.ShapeDtypeStruct((3, band, cols), f32),
             jax.ShapeDtypeStruct((band, cols), f32),
         ),
-        in_specs=[smem, vmem],
+        in_specs=[vmem, vmem],
         out_specs=(vmem, vmem),
         name="compose",
-    )(tf_colour, pieces)
+    )(consts, pieces)
 
 
 def solution(mesh):

time: 78.1 us -> 79.1 us (1.013)
  starting transfers between devices: 21 us -> 29.4 us
  blocking collectives: 36.2 us -> 28 us
  waiting for transfers between devices: 0.2 us -> 2.13 us
  Pallas kernels: 17.9 us -> 16.5 us
    all_to_all x1, blocking collectives: 36.2 us -> 28 us  [on_device(): lax.all_to_all(codes.reshape(quads, tiles * SUB, LANES), 'gz', split_axis...]
    ppermute x1 -> x3, starting transfers between devices: 4.5 us -> 12.7 us  [send(): lax.ppermute(words, 'gz', [(i, i ^ mate) for i in range(count)])]
    pallas_call x1, Pallas kernels: 5.66 us -> 2.31 us  [on_device(): pl.pallas_call(functools.partial(ours_kernel, depth_total=depth_total), o...]
    pallas_call x3 -> x5, Pallas kernels: 10.1 us -> 12.2 us  [the longest x2 5.09 us: on_device(): pl.pallas_call(functools.partial(later_kernel, mate=mate, depth_total=dep...]
    ppermute x1 -> x3, waiting for transfers between devices: 0.19 us -> 2.11 us  [send(): lax.ppermute(words, 'gz', [(i, i ^ mate) for i in range(count)])]
    unnamed x8 -> x12, local copies, waits for them, and re-layouts: 1.6 us -> 1.6 us
  transfers between devices with their start and end apart: 7 -> 9, of which waited for: 1 -> 1; matrix products, arithmetic and copies ran while one was open for 0% -> 0% of each run, Pallas kernels for 10% -> 13%
where the time goes in v3:
time: 79.1 us; the launch traced here: 78.5 us
  starting transfers between devices  29.4 us (37%)
  blocking collectives  28 us (35%)
  Pallas kernels  16.5 us (21%)
  waiting for transfers between devices  2.13 us (3%)
  local copies, waits for them, and re-layouts  1.6 us (2%)
  between operations  0.86 us (1%)
    all_to_all x1, blocking collectives, on_device(): lax.all_to_all(codes.reshape(quads, tiles * SUB, LANES), 'gz', split_axis...  28 us
    ppermute x6, starting transfers between devices, neighbours(): return (lax.ppermute(last, axis, up), lax.ppermute(initial, axis, down))  16.7 us
    ppermute x3, starting transfers between devices, send(): lax.ppermute(words, 'gz', [(i, i ^ mate) for i in range(count)])  12.7 us
    pallas_call x2, Pallas kernels, on_device(): pl.pallas_call(functools.partial(later_kernel, mate=mate, depth_total=dep...  5.09 us
    pallas_call x1, Pallas kernels, on_device(): pl.pallas_call(functools.partial(first_kernel, mate=2, depth_total=depth_...  3.55 us
    pallas_call x1, Pallas kernels, on_device(): pl.pallas_call(functools.partial(spread_kernel, depth_total=depth_total),...  3.07 us
    pallas_call x1, Pallas kernels, on_device(): pl.pallas_call(functools.partial(ours_kernel, depth_total=depth_total), o...  2.31 us
    ppermute x3, waiting for transfers between devices, send(): lax.ppermute(words, 'gz', [(i, i ^ mate) for i in range(count)])  2.11 us
  transfers between devices with their start and end apart: 9, of which 1 were waited for; matrix products, arithmetic and copies ran while one was open for 0% of the time, Pallas kernels for 13%

profile of v3, /device:TPU:10, one launch (start us, length us, event | category | flops | bytes accessed | tf_op | source)
XLA Modules:
  0.0 78.5 jit_solution(2705492156516012292)
XLA Ops:
  0.6 1.6 %copy-done = bf16[16,64,1024]{2,1,0:T(8,128)(2,1)S(1)} copy-done((bf16[16,64,1024]{2,1,0:T(8,128)(2,1)S(1)}, bf16[16,64,1024]{2,1,0:T(8,128)(2,1)}, u32[]{:S(2)}) %copy-start) | copy-done | bytes 2097176
  2.2 0.3 edges.1
  2.6 4.0 %collective-permute-start.4 = (bf16[64,1024]{1,0:T(8,128)(2,1)S(1)}, bf16[64,1024]{1,0:T(8,128)(2,1)S(1)}, u32[]{:S(2)}, u32[]{:S(2)}) collective-permute-start(bf16[64,1024]{1,0:T(8,128)(2,1)S(1)} %get-tuple-element.20), channel_id=1, source_target_pairs={{0,1},{1,2},{2,3},{3,4},{4,5},{5,6},{6,7},{7,8},{8,9},{9,10},{10,1... | collective-permute-start | bytes 393224 | tf_op jit(solution)/shard_map/ppermute | solution.py:368
  6.5 1.3 %collective-permute-start.5 = (bf16[64,1024]{1,0:T(8,128)(2,1)S(1)}, bf16[64,1024]{1,0:T(8,128)(2,1)S(1)}, u32[]{:S(2)}, u32[]{:S(2)}) collective-permute-start(bf16[64,1024]{1,0:T(8,128)(2,1)S(1)} %get-tuple-element.21), channel_id=1, source_target_pairs={{1,0},{2,1},{3,2},{4,3},{5,4},{6,5},{7,6},{8,7},{9,8},{10,9},{11,1... | collective-permute-start | bytes 393224 | tf_op jit(solution)/shard_map/ppermute | solution.py:368
  7.8 1.9 %collective-permute-start = (bf16[16,1024]{1,0:T(8,128)(2,1)S(1)}, bf16[16,1024]{1,0:T(8,128)(2,1)S(1)}, u32[]{:S(2)}, u32[]{:S(2)}) collective-permute-start(bf16[16,1024]{1,0:T(8,128)(2,1)S(1)} %get-tuple-element.17), channel_id=1, source_target_pairs={{0,64},{64,128},{128,192},{192,256},{256,320},{320,384},{384,448},... | collective-permute-start | bytes 98312 | tf_op jit(solution)/shard_map/ppermute | solution.py:368
  9.7 3.6 %collective-permute-start.1 = (bf16[16,1024]{1,0:T(8,128)(2,1)S(1)}, bf16[16,1024]{1,0:T(8,128)(2,1)S(1)}, u32[]{:S(2)}, u32[]{:S(2)}) collective-permute-start(bf16[16,1024]{1,0:T(8,128)(2,1)S(1)} %get-tuple-element.18), channel_id=1, source_target_pairs={{64,0},{128,64},{192,128},{256,192},{320,256},{384,320},{448,384},... | collective-permute-start | bytes 98312 | tf_op jit(solution)/shard_map/ppermute | solution.py:368
  13.4 2.4 %collective-permute-start.3 = (f32[64,128]{1,0:T(8,128)S(1)}, f32[64,128]{1,0:T(8,128)S(1)}, u32[]{:S(2)}, u32[]{:S(2)}) collective-permute-start(f32[64,128]{1,0:T(8,128)S(1)} %get-tuple-element.19), channel_id=1, source_target_pairs={{16,0},{32,16},{48,32},{17,1},{33,17},{49,33},{18,2},{34,18},{50,3... | collective-permute-start | bytes 98312 | tf_op jit(solution)/shard_map/ppermute | solution.py:368
  15.8 0.0 collective-permute-done.bx_ref
  15.9 3.4 %collective-permute-start.2 = (f32[64,128]{1,0:T(8,128)S(1)}, f32[64,128]{1,0:T(8,128)S(1)}, u32[]{:S(2)}, u32[]{:S(2)}) collective-permute-start(f32[64,128]{1,0:T(8,128)S(1)} %get-tuple-element.19), channel_id=1, source_target_pairs={{0,16},{16,32},{32,48},{1,17},{17,33},{33,49},{2,18},{18,34},{34,5... | collective-permute-start | bytes 98312 | tf_op jit(solution)/shard_map/ppermute | solution.py:368
  19.3 3.1 %spread.1 = (f32[8,16,72,128]{3,2,1,0:T(8,128)S(1)}, f32[8,16,72,128]{3,2,1,0:T(8,128)S(1)}, f32[41,8,128]{2,1,0:T(8,128)S(1)}) custom-call(s32[8]{0:T(128)S(1)} %copy-done.4, f32[3,8]{1,0:T(4,128)S(1)} %copy-done.3, f32[8]{0:T(128)S(1)} %copy-done.5, bf16[16,64,1024]{2,1,0:T(8,128)(2,1)S(1)} %copy-done.1), custom_call_target="tpu_custom_call" | custom-call | flops 8388608 | bytes 2097152 | tf_op jit(solution)/shard_map/spread/pallas_call | solution.py:417
  22.4 0.0 collective-permute-done.1.ax_ref
  22.4 0.0 collective-permute-done.3.ay_ref
  22.4 0.0 collective-permute-done.4.bz_ref
  22.5 3.6 %first.1 = (s32[4,8,8,128]{3,2,1,0:T(8,128)S(1)}, f32[8,16,72,128]{3,2,1,0:T(8,128)S(1)}, f32[8,16,72,128]{3,2,1,0:T(8,128)S(1)}, f32[2,8,72,128]{3,2,1,0:T(8,128)S(1)}) custom-call(f32[41,8,128]{2,1,0:T(8,128)S(1)} %get-tuple-element.14.consts, f32[8,16,72,128]{3,2,1,0:T(8,128)S(1)} %get-tuple-element.15.cells_in, ...), custom_call_target="tpu_custom_call", output_to_operand_aliasing={{1}: (1, {}), {2}: (2, {})} | custom-call | flops 67108864 | bytes 4194304 | tf_op jit(solution)/shard_map/first/pallas_call | solution.py:433
  26.0 5.9 %collective-permute-start.7 = (s32[4,8,8,128]{3,2,1,0:T(8,128)S(1)}, s32[4,8,8,128]{3,2,1,0:T(8,128)S(1)}, u32[]{:S(2)}, u32[]{:S(2)}) collective-permute-start(s32[4,8,8,128]{3,2,1,0:T(8,128)S(1)} %get-tuple-element.25._), channel_id=1, source_target_pairs={{0,2},{1,3},{2,0},{3,1},{4,6},{5,7},{6,4},{7,5},{8,10},{9,11},{10,... | collective-permute-start | bytes 393224 | tf_op jit(solution)/shard_map/ppermute | solution.py:431
  31.9 2.5 %later.2 = s32[4,8,8,128]{3,2,1,0:T(8,128)S(1)} custom-call(f32[41,8,128]{2,1,0:T(8,128)S(1)} %get-tuple-element.14.consts, f32[8,16,72,128]{3,2,1,0:T(8,128)S(1)} %get-tuple-element.22.cells, f32[8,16,72,128]{3,2,1,0:T(8,128)S(1)} %get-tuple-element.23.grads, f32[2,8,72,128]{3,2,1,0:T(8,128)S(1)} %get-tuple-element.24.sides, ...), custom_call_target="tpu_custom_call" | custom-call | flops 67108864 | bytes 4194304 | tf_op jit(solution)/shard_map/later/pallas_call | solution.py:451
  34.5 4.4 %collective-permute-start.6 = (s32[4,8,8,128]{3,2,1,0:T(8,128)S(1)}, s32[4,8,8,128]{3,2,1,0:T(8,128)S(1)}, u32[]{:S(2)}, u32[]{:S(2)}) collective-permute-start(s32[4,8,8,128]{3,2,1,0:T(8,128)S(1)} %later.2), channel_id=1, source_target_pairs={{0,3},{1,2},{2,1},{3,0},{4,7},{5,6},{6,5},{7,4},{8,11},{9,10},{10,... | collective-permute-start | bytes 393224 | tf_op jit(solution)/shard_map/ppermute | solution.py:431
  38.9 2.5 %later.3 = s32[4,8,8,128]{3,2,1,0:T(8,128)S(1)} custom-call(f32[41,8,128]{2,1,0:T(8,128)S(1)} %get-tuple-element.14.consts, f32[8,16,72,128]{3,2,1,0:T(8,128)S(1)} %get-tuple-element.22.cells, f32[8,16,72,128]{3,2,1,0:T(8,128)S(1)} %get-tuple-element.23.grads, f32[2,8,72,128]{3,2,1,0:T(8,128)S(1)} %get-tuple-element.24.sides, ...), custom_call_target="tpu_custom_call" | custom-call | flops 67108864 | bytes 4194304 | tf_op jit(solution)/shard_map/later/pallas_call | solution.py:451
  41.4 2.4 %collective-permute-start.8 = (s32[4,8,8,128]{3,2,1,0:T(8,128)S(1)}, s32[4,8,8,128]{3,2,1,0:T(8,128)S(1)}, u32[]{:S(2)}, u32[]{:S(2)}) collective-permute-start(s32[4,8,8,128]{3,2,1,0:T(8,128)S(1)} %later.3), channel_id=1, source_target_pairs={{0,1},{1,0},{2,3},{3,2},{4,5},{5,4},{6,7},{7,6},{8,9},{9,8},{10,11... | collective-permute-start | bytes 393224 | tf_op jit(solution)/shard_map/ppermute | solution.py:431
  43.9 2.3 %ours.1.ours_ref = f32[8,8,8,128]{3,2,1,0:T(8,128)S(1)} custom-call(f32[41,8,128]{2,1,0:T(8,128)S(1)} %get-tuple-element.14.consts, f32[8,16,72,128]{3,2,1,0:T(8,128)S(1)} %get-tuple-element.22.cells, f32[8,16,72,128]{3,2,1,0:T(8,128)S(1)} %get-tuple-element.23.grads, f32[2,8,72,128]{3,2,1,0:T(8,128)S(1)} %get-tuple-element.24.sides, ...), custom_call_target="tpu_custom_call" | custom-call | flops 67108864 | bytes 4194304 | tf_op jit(solution)/shard_map/ours/pallas_call | solution.py:461
  46.2 2.1 %collective-permute-done.8.mate1_ref = s32[4,8,8,128]{3,2,1,0:T(8,128)S(1)} collective-permute-done((s32[4,8,8,128]{3,2,1,0:T(8,128)S(1)}, s32[4,8,8,128]{3,2,1,0:T(8,128)S(1)}, u32[]{:S(2)}, u32[]{:S(2)}) %collective-permute-start.8) | collective-permute-done | bytes 131104 | tf_op jit(solution)/shard_map/ppermute | solution.py:431
  48.3 0.5 quad.1
  48.8 28.0 %all_to_all.5.pieces_ref = s32[4,64,128]{2,1,0:T(8,128)} all-to-all(s32[4,64,128]{2,1,0:T(8,128)S(1)} %bitcast.1), channel_id=1, replica_groups={{0,4,8,12},{1,5,9,13},{2,6,10,14},{3,7,11,15},{16,20,24,28},{17,21,25,2..., dimensions={0} | all-to-all | bytes 262144 | tf_op jit(solution)/shard_map/all_to_all | solution.py:479
  76.8 1.7 %compose.1 = (f32[3,4,1024]{2,1,0:T(4,128)}, f32[4,1024]{1,0:T(4,128)}) custom-call(f32[41,8,128]{2,1,0:T(8,128)} %copy-done.2, s32[4,64,128]{2,1,0:T(8,128)} %all_to_all.5.pieces_ref), custom_call_target="tpu_custom_call" | custom-call | tf_op jit(solution)/shard_map/compose/pallas_call | solution.py:488
  (15 shorter events, 0.0 us)
Async XLA Ops:
  0.6 1.6 %copy-start = (bf16[16,64,1024]{2,1,0:T(8,128)(2,1)S(1)}, bf16[16,64,1024]{2,1,0:T(8,128)(2,1)}, u32[]{:S(2)}) copy-start(bf16[16,64,1024]{2,1,0:T(8,128)(2,1)} %z_high.1) | copy-start | bytes 6291460
  2.2 17.0 %copy-start.1 = (bf16[16,64,1024]{2,1,0:T(8,128)(2,1)S(1)}, bf16[16,64,1024]{2,1,0:T(8,128)(2,1)}, u32[]{:S(2)}) copy-start(bf16[16,64,1024]{2,1,0:T(8,128)(2,1)} %z_high.1) | copy-start | bytes 6291460
  2.2 17.1 %copy-start.3 = (f32[3,8]{1,0:T(4,128)S(1)}, f32[3,8]{1,0:T(4,128)}, u32[]{:S(2)}) copy-start(f32[3,8]{1,0:T(4,128)} %colour_ref.1) | copy-start | bytes 292
  2.2 17.1 %copy-start.4 = (s32[8]{0:T(128)S(1)}, s32[8]{0:T(128)}, u32[]{:S(2)}) copy-start(s32[8]{0:T(128)} %knots_ref.1) | copy-start | bytes 100
  2.2 17.1 %copy-start.5 = (f32[8]{0:T(128)S(1)}, f32[8]{0:T(128)}, u32[]{:S(2)}) copy-start(f32[8]{0:T(128)} %density_ref.1) | copy-start | bytes 100
  2.6 19.9 %collective-permute-start.4 = (bf16[64,1024]{1,0:T(8,128)(2,1)S(1)}, bf16[64,1024]{1,0:T(8,128)(2,1)S(1)}, u32[]{:S(2)}, u32[]{:S(2)}) collective-permute-start(bf16[64,1024]{1,0:T(8,128)(2,1)S(1)} %get-tuple-element.20), channel_id=1, source_target_pairs={{0,1},{1,2},{2,3},{3,4},{4,5},{5,6},{6,7},{7,8},{8,9},{9,10},{10,1... | collective-permute-start | bytes 393224 | tf_op jit(solution)/shard_map/ppermute | solution.py:368
  6.5 15.9 %collective-permute-start.5 = (bf16[64,1024]{1,0:T(8,128)(2,1)S(1)}, bf16[64,1024]{1,0:T(8,128)(2,1)S(1)}, u32[]{:S(2)}, u32[]{:S(2)}) collective-permute-start(bf16[64,1024]{1,0:T(8,128)(2,1)S(1)} %get-tuple-element.21), channel_id=1, source_target_pairs={{1,0},{2,1},{3,2},{4,3},{5,4},{6,5},{7,6},{8,7},{9,8},{10,9},{11,1... | collective-permute-start | bytes 393224 | tf_op jit(solution)/shard_map/ppermute | solution.py:368
  7.8 8.0 %collective-permute-start = (bf16[16,1024]{1,0:T(8,128)(2,1)S(1)}, bf16[16,1024]{1,0:T(8,128)(2,1)S(1)}, u32[]{:S(2)}, u32[]{:S(2)}) collective-permute-start(bf16[16,1024]{1,0:T(8,128)(2,1)S(1)} %get-tuple-element.17), channel_id=1, source_target_pairs={{0,64},{64,128},{128,192},{192,256},{256,320},{320,384},{384,448},... | collective-permute-start | bytes 98312 | tf_op jit(solution)/shard_map/ppermute | solution.py:368
  9.7 12.7 %collective-permute-start.1 = (bf16[16,1024]{1,0:T(8,128)(2,1)S(1)}, bf16[16,1024]{1,0:T(8,128)(2,1)S(1)}, u32[]{:S(2)}, u32[]{:S(2)}) collective-permute-start(bf16[16,1024]{1,0:T(8,128)(2,1)S(1)} %get-tuple-element.18), channel_id=1, source_target_pairs={{64,0},{128,64},{192,128},{256,192},{320,256},{384,320},{448,384},... | collective-permute-start | bytes 98312 | tf_op jit(solution)/shard_map/ppermute | solution.py:368
  13.4 9.0 %collective-permute-start.3 = (f32[64,128]{1,0:T(8,128)S(1)}, f32[64,128]{1,0:T(8,128)S(1)}, u32[]{:S(2)}, u32[]{:S(2)}) collective-permute-start(f32[64,128]{1,0:T(8,128)S(1)} %get-tuple-element.19), channel_id=1, source_target_pairs={{16,0},{32,16},{48,32},{17,1},{33,17},{49,33},{18,2},{34,18},{50,3... | collective-permute-start | bytes 98312 | tf_op jit(solution)/shard_map/ppermute | solution.py:368
  15.9 6.6 %collective-permute-start.2 = (f32[64,128]{1,0:T(8,128)S(1)}, f32[64,128]{1,0:T(8,128)S(1)}, u32[]{:S(2)}, u32[]{:S(2)}) collective-permute-start(f32[64,128]{1,0:T(8,128)S(1)} %get-tuple-element.19), channel_id=1, source_target_pairs={{0,16},{16,32},{32,48},{1,17},{17,33},{33,49},{2,18},{18,34},{34,5... | collective-permute-start | bytes 98312 | tf_op jit(solution)/shard_map/ppermute | solution.py:368
  22.4 21.5 %copy-start.2 = (f32[41,8,128]{2,1,0:T(8,128)}, f32[41,8,128]{2,1,0:T(8,128)S(1)}, u32[]{:S(2)}) copy-start(f32[41,8,128]{2,1,0:T(8,128)S(1)} %get-tuple-element.14.consts) | copy-start | bytes 503812
  26.0 12.9 %collective-permute-start.7 = (s32[4,8,8,128]{3,2,1,0:T(8,128)S(1)}, s32[4,8,8,128]{3,2,1,0:T(8,128)S(1)}, u32[]{:S(2)}, u32[]{:S(2)}) collective-permute-start(s32[4,8,8,128]{3,2,1,0:T(8,128)S(1)} %get-tuple-element.25._), channel_id=1, source_target_pairs={{0,2},{1,3},{2,0},{3,1},{4,6},{5,7},{6,4},{7,5},{8,10},{9,11},{10,... | collective-permute-start | bytes 393224 | tf_op jit(solution)/shard_map/ppermute | solution.py:431
  34.5 9.4 %collective-permute-start.6 = (s32[4,8,8,128]{3,2,1,0:T(8,128)S(1)}, s32[4,8,8,128]{3,2,1,0:T(8,128)S(1)}, u32[]{:S(2)}, u32[]{:S(2)}) collective-permute-start(s32[4,8,8,128]{3,2,1,0:T(8,128)S(1)} %later.2), channel_id=1, source_target_pairs={{0,3},{1,2},{2,1},{3,0},{4,7},{5,6},{6,5},{7,4},{8,11},{9,10},{10,... | collective-permute-start | bytes 393224 | tf_op jit(solution)/shard_map/ppermute | solution.py:431
  41.4 6.9 %collective-permute-start.8 = (s32[4,8,8,128]{3,2,1,0:T(8,128)S(1)}, s32[4,8,8,128]{3,2,1,0:T(8,128)S(1)}, u32[]{:S(2)}, u32[]{:S(2)}) collective-permute-start(s32[4,8,8,128]{3,2,1,0:T(8,128)S(1)} %later.3), channel_id=1, source_target_pairs={{0,1},{1,0},{2,3},{3,2},{4,5},{5,4},{6,7},{7,6},{8,9},{9,8},{10,11... | collective-permute-start | bytes 393224 | tf_op jit(solution)/shard_map/ppermute | solution.py:431

commit v4 on v3

--- a/solution.py
+++ b/solution.py
@@ -292,7 +292,12 @@
     quarter_loop(consts, cells, grads, sides, place_in_quad(), depth_total, store)
 
 
-def quad_kernel(ours_ref, mate1_ref, mate2_ref, mate3_ref, out_ref):
+def quad_index():
+    return lax.axis_index("gz") // QUAD
+
+
+def quad_kernel(ours_ref, mate1_ref, mate2_ref, mate3_ref, *refs):
+    outs, out_ref = refs[:QUAD], refs[QUAD]
     tiles = ours_ref.shape[1]
     mates = (ours_ref, mate1_ref, mate2_ref, mate3_ref)
 
@@ -326,9 +331,17 @@
 
             lax.fori_loop(0, tiles, step, 0)
 
-
-def compose_kernel(consts, pieces_ref, image_ref, coverage_ref):
-    count = pieces_ref.shape[0]
+    rows = tiles * SUB
+    for k, ref in enumerate(outs):
+        start = pl.multiple_of((quad_index() ^ k) * rows, SUB)
+        ref[...] = out_ref[pl.ds(start, rows), :]
+
+
+def compose_kernel(consts, *refs):
+    swapped, (image_ref, coverage_ref, pieces_ref) = refs[:QUAD], refs[QUAD:]
+    count = QUAD
+    for k, ref in enumerate(swapped):
+        pieces_ref[quad_index() ^ k] = ref[...]
     low_rows = lax.broadcasted_iota(jnp.int32, (SUB, LANES), 0) < 4
     scales = [consts[SCALES + c] for c in range(3)]
     step = COLOUR_SPAN / CODES
@@ -467,23 +480,19 @@
         cost_estimate=work,
         name="ours",
     )(consts, cells, grads, sides, arrived[3])
-    quads = count // QUAD
-    codes = pl.pallas_call(
+    piece = jax.ShapeDtypeStruct((tiles * SUB, LANES), jnp.int32)
+    pieces = pl.pallas_call(
         quad_kernel,
-        out_shape=jax.ShapeDtypeStruct((quads * tiles * SUB, LANES), jnp.int32),
-        in_specs=[vmem] * 4,
-        out_specs=vmem,
+        out_shape=(piece,) * QUAD,
+        in_specs=[vmem] * QUAD,
+        out_specs=(vmem,) * QUAD,
+        scratch_shapes=[pltpu.VMEM((QUAD * tiles * SUB, LANES), jnp.int32)],
         compiler_params=params,
         name="quad",
     )(ours, arrived[1], arrived[2], arrived[3])
-    pieces = lax.all_to_all(
-        codes.reshape(quads, tiles * SUB, LANES),
-        "gz",
-        split_axis=0,
-        concat_axis=0,
-        tiled=True,
-        axis_index_groups=[[QUAD * i + e for i in range(quads)] for e in range(QUAD)],
-    )
+    swapped = {0: pieces[0]}
+    for k in (2, 1, 3):
+        swapped[k] = lax.ppermute(pieces[k], "gz", [(i, i ^ (QUAD * k)) for i in range(count)])
     band = rows // count
     return pl.pallas_call(
         compose_kernel,
@@ -491,10 +500,11 @@
             jax.ShapeDtypeStruct((3, band, cols), f32),
             jax.ShapeDtypeStruct((band, cols), f32),
         ),
-        in_specs=[vmem, vmem],
+        in_specs=[vmem] * (1 + QUAD),
         out_specs=(vmem, vmem),
+        scratch_shapes=[pltpu.VMEM((QUAD, tiles * SUB, LANES), jnp.int32)],
         name="compose",
-    )(consts, pieces)
+    )(consts, *[swapped[k] for k in range(QUAD)])
 
 
 def solution(mesh):

time: 79.1 us -> 81.6 us (1.032)
  the two profiles are of different devices: /device:TPU:10 before, /device:TPU:30 now
where the time goes in v4:
time: 81.6 us; the launch traced here: 81.1 us
  starting transfers between devices  49.7 us (61%)
  Pallas kernels  16.5 us (20%)
  waiting for transfers between devices  11.2 us (14%)
  local copies, waits for them, and re-layouts  2.82 us (3%)
  between operations  0.89 us (1%)
    ppermute x3, starting transfers between devices, on_device(): lax.ppermute(pieces[k], 'gz', [(i, i ^ QUAD * k) for i in range(count)])  22.1 us
    ppermute x6, starting transfers between devices, neighbours(): return (lax.ppermute(last, axis, up), lax.ppermute(initial, axis, down))  14.8 us
    ppermute x3, starting transfers between devices, send(): lax.ppermute(words, 'gz', [(i, i ^ mate) for i in range(count)])  12.7 us
    ppermute x3, waiting for transfers between devices, on_device(): lax.ppermute(pieces[k], 'gz', [(i, i ^ QUAD * k) for i in range(count)])  7.77 us
    pallas_call x2, Pallas kernels, on_device(): pl.pallas_call(functools.partial(later_kernel, mate=mate, depth_total=dep...  5.09 us
    pallas_call x1, Pallas kernels, on_device(): pl.pallas_call(functools.partial(first_kernel, mate=2, depth_total=depth_...  3.55 us
    pallas_call x1, Pallas kernels, on_device(): pl.pallas_call(functools.partial(spread_kernel, depth_total=depth_total),...  3.07 us
    unnamed x20, local copies, waits for them, and re-layouts  2.82 us
  transfers between devices with their start and end apart: 12, of which 4 were waited for; matrix products, arithmetic and copies ran while one was open for 0% of the time, Pallas kernels for 13%

profile of v4, /device:TPU:30, one launch (start us, length us, event | category | flops | bytes accessed | tf_op | source)
XLA Modules:
  0.0 81.1 jit_solution(2911295523317113756)
XLA Ops:
  0.6 1.6 %copy-done = bf16[16,64,1024]{2,1,0:T(8,128)(2,1)S(1)} copy-done((bf16[16,64,1024]{2,1,0:T(8,128)(2,1)S(1)}, bf16[16,64,1024]{2,1,0:T(8,128)(2,1)}, u32[]{:S(2)}) %copy-start) | copy-done | bytes 2097176
  2.6 4.0 %collective-permute-start.4 = (bf16[64,1024]{1,0:T(8,128)(2,1)S(1)}, bf16[64,1024]{1,0:T(8,128)(2,1)S(1)}, u32[]{:S(2)}, u32[]{:S(2)}) collective-permute-start(bf16[64,1024]{1,0:T(8,128)(2,1)S(1)} %get-tuple-element.24), channel_id=1, source_target_pairs={{0,1},{1,2},{2,3},{3,4},{4,5},{5,6},{6,7},{7,8},{8,9},{9,10},{10,1... | collective-permute-start | bytes 393224 | tf_op jit(solution)/shard_map/ppermute | solution.py:381
  6.5 1.3 %collective-permute-start.5 = (bf16[64,1024]{1,0:T(8,128)(2,1)S(1)}, bf16[64,1024]{1,0:T(8,128)(2,1)S(1)}, u32[]{:S(2)}, u32[]{:S(2)}) collective-permute-start(bf16[64,1024]{1,0:T(8,128)(2,1)S(1)} %get-tuple-element.25), channel_id=1, source_target_pairs={{1,0},{2,1},{3,2},{4,3},{5,4},{6,5},{7,6},{8,7},{9,8},{10,9},{11,1... | collective-permute-start | bytes 393224 | tf_op jit(solution)/shard_map/ppermute | solution.py:381
  7.8 1.9 %collective-permute-start = (bf16[16,1024]{1,0:T(8,128)(2,1)S(1)}, bf16[16,1024]{1,0:T(8,128)(2,1)S(1)}, u32[]{:S(2)}, u32[]{:S(2)}) collective-permute-start(bf16[16,1024]{1,0:T(8,128)(2,1)S(1)} %get-tuple-element.21), channel_id=1, source_target_pairs={{0,64},{64,128},{128,192},{192,256},{256,320},{320,384},{384,448},... | collective-permute-start | bytes 98312 | tf_op jit(solution)/shard_map/ppermute | solution.py:381
  9.7 3.6 %collective-permute-start.1 = (bf16[16,1024]{1,0:T(8,128)(2,1)S(1)}, bf16[16,1024]{1,0:T(8,128)(2,1)S(1)}, u32[]{:S(2)}, u32[]{:S(2)}) collective-permute-start(bf16[16,1024]{1,0:T(8,128)(2,1)S(1)} %get-tuple-element.22), channel_id=1, source_target_pairs={{64,0},{128,64},{192,128},{256,192},{320,256},{384,320},{448,384},... | collective-permute-start | bytes 98312 | tf_op jit(solution)/shard_map/ppermute | solution.py:381
  13.4 2.7 %collective-permute-start.3 = (f32[64,128]{1,0:T(8,128)S(1)}, f32[64,128]{1,0:T(8,128)S(1)}, u32[]{:S(2)}, u32[]{:S(2)}) collective-permute-start(f32[64,128]{1,0:T(8,128)S(1)} %get-tuple-element.23), channel_id=1, source_target_pairs={{16,0},{32,16},{48,32},{17,1},{33,17},{49,33},{18,2},{34,18},{50,3... | collective-permute-start | bytes 98312 | tf_op jit(solution)/shard_map/ppermute | solution.py:381
  16.1 1.3 %collective-permute-start.2 = (f32[64,128]{1,0:T(8,128)S(1)}, f32[64,128]{1,0:T(8,128)S(1)}, u32[]{:S(2)}, u32[]{:S(2)}) collective-permute-start(f32[64,128]{1,0:T(8,128)S(1)} %get-tuple-element.23), channel_id=1, source_target_pairs={{0,16},{16,32},{32,48},{1,17},{17,33},{33,49},{2,18},{18,34},{34,5... | collective-permute-start | bytes 98312 | tf_op jit(solution)/shard_map/ppermute | solution.py:381
  17.5 3.1 %spread.1 = (f32[8,16,72,128]{3,2,1,0:T(8,128)S(1)}, f32[8,16,72,128]{3,2,1,0:T(8,128)S(1)}, f32[41,8,128]{2,1,0:T(8,128)S(1)}) custom-call(s32[8]{0:T(128)S(1)} %copy-done.5, f32[3,8]{1,0:T(4,128)S(1)} %copy-done.4, f32[8]{0:T(128)S(1)} %copy-done.6, bf16[16,64,1024]{2,1,0:T(8,128)(2,1)S(1)} %copy-done.1), custom_call_target="tpu_custom_call" | custom-call | flops 8388608 | bytes 2097152 | tf_op jit(solution)/shard_map/spread/pallas_call | solution.py:430
  20.6 1.4 %collective-permute-done.2.by_ref = f32[64,128]{1,0:T(8,128)S(1)} collective-permute-done((f32[64,128]{1,0:T(8,128)S(1)}, f32[64,128]{1,0:T(8,128)S(1)}, u32[]{:S(2)}, u32[]{:S(2)}) %collective-permute-start.2) | collective-permute-done | bytes 32800 | tf_op jit(solution)/shard_map/ppermute | solution.py:381
  22.0 3.6 %first.1 = (s32[4,8,8,128]{3,2,1,0:T(8,128)S(1)}, f32[8,16,72,128]{3,2,1,0:T(8,128)S(1)}, f32[8,16,72,128]{3,2,1,0:T(8,128)S(1)}, f32[2,8,72,128]{3,2,1,0:T(8,128)S(1)}) custom-call(f32[41,8,128]{2,1,0:T(8,128)S(1)} %get-tuple-element.18.consts, f32[8,16,72,128]{3,2,1,0:T(8,128)S(1)} %get-tuple-element.19.cells_in, ...), custom_call_target="tpu_custom_call", output_to_operand_aliasing={{1}: (1, {}), {2}: (2, {})} | custom-call | flops 67108864 | bytes 4194304 | tf_op jit(solution)/shard_map/first/pallas_call | solution.py:446
  25.5 5.9 %collective-permute-start.7 = (s32[4,8,8,128]{3,2,1,0:T(8,128)S(1)}, s32[4,8,8,128]{3,2,1,0:T(8,128)S(1)}, u32[]{:S(2)}, u32[]{:S(2)}) collective-permute-start(s32[4,8,8,128]{3,2,1,0:T(8,128)S(1)} %get-tuple-element.29._), channel_id=1, source_target_pairs={{0,2},{1,3},{2,0},{3,1},{4,6},{5,7},{6,4},{7,5},{8,10},{9,11},{10,... | collective-permute-start | bytes 393224 | tf_op jit(solution)/shard_map/ppermute | solution.py:444
  31.4 2.5 %later.2 = s32[4,8,8,128]{3,2,1,0:T(8,128)S(1)} custom-call(f32[41,8,128]{2,1,0:T(8,128)S(1)} %get-tuple-element.18.consts, f32[8,16,72,128]{3,2,1,0:T(8,128)S(1)} %get-tuple-element.26.cells, f32[8,16,72,128]{3,2,1,0:T(8,128)S(1)} %get-tuple-element.27.grads, f32[2,8,72,128]{3,2,1,0:T(8,128)S(1)} %get-tuple-element.28.sides, ...), custom_call_target="tpu_custom_call" | custom-call | flops 67108864 | bytes 4194304 | tf_op jit(solution)/shard_map/later/pallas_call | solution.py:464
  34.0 4.4 %collective-permute-start.6 = (s32[4,8,8,128]{3,2,1,0:T(8,128)S(1)}, s32[4,8,8,128]{3,2,1,0:T(8,128)S(1)}, u32[]{:S(2)}, u32[]{:S(2)}) collective-permute-start(s32[4,8,8,128]{3,2,1,0:T(8,128)S(1)} %later.2), channel_id=1, source_target_pairs={{0,3},{1,2},{2,1},{3,0},{4,7},{5,6},{6,5},{7,4},{8,11},{9,10},{10,... | collective-permute-start | bytes 393224 | tf_op jit(solution)/shard_map/ppermute | solution.py:444
  38.4 2.5 %later.3 = s32[4,8,8,128]{3,2,1,0:T(8,128)S(1)} custom-call(f32[41,8,128]{2,1,0:T(8,128)S(1)} %get-tuple-element.18.consts, f32[8,16,72,128]{3,2,1,0:T(8,128)S(1)} %get-tuple-element.26.cells, f32[8,16,72,128]{3,2,1,0:T(8,128)S(1)} %get-tuple-element.27.grads, f32[2,8,72,128]{3,2,1,0:T(8,128)S(1)} %get-tuple-element.28.sides, ...), custom_call_target="tpu_custom_call" | custom-call | flops 67108864 | bytes 4194304 | tf_op jit(solution)/shard_map/later/pallas_call | solution.py:464
  40.9 2.4 %collective-permute-start.8 = (s32[4,8,8,128]{3,2,1,0:T(8,128)S(1)}, s32[4,8,8,128]{3,2,1,0:T(8,128)S(1)}, u32[]{:S(2)}, u32[]{:S(2)}) collective-permute-start(s32[4,8,8,128]{3,2,1,0:T(8,128)S(1)} %later.3), channel_id=1, source_target_pairs={{0,1},{1,0},{2,3},{3,2},{4,5},{5,4},{6,7},{7,6},{8,9},{9,8},{10,11... | collective-permute-start | bytes 393224 | tf_op jit(solution)/shard_map/ppermute | solution.py:444
  43.4 2.3 %ours.1.ours_ref = f32[8,8,8,128]{3,2,1,0:T(8,128)S(1)} custom-call(f32[41,8,128]{2,1,0:T(8,128)S(1)} %get-tuple-element.18.consts, f32[8,16,72,128]{3,2,1,0:T(8,128)S(1)} %get-tuple-element.26.cells, f32[8,16,72,128]{3,2,1,0:T(8,128)S(1)} %get-tuple-element.27.grads, f32[2,8,72,128]{3,2,1,0:T(8,128)S(1)} %get-tuple-element.28.sides, ...), custom_call_target="tpu_custom_call" | custom-call | flops 67108864 | bytes 4194304 | tf_op jit(solution)/shard_map/ours/pallas_call | solution.py:474
  45.7 2.1 %collective-permute-done.8.mate1_ref = s32[4,8,8,128]{3,2,1,0:T(8,128)S(1)} collective-permute-done((s32[4,8,8,128]{3,2,1,0:T(8,128)S(1)}, s32[4,8,8,128]{3,2,1,0:T(8,128)S(1)}, u32[]{:S(2)}, u32[]{:S(2)}) %collective-permute-start.8) | collective-permute-done | bytes 131104 | tf_op jit(solution)/shard_map/ppermute | solution.py:444
  48.3 0.6 copy-done.3
  48.9 9.1 %collective-permute-start.9 = (s32[64,128]{1,0:T(8,128)S(1)}, s32[64,128]{1,0:T(8,128)S(1)}, u32[]{:S(2)}, u32[]{:S(2)}) collective-permute-start(s32[64,128]{1,0:T(8,128)S(1)} %get-tuple-element.31), channel_id=1, source_target_pairs={{0,4},{1,5},{2,6},{3,7},{4,0},{5,1},{6,2},{7,3},{8,12},{9,13},{10,... | collective-permute-start | bytes 98312 | tf_op jit(solution)/shard_map/ppermute | solution.py:495
  58.0 11.1 %collective-permute-start.10 = (s32[64,128]{1,0:T(8,128)S(1)}, s32[64,128]{1,0:T(8,128)S(1)}, u32[]{:S(2)}, u32[]{:S(2)}) collective-permute-start(s32[64,128]{1,0:T(8,128)S(1)} %get-tuple-element.32), channel_id=1, source_target_pairs={{0,8},{1,9},{2,10},{3,11},{4,12},{5,13},{6,14},{7,15},{8,0},{9,1},... | collective-permute-start | bytes 98312 | tf_op jit(solution)/shard_map/ppermute | solution.py:495
  69.1 1.9 %collective-permute-start.11 = (s32[64,128]{1,0:T(8,128)S(1)}, s32[64,128]{1,0:T(8,128)S(1)}, u32[]{:S(2)}, u32[]{:S(2)}) collective-permute-start(s32[64,128]{1,0:T(8,128)S(1)} %get-tuple-element.33), channel_id=1, source_target_pairs={{0,12},{1,13},{2,14},{3,15},{4,8},{5,9},{6,10},{7,11},{8,4},{9,5},... | collective-permute-start | bytes 98312 | tf_op jit(solution)/shard_map/ppermute | solution.py:495
  71.1 1.9 %collective-permute-done.10.refs_2_ = s32[64,128]{1,0:T(8,128)S(1)} collective-permute-done((s32[64,128]{1,0:T(8,128)S(1)}, s32[64,128]{1,0:T(8,128)S(1)}, u32[]{:S(2)}, u32[]{:S(2)}) %collective-permute-start.10) | collective-permute-done | bytes 32800 | tf_op jit(solution)/shard_map/ppermute | solution.py:495
  73.0 5.9 %collective-permute-done.11.refs_3_ = s32[64,128]{1,0:T(8,128)S(1)} collective-permute-done((s32[64,128]{1,0:T(8,128)S(1)}, s32[64,128]{1,0:T(8,128)S(1)}, u32[]{:S(2)}, u32[]{:S(2)}) %collective-permute-start.11) | collective-permute-done | bytes 32800 | tf_op jit(solution)/shard_map/ppermute | solution.py:495
  79.5 1.7 %compose.1 = (f32[3,4,1024]{2,1,0:T(4,128)}, f32[4,1024]{1,0:T(4,128)}) custom-call(f32[41,8,128]{2,1,0:T(8,128)} %copy-done.2, s32[64,128]{1,0:T(8,128)} %copy-done.3, s32[64,128]{1,0:T(8,128)} %copy-done.7, s32[64,128]{1,0:T(8,128)} %copy-done.8, s32[64,128]{1,0:T(8,128)} %copy-done.9), custom_call_target="tpu_custom_call" | custom-call | tf_op jit(solution)/shard_map/compose/pallas_call | solution.py:497
  (28 shorter events, 1.5 us)
Async XLA Ops:
  0.6 1.6 %copy-start = (bf16[16,64,1024]{2,1,0:T(8,128)(2,1)S(1)}, bf16[16,64,1024]{2,1,0:T(8,128)(2,1)}, u32[]{:S(2)}) copy-start(bf16[16,64,1024]{2,1,0:T(8,128)(2,1)} %z_high.1) | copy-start | bytes 6291460
  2.2 15.2 %copy-start.1 = (bf16[16,64,1024]{2,1,0:T(8,128)(2,1)S(1)}, bf16[16,64,1024]{2,1,0:T(8,128)(2,1)}, u32[]{:S(2)}) copy-start(bf16[16,64,1024]{2,1,0:T(8,128)(2,1)} %z_high.1) | copy-start | bytes 6291460
  2.2 15.2 %copy-start.4 = (f32[3,8]{1,0:T(4,128)S(1)}, f32[3,8]{1,0:T(4,128)}, u32[]{:S(2)}) copy-start(f32[3,8]{1,0:T(4,128)} %colour_ref.1) | copy-start | bytes 292
  2.2 15.2 %copy-start.5 = (s32[8]{0:T(128)S(1)}, s32[8]{0:T(128)}, u32[]{:S(2)}) copy-start(s32[8]{0:T(128)} %knots_ref.1) | copy-start | bytes 100
  2.2 15.3 %copy-start.6 = (f32[8]{0:T(128)S(1)}, f32[8]{0:T(128)}, u32[]{:S(2)}) copy-start(f32[8]{0:T(128)} %density_ref.1) | copy-start | bytes 100
  2.6 19.4 %collective-permute-start.4 = (bf16[64,1024]{1,0:T(8,128)(2,1)S(1)}, bf16[64,1024]{1,0:T(8,128)(2,1)S(1)}, u32[]{:S(2)}, u32[]{:S(2)}) collective-permute-start(bf16[64,1024]{1,0:T(8,128)(2,1)S(1)} %get-tuple-element.24), channel_id=1, source_target_pairs={{0,1},{1,2},{2,3},{3,4},{4,5},{5,6},{6,7},{7,8},{8,9},{9,10},{10,1... | collective-permute-start | bytes 393224 | tf_op jit(solution)/shard_map/ppermute | solution.py:381
  6.5 15.4 %collective-permute-start.5 = (bf16[64,1024]{1,0:T(8,128)(2,1)S(1)}, bf16[64,1024]{1,0:T(8,128)(2,1)S(1)}, u32[]{:S(2)}, u32[]{:S(2)}) collective-permute-start(bf16[64,1024]{1,0:T(8,128)(2,1)S(1)} %get-tuple-element.25), channel_id=1, source_target_pairs={{1,0},{2,1},{3,2},{4,3},{5,4},{6,5},{7,6},{8,7},{9,8},{10,9},{11,1... | collective-permute-start | bytes 393224 | tf_op jit(solution)/shard_map/ppermute | solution.py:381
  7.8 8.3 %collective-permute-start = (bf16[16,1024]{1,0:T(8,128)(2,1)S(1)}, bf16[16,1024]{1,0:T(8,128)(2,1)S(1)}, u32[]{:S(2)}, u32[]{:S(2)}) collective-permute-start(bf16[16,1024]{1,0:T(8,128)(2,1)S(1)} %get-tuple-element.21), channel_id=1, source_target_pairs={{0,64},{64,128},{128,192},{192,256},{256,320},{320,384},{384,448},... | collective-permute-start | bytes 98312 | tf_op jit(solution)/shard_map/ppermute | solution.py:381
  9.7 10.8 %collective-permute-start.1 = (bf16[16,1024]{1,0:T(8,128)(2,1)S(1)}, bf16[16,1024]{1,0:T(8,128)(2,1)S(1)}, u32[]{:S(2)}, u32[]{:S(2)}) collective-permute-start(bf16[16,1024]{1,0:T(8,128)(2,1)S(1)} %get-tuple-element.22), channel_id=1, source_target_pairs={{64,0},{128,64},{192,128},{256,192},{320,256},{384,320},{448,384},... | collective-permute-start | bytes 98312 | tf_op jit(solution)/shard_map/ppermute | solution.py:381
  13.4 7.2 %collective-permute-start.3 = (f32[64,128]{1,0:T(8,128)S(1)}, f32[64,128]{1,0:T(8,128)S(1)}, u32[]{:S(2)}, u32[]{:S(2)}) collective-permute-start(f32[64,128]{1,0:T(8,128)S(1)} %get-tuple-element.23), channel_id=1, source_target_pairs={{16,0},{32,16},{48,32},{17,1},{33,17},{49,33},{18,2},{34,18},{50,3... | collective-permute-start | bytes 98312 | tf_op jit(solution)/shard_map/ppermute | solution.py:381
  16.1 5.8 %collective-permute-start.2 = (f32[64,128]{1,0:T(8,128)S(1)}, f32[64,128]{1,0:T(8,128)S(1)}, u32[]{:S(2)}, u32[]{:S(2)}) collective-permute-start(f32[64,128]{1,0:T(8,128)S(1)} %get-tuple-element.23), channel_id=1, source_target_pairs={{0,16},{16,32},{32,48},{1,17},{17,33},{33,49},{2,18},{18,34},{34,5... | collective-permute-start | bytes 98312 | tf_op jit(solution)/shard_map/ppermute | solution.py:381
  20.6 22.8 %copy-start.2 = (f32[41,8,128]{2,1,0:T(8,128)}, f32[41,8,128]{2,1,0:T(8,128)S(1)}, u32[]{:S(2)}) copy-start(f32[41,8,128]{2,1,0:T(8,128)S(1)} %get-tuple-element.18.consts) | copy-start | bytes 503812
  25.5 12.9 %collective-permute-start.7 = (s32[4,8,8,128]{3,2,1,0:T(8,128)S(1)}, s32[4,8,8,128]{3,2,1,0:T(8,128)S(1)}, u32[]{:S(2)}, u32[]{:S(2)}) collective-permute-start(s32[4,8,8,128]{3,2,1,0:T(8,128)S(1)} %get-tuple-element.29._), channel_id=1, source_target_pairs={{0,2},{1,3},{2,0},{3,1},{4,6},{5,7},{6,4},{7,5},{8,10},{9,11},{10,... | collective-permute-start | bytes 393224 | tf_op jit(solution)/shard_map/ppermute | solution.py:444
  34.0 9.4 %collective-permute-start.6 = (s32[4,8,8,128]{3,2,1,0:T(8,128)S(1)}, s32[4,8,8,128]{3,2,1,0:T(8,128)S(1)}, u32[]{:S(2)}, u32[]{:S(2)}) collective-permute-start(s32[4,8,8,128]{3,2,1,0:T(8,128)S(1)} %later.2), channel_id=1, source_target_pairs={{0,3},{1,2},{2,1},{3,0},{4,7},{5,6},{6,5},{7,4},{8,11},{9,10},{10,... | collective-permute-start | bytes 393224 | tf_op jit(solution)/shard_map/ppermute | solution.py:444
  40.9 6.9 %collective-permute-start.8 = (s32[4,8,8,128]{3,2,1,0:T(8,128)S(1)}, s32[4,8,8,128]{3,2,1,0:T(8,128)S(1)}, u32[]{:S(2)}, u32[]{:S(2)}) collective-permute-start(s32[4,8,8,128]{3,2,1,0:T(8,128)S(1)} %later.3), channel_id=1, source_target_pairs={{0,1},{1,0},{2,3},{3,2},{4,5},{5,4},{6,7},{7,6},{8,9},{9,8},{10,11... | collective-permute-start | bytes 393224 | tf_op jit(solution)/shard_map/ppermute | solution.py:444
  48.3 0.6 copy-start.3
  48.9 22.1 %collective-permute-start.9 = (s32[64,128]{1,0:T(8,128)S(1)}, s32[64,128]{1,0:T(8,128)S(1)}, u32[]{:S(2)}, u32[]{:S(2)}) collective-permute-start(s32[64,128]{1,0:T(8,128)S(1)} %get-tuple-element.31), channel_id=1, source_target_pairs={{0,4},{1,5},{2,6},{3,7},{4,0},{5,1},{6,2},{7,3},{8,12},{9,13},{10,... | collective-permute-start | bytes 98312 | tf_op jit(solution)/shard_map/ppermute | solution.py:495
  58.0 15.0 %collective-permute-start.10 = (s32[64,128]{1,0:T(8,128)S(1)}, s32[64,128]{1,0:T(8,128)S(1)}, u32[]{:S(2)}, u32[]{:S(2)}) collective-permute-start(s32[64,128]{1,0:T(8,128)S(1)} %get-tuple-element.32), channel_id=1, source_target_pairs={{0,8},{1,9},{2,10},{3,11},{4,12},{5,13},{6,14},{7,15},{8,0},{9,1},... | collective-permute-start | bytes 98312 | tf_op jit(solution)/shard_map/ppermute | solution.py:495
  69.1 9.7 %collective-permute-start.11 = (s32[64,128]{1,0:T(8,128)S(1)}, s32[64,128]{1,0:T(8,128)S(1)}, u32[]{:S(2)}, u32[]{:S(2)}) collective-permute-start(s32[64,128]{1,0:T(8,128)S(1)} %get-tuple-element.33), channel_id=1, source_target_pairs={{0,12},{1,13},{2,14},{3,15},{4,8},{5,9},{6,10},{7,11},{8,4},{9,5},... | collective-permute-start | bytes 98312 | tf_op jit(solution)/shard_map/ppermute | solution.py:495
  71.1 7.8 %copy-start.7 = (s32[64,128]{1,0:T(8,128)}, s32[64,128]{1,0:T(8,128)S(1)}, u32[]{:S(2)}) copy-start(s32[64,128]{1,0:T(8,128)S(1)} %collective-permute-done.9.refs_1_) | copy-start | bytes 98308
  73.0 5.9 %copy-start.8 = (s32[64,128]{1,0:T(8,128)}, s32[64,128]{1,0:T(8,128)S(1)}, u32[]{:S(2)}) copy-start(s32[64,128]{1,0:T(8,128)S(1)} %collective-permute-done.10.refs_2_) | copy-start | bytes 98308
  78.8 0.6 copy-start.9

commit v5 on v2

--- a/solution.py
+++ b/solution.py
@@ -17,6 +17,9 @@
 SUB = 8
 GROUPS = 8
 PITCH = 9
+ABOVE = PITCH * (GROUPS - 1) - 1
+BELOW = GROUPS
+SCALES = 38
 
 COLOUR_SPAN = 26.0
 COVER_SPAN = 9.0
@@ -37,9 +40,12 @@
 
 def opacity_terms(largest):
     half = 0.5 * largest
-    nodes = [half + half * math.cos(math.pi * (2 * i + 1) / 8.0) for i in range(4)]
+    nodes = [half + half * math.cos(math.pi * (2 * i + 1) / 6.0) for i in range(3)]
     values = [-math.expm1(-y) / y for y in nodes]
-    return [float(c) for c in np.polynomial.polynomial.polyfit(nodes, values, 3)]
+    c0, c1, c2 = (float(c) for c in np.polynomial.polynomial.polyfit(nodes, values, 2))
+    k = c2 ** (1.0 / 3.0)
+    a = c1 / (2.0 * k * k)
+    return k, a, c0 / k - a * a
 
 
 def full(x):
@@ -65,7 +71,7 @@
     top[...] = rows_x[0].astype(top.dtype)
     bottom[...] = rows_x[1].astype(bottom.dtype)
     lane = lane_index()
-    for i in range(GROUPS // 2):
+    for i in range(y_low.shape[1] // 16):
         sides = [jnp.zeros((SUB, LANES), jnp.float32)] * 2
         for z in range(depth):
             low = y_low[z, 16 * i:16 * i + 16, :].astype(jnp.float32)
@@ -80,10 +86,15 @@
     rear[...] = z_high[0]
 
 
-def spread_kernel(vol_ref, cells, grads):
+def slots_of(i):
+    return pl.ds(i, SUB, stride=PITCH)
+
+
+def spread_kernel(knots_ref, colour_ref, density_ref, vol_ref, cells, grads, consts, *, depth_total):
     depth, rows, cols = vol_ref.shape
     lane = lax.broadcasted_iota(jnp.int32, (16, LANES), 1)
     tiles = cols // LANES
+    prepare(consts, knots_ref, colour_ref, density_ref, depth_total)
 
     def step(z, carry):
         for c in range(rows // 16):
@@ -99,10 +110,9 @@
                 across = r - l
                 own = plane[:, lanes_of(t)]
                 for part in range(2):
-                    i = 2 * c + part
                     at = slice(8 * part, 8 * part + 8)
-                    cells[t, z, pl.ds(i, SUB, stride=PITCH), :] = own[at]
-                    grads[t, z, pl.ds(i, SUB, stride=PITCH), :] = across[at]
+                    cells[t, z, slots_of(2 * c + part), :] = own[at]
+                    grads[t, z, slots_of(2 * c + part), :] = across[at]
         return carry
 
     lax.fori_loop(0, depth, step, 0)
@@ -117,12 +127,14 @@
         spans.append((high - low) * (1.0 / top))
         if k:
             consts[k - 1] = low / top
-    consts[6] = full(density_ref[0]) * (1.0 / depth_total)
+    unit = opacity_terms(10.0 / depth_total)[0] / depth_total
+    consts[6] = full(density_ref[0]) * unit
     for k in range(SEGMENTS):
         step = full(density_ref[k + 1]) - full(density_ref[k])
-        consts[7 + k] = step * (1.0 / depth_total) / spans[k]
+        consts[7 + k] = step * unit / spans[k]
     for c in range(3):
         scale = full(colour_scale(colour_ref, c))
+        consts[SCALES + c] = scale
         consts[14 + 8 * c] = full(colour_ref[c, 0]) / scale
         for k in range(SEGMENTS):
             step = full(colour_ref[c, k + 1]) - full(colour_ref[c, k])
@@ -130,7 +142,7 @@
 
 
 def composite(consts, cell, grad_x, grad_y, depth, depth_total):
-    c0, c1, c2, c3 = opacity_terms(10.0 / depth_total)
+    _, shift, rest = opacity_terms(10.0 / depth_total)
     points = [consts[k] for k in range(6)]
     first = consts[6]
     slopes = [consts[7 + k] for k in range(SEGMENTS)]
@@ -151,7 +163,8 @@
         y = first
         for k in range(SEGMENTS):
             y = y + ramps[k] * slopes[k]
-        taken = transmit * (y * (c0 + y * (c1 + y * (c2 + y * c3))))
+        shifted = y + shift
+        taken = transmit * (y * (shifted * shifted + rest))
         transmit = transmit - taken
         shaded = taken * shading
         if z == 0:
@@ -175,20 +188,20 @@
         plane = ref[16 * c:16 * c + 16, :].astype(jnp.float32)
         for t in range(sides.shape[1]):
             for part in range(2):
-                own = plane[8 * part:8 * part + 8, lanes_of(t)]
-                sides[side, t, pl.ds(2 * c + part, SUB, stride=PITCH), :] = own
-
-
-def place_edges(cells, grads, bx_ref, ax_ref, by_ref, ay_ref):
+                sides[side, t, slots_of(2 * c + part), :] = plane[8 * part:8 * part + 8, lanes_of(t)]
+
+
+def place_edges(cells, grads, bx_ref, ax_ref, by_ref, ay_ref, parity):
     tiles, depth = cells.shape[:2]
-    for slot, ref in ((PITCH * (GROUPS - 1) - 1, bx_ref), (GROUPS, ax_ref)):
-        edge = ref[...].astype(jnp.float32)
-        for z in range(depth):
-            for t in range(tiles):
-                cells[t, z, slot:slot + 1, :] = edge[z:z + 1, lanes_of(t)]
+    slot = jnp.where(parity == 0, ABOVE, BELOW)
+    edge = jnp.where(parity == 0, bx_ref[...].astype(jnp.float32), ax_ref[...].astype(jnp.float32))
+    for z in range(depth):
+        for t in range(tiles):
+            cells[t, z, pl.ds(slot, 1), :] = edge[z:z + 1, lanes_of(t)]
     lane = lane_index()
 
-    def step(r, carry):
+    def step(j, carry):
+        r = 4 * parity + j
         rows = pl.ds(pl.multiple_of(SUB * r, SUB), SUB)
         at = pl.ds(PITCH * r, SUB)
         before, after = by_ref[rows, :], ay_ref[rows, :]
@@ -199,40 +212,42 @@
             grads[tiles - 1, z, at, :] = grads[tiles - 1, z, at, :] + last
         return carry
 
-    lax.fori_loop(0, GROUPS, step, 0)
+    lax.fori_loop(0, 4, step, 0)
 
 
 def half_loop(consts, cells, grads, sides, parity, depth_total, store):
     tiles, depth = cells.shape[:2]
 
-    def tile_step(t, carry):
-        def row_step(j, carry):
-            r = 4 * parity + j
-            at = pl.ds(PITCH * r, SUB)
-            above = pl.ds(jnp.where(r == 0, PITCH * (GROUPS - 1) - 1, PITCH * r - PITCH), SUB)
-            below = pl.ds(jnp.where(r == GROUPS - 1, 1, PITCH * r + PITCH), SUB)
-
-            def cell(z):
-                if z < 0:
-                    return sides[0, t, at, :]
-                if z == depth:
-                    return sides[1, t, at, :]
-                return cells[t, z, at, :]
-
-            values = composite(
-                consts,
-                cell,
-                lambda z: cells[t, z, below, :] - cells[t, z, above, :],
-                lambda z: grads[t, z, at, :],
-                depth,
-                depth_total,
-            )
-            store(t, j, values)
-            return carry
-
-        return lax.fori_loop(0, 4, row_step, carry, unroll=2)
-
-    lax.fori_loop(0, tiles, tile_step, 0)
+    def work(t, j):
+        r = 4 * parity + j
+        at = pl.ds(PITCH * r, SUB)
+        above = pl.ds(jnp.where(r == 0, ABOVE, PITCH * r - PITCH), SUB)
+        below = pl.ds(jnp.where(r == GROUPS - 1, 1, PITCH * r + PITCH), SUB)
+
+        def cell(z):
+            if z < 0:
+                return sides[0, t, at, :]
+            if z == depth:
+                return sides[1, t, at, :]
+            return cells[t, z, at, :]
+
+        values = composite(
+            consts,
+            cell,
+            lambda z: cells[t, z, below, :] - cells[t, z, above, :],
+            lambda z: grads[t, z, at, :],
+            depth,
+            depth_total,
+        )
+        store(t, j, values)
+
+    def step(n, carry):
+        t, j = n // 2, 2 * (n % 2)
+        work(t, j)
+        work(t, j + 1)
+        return carry
+
+    lax.fori_loop(0, 2 * tiles, step, 0)
 
 
 def pack(values):
@@ -245,34 +260,38 @@
     return jnp.where(code > 0, value, 0.0)
 
 
+def my_parity():
+    return lax.rem(lax.axis_index("gz"), 2)
+
+
 def theirs_kernel(
-    knots_ref, colour_ref, density_ref, cells_in, grads_in, bx_ref, ax_ref, by_ref, ay_ref, bz_ref, az_ref,
-    out_ref, cells, grads, sides, consts, *, depth_total,
+    consts, cells_in, grads_in, bx_ref, ax_ref, by_ref, ay_ref, bz_ref, az_ref,
+    out_ref, cells, grads, sides, *, depth_total,
 ):
-    prepare(consts, knots_ref, colour_ref, density_ref, depth_total)
+    parity = 1 - my_parity()
     spread_side(bz_ref, sides, 0)
     spread_side(az_ref, sides, 1)
-    place_edges(cells, grads, bx_ref, ax_ref, by_ref, ay_ref)
+    place_edges(cells, grads, bx_ref, ax_ref, by_ref, ay_ref, parity)
 
     def store(t, j, values):
         first, second = pack(values)
         out_ref[j, t] = first
         out_ref[4 + j, t] = second
 
-    parity = 1 - lax.rem(lax.axis_index("gz"), 2)
     half_loop(consts, cells, grads, sides, parity, depth_total, store)
 
 
 def ours_kernel(
-    knots_ref, colour_ref, density_ref, cells, grads, sides, out_ref, consts, *, depth_total,
+    consts, cells_in, grads_in, bx_ref, ax_ref, by_ref, ay_ref, sides,
+    out_ref, cells, grads, *, depth_total,
 ):
-    prepare(consts, knots_ref, colour_ref, density_ref, depth_total)
+    parity = my_parity()
+    place_edges(cells, grads, bx_ref, ax_ref, by_ref, ay_ref, parity)
 
     def store(t, j, values):
         for c in range(4):
             out_ref[4 * c + j, t] = values[c]
 
-    parity = lax.rem(lax.axis_index("gz"), 2)
     half_loop(consts, cells, grads, sides, parity, depth_total, store)
 
 
@@ -300,10 +319,10 @@
     lax.fori_loop(0, tiles, step, 0)
 
 
-def compose_kernel(colour_ref, pieces_ref, image_ref, coverage_ref):
+def compose_kernel(consts, pieces_ref, image_ref, coverage_ref):
     count = pieces_ref.shape[0]
     low_rows = lax.broadcasted_iota(jnp.int32, (SUB, LANES), 0) < 4
-    scales = [full(colour_scale(colour_ref, c)) for c in range(3)]
+    scales = [consts[SCALES + c] for c in range(3)]
     step = COLOUR_SPAN / CODES
     steps_hi = jnp.where(low_rows, step, COVER_SPAN / CODES)
     start_hi = jnp.where(low_rows, -COLOUR_SPAN - step, -COVER_SPAN - COVER_SPAN / CODES)
@@ -386,17 +405,17 @@
     by, ay = neighbours(y_edges, y_edges, "gy")
     bx, ax = neighbours(bottom, top, "gx")
     spread_shape = jax.ShapeDtypeStruct((tiles, depth, PITCH * GROUPS, LANES), f32)
-    cells, grads = pl.pallas_call(
-        spread_kernel,
-        out_shape=(spread_shape, spread_shape),
-        in_specs=[vmem],
-        out_specs=(vmem, vmem),
+    consts_shape = jax.ShapeDtypeStruct((SCALES + 3, SUB, LANES), f32)
+    cells, grads, consts = pl.pallas_call(
+        functools.partial(spread_kernel, depth_total=depth_total),
+        out_shape=(spread_shape, spread_shape, consts_shape),
+        in_specs=[smem] * 3 + [vmem],
+        out_specs=(vmem,) * 3,
         compiler_params=params,
         cost_estimate=cost(1 << 23, 2 << 20),
         name="spread",
-    )(volume)
-    tables = (knot_bins, tf_colour, tf_density)
-    consts = [pltpu.VMEM((40, SUB, LANES), f32)]
+    )(knot_bins, tf_colour, tf_density, volume)
+    work = cost(1 << 26, 1 << 23)
     theirs, cells, grads, sides = pl.pallas_call(
         functools.partial(theirs_kernel, depth_total=depth_total),
         out_shape=(
@@ -405,26 +424,24 @@
             spread_shape,
             jax.ShapeDtypeStruct((2, tiles, PITCH * GROUPS, LANES), f32),
         ),
-        in_specs=[smem] * 3 + [vmem] * 8,
+        in_specs=[vmem] * 9,
         out_specs=(vmem,) * 4,
-        input_output_aliases={3: 1, 4: 2},
-        scratch_shapes=consts,
+        input_output_aliases={1: 1, 2: 2},
         compiler_params=params,
-        cost_estimate=cost(1 << 26, 1 << 23),
+        cost_estimate=work,
         name="theirs",
-    )(*tables, cells, grads, bx, ax, by, ay, bz, az)
-    pairs = [(i, i ^ 1) for i in range(count)]
-    arrived = lax.ppermute(theirs, "gz", pairs)
-    ours = pl.pallas_call(
+    )(consts, cells, grads, bx, ax, by, ay, bz, az)
+    arrived = lax.ppermute(theirs, "gz", [(i, i ^ 1) for i in range(count)])
+    ours, _, _ = pl.pallas_call(
         functools.partial(ours_kernel, depth_total=depth_total),
-        out_shape=jax.ShapeDtypeStruct((16, tiles, SUB, LANES), f32),
-        in_specs=[smem] * 3 + [vmem] * 3,
-        out_specs=vmem,
-        scratch_shapes=consts,
+        out_shape=(jax.ShapeDtypeStruct((16, tiles, SUB, LANES), f32), spread_shape, spread_shape),
+        in_specs=[vmem] * 8,
+        out_specs=(vmem,) * 3,
+        input_output_aliases={1: 1, 2: 2},
         compiler_params=params,
-        cost_estimate=cost(1 << 26, 1 << 23),
+        cost_estimate=work,
         name="ours",
-    )(*tables, cells, grads, sides)
+    )(consts, cells, grads, bx, ax, by, ay, sides)
     half = count // 2
     codes = pl.pallas_call(
         pair_kernel,
@@ -449,10 +466,10 @@
             jax.ShapeDtypeStruct((3, band, cols), f32),
             jax.ShapeDtypeStruct((band, cols), f32),
         ),
-        in_specs=[smem, vmem],
+        in_specs=[vmem, vmem],
         out_specs=(vmem, vmem),
         name="compose",
-    )(tf_colour, pieces)
+    )(consts, pieces)
 
 
 def solution(mesh):

time: 78.1 us -> 76.9 us (0.985)
  the two profiles are of different devices: /device:TPU:10 before, /device:TPU:18 now
where the time goes in v5:
time: 76.9 us; the launch traced here: 76.5 us
  blocking collectives  35.9 us (47%)
  starting transfers between devices  21.2 us (28%)
  Pallas kernels  16.8 us (22%)
  local copies, waits for them, and re-layouts  1.6 us (2%)
  between operations  0.82 us (1%)
    all_to_all x1, blocking collectives, on_device(): lax.all_to_all(codes.reshape(half, tiles * SUB, LANES), 'gz', split_axis=...  35.9 us
    ppermute x6, starting transfers between devices, neighbours(): return (lax.ppermute(last, axis, up), lax.ppermute(initial, axis, down))  16.7 us
    pallas_call x1, Pallas kernels, on_device(): pl.pallas_call(functools.partial(theirs_kernel, depth_total=depth_total),...  5.67 us
    pallas_call x1, Pallas kernels, on_device(): pl.pallas_call(functools.partial(ours_kernel, depth_total=depth_total), o...  5.29 us
    ppermute x1, starting transfers between devices, on_device(): arrived = lax.ppermute(theirs, 'gz', [(i, i ^ 1) for i in range(count)])  4.55 us
    pallas_call x1, Pallas kernels, on_device(): pl.pallas_call(functools.partial(spread_kernel, depth_total=depth_total),...  3.05 us
    pallas_call x1, Pallas kernels, on_device(): pl.pallas_call(compose_kernel, out_shape=(jax.ShapeDtypeStruct((3, band,...  1.85 us
    unnamed x12, local copies, waits for them, and re-layouts  1.6 us
  transfers between devices with their start and end apart: 7, of which 1 were waited for; matrix products, arithmetic and copies ran while one was open for 0% of the time, Pallas kernels for 11%

profile of v5, /device:TPU:18, one launch (start us, length us, event | category | flops | bytes accessed | tf_op | source)
XLA Modules:
  0.0 76.5 jit_solution(16638621251190186667)
XLA Ops:
  0.6 0.0 copy-start
  0.6 1.6 %copy-done = bf16[16,64,1024]{2,1,0:T(8,128)(2,1)S(1)} copy-done((bf16[16,64,1024]{2,1,0:T(8,128)(2,1)S(1)}, bf16[16,64,1024]{2,1,0:T(8,128)(2,1)}, u32[]{:S(2)}) %copy-start) | copy-done | bytes 2097176
  2.2 0.3 edges.1
  2.6 4.0 %collective-permute-start.4 = (bf16[64,1024]{1,0:T(8,128)(2,1)S(1)}, bf16[64,1024]{1,0:T(8,128)(2,1)S(1)}, u32[]{:S(2)}, u32[]{:S(2)}) collective-permute-start(bf16[64,1024]{1,0:T(8,128)(2,1)S(1)} %get-tuple-element.21), channel_id=1, source_target_pairs={{0,1},{1,2},{2,3},{3,4},{4,5},{5,6},{6,7},{7,8},{8,9},{9,10},{10,1... | collective-permute-start | bytes 393224 | tf_op jit(solution)/shard_map/ppermute | solution.py:360
  6.5 1.3 %collective-permute-start.5 = (bf16[64,1024]{1,0:T(8,128)(2,1)S(1)}, bf16[64,1024]{1,0:T(8,128)(2,1)S(1)}, u32[]{:S(2)}, u32[]{:S(2)}) collective-permute-start(bf16[64,1024]{1,0:T(8,128)(2,1)S(1)} %get-tuple-element.22), channel_id=1, source_target_pairs={{1,0},{2,1},{3,2},{4,3},{5,4},{6,5},{7,6},{8,7},{9,8},{10,9},{11,1... | collective-permute-start | bytes 393224 | tf_op jit(solution)/shard_map/ppermute | solution.py:360
  7.8 1.9 %collective-permute-start = (bf16[16,1024]{1,0:T(8,128)(2,1)S(1)}, bf16[16,1024]{1,0:T(8,128)(2,1)S(1)}, u32[]{:S(2)}, u32[]{:S(2)}) collective-permute-start(bf16[16,1024]{1,0:T(8,128)(2,1)S(1)} %get-tuple-element.18), channel_id=1, source_target_pairs={{0,64},{64,128},{128,192},{192,256},{256,320},{320,384},{384,448},... | collective-permute-start | bytes 98312 | tf_op jit(solution)/shard_map/ppermute | solution.py:360
  9.7 3.6 %collective-permute-start.1 = (bf16[16,1024]{1,0:T(8,128)(2,1)S(1)}, bf16[16,1024]{1,0:T(8,128)(2,1)S(1)}, u32[]{:S(2)}, u32[]{:S(2)}) collective-permute-start(bf16[16,1024]{1,0:T(8,128)(2,1)S(1)} %get-tuple-element.19), channel_id=1, source_target_pairs={{64,0},{128,64},{192,128},{256,192},{320,256},{384,320},{448,384},... | collective-permute-start | bytes 98312 | tf_op jit(solution)/shard_map/ppermute | solution.py:360
  13.4 2.4 %collective-permute-start.3 = (f32[64,128]{1,0:T(8,128)S(1)}, f32[64,128]{1,0:T(8,128)S(1)}, u32[]{:S(2)}, u32[]{:S(2)}) collective-permute-start(f32[64,128]{1,0:T(8,128)S(1)} %get-tuple-element.20), channel_id=1, source_target_pairs={{16,0},{32,16},{48,32},{17,1},{33,17},{49,33},{18,2},{34,18},{50,3... | collective-permute-start | bytes 98312 | tf_op jit(solution)/shard_map/ppermute | solution.py:360
  15.8 0.0 collective-permute-done.bx_ref
  15.9 3.4 %collective-permute-start.2 = (f32[64,128]{1,0:T(8,128)S(1)}, f32[64,128]{1,0:T(8,128)S(1)}, u32[]{:S(2)}, u32[]{:S(2)}) collective-permute-start(f32[64,128]{1,0:T(8,128)S(1)} %get-tuple-element.20), channel_id=1, source_target_pairs={{0,16},{16,32},{32,48},{1,17},{17,33},{33,49},{2,18},{18,34},{34,5... | collective-permute-start | bytes 98312 | tf_op jit(solution)/shard_map/ppermute | solution.py:360
  19.3 0.0 copy-done.1
  19.3 3.1 %spread.1 = (f32[8,16,72,128]{3,2,1,0:T(8,128)S(1)}, f32[8,16,72,128]{3,2,1,0:T(8,128)S(1)}, f32[41,8,128]{2,1,0:T(8,128)S(1)}) custom-call(s32[8]{0:T(128)S(1)} %copy-done.4, f32[3,8]{1,0:T(4,128)S(1)} %copy-done.3, f32[8]{0:T(128)S(1)} %copy-done.5, bf16[16,64,1024]{2,1,0:T(8,128)(2,1)S(1)} %copy-done.1), custom_call_target="tpu_custom_call" | custom-call | flops 8388608 | bytes 2097152 | tf_op jit(solution)/shard_map/spread/pallas_call | solution.py:409
  22.4 0.0 collective-permute-done.1.ax_ref
  22.4 0.0 collective-permute-done.3.ay_ref
  22.4 0.0 collective-permute-done.2.by_ref
  22.4 0.0 collective-permute-done.4.bz_ref
  22.4 0.0 collective-permute-done.5.az_ref
  22.4 5.7 %theirs.1 = (s32[8,8,8,128]{3,2,1,0:T(8,128)S(1)}, f32[8,16,72,128]{3,2,1,0:T(8,128)S(1)}, f32[8,16,72,128]{3,2,1,0:T(8,128)S(1)}, f32[2,8,72,128]{3,2,1,0:T(8,128)S(1)}) custom-call(f32[41,8,128]{2,1,0:T(8,128)S(1)} %get-tuple-element.15.consts, f32[8,16,72,128]{3,2,1,0:T(8,128)S(1)} %get-tuple-element.16.cells_in, ...), custom_call_target="tpu_custom_call", output_to_operand_aliasing={{1}: (1, {}), {2}: (2, {})} | custom-call | flops 67108864 | bytes 8388608 | tf_op jit(solution)/shard_map/theirs/pallas_call | solution.py:419
  28.1 4.6 %collective-permute-start.6 = (s32[8,8,8,128]{3,2,1,0:T(8,128)S(1)}, s32[8,8,8,128]{3,2,1,0:T(8,128)S(1)}, u32[]{:S(2)}, u32[]{:S(2)}) collective-permute-start(s32[8,8,8,128]{3,2,1,0:T(8,128)S(1)} %get-tuple-element.27), channel_id=1, source_target_pairs={{0,1},{1,0},{2,3},{3,2},{4,5},{5,4},{6,7},{7,6},{8,9},{9,8},{10,11... | collective-permute-start | bytes 786440 | tf_op jit(solution)/shard_map/ppermute | solution.py:434
  32.7 5.3 %ours.1 = (f32[16,8,8,128]{3,2,1,0:T(8,128)S(1)}, f32[8,16,72,128]{3,2,1,0:T(8,128)S(1)}, f32[8,16,72,128]{3,2,1,0:T(8,128)S(1)}) custom-call(f32[41,8,128]{2,1,0:T(8,128)S(1)} %get-tuple-element.15.consts, f32[8,16,72,128]{3,2,1,0:T(8,128)S(1)} %get-tuple-element.23.cells_in, ...), custom_call_target="tpu_custom_call", output_to_operand_aliasing={{1}: (1, {}), {2}: (2, {})} | custom-call | flops 67108864 | bytes 8388608 | tf_op jit(solution)/shard_map/ours/pallas_call | solution.py:435
  38.0 0.3 collective-permute-done.6.theirs_ref
  38.2 0.6 pair.1
  38.8 35.9 %all_to_all.5.pieces_ref = s32[8,64,128]{2,1,0:T(8,128)} all-to-all(s32[8,64,128]{2,1,0:T(8,128)S(1)} %bitcast.1), channel_id=1, replica_groups={{0,2,4,6,8,10,12,14},{1,3,5,7,9,11,13,15},{16,18,20,22,24,26,28,30},{17..., dimensions={0} | all-to-all | bytes 524288 | tf_op jit(solution)/shard_map/all_to_all | solution.py:454
  74.7 1.8 %compose.1 = (f32[3,4,1024]{2,1,0:T(4,128)}, f32[4,1024]{1,0:T(4,128)}) custom-call(f32[41,8,128]{2,1,0:T(8,128)} %copy-done.2, s32[8,64,128]{2,1,0:T(8,128)} %all_to_all.5.pieces_ref), custom_call_target="tpu_custom_call" | custom-call | tf_op jit(solution)/shard_map/compose/pallas_call | solution.py:463
  (9 shorter events, 0.0 us)
Async XLA Ops:
  0.6 1.6 %copy-start = (bf16[16,64,1024]{2,1,0:T(8,128)(2,1)S(1)}, bf16[16,64,1024]{2,1,0:T(8,128)(2,1)}, u32[]{:S(2)}) copy-start(bf16[16,64,1024]{2,1,0:T(8,128)(2,1)} %z_high.1) | copy-start | bytes 6291460
  2.2 17.0 %copy-start.1 = (bf16[16,64,1024]{2,1,0:T(8,128)(2,1)S(1)}, bf16[16,64,1024]{2,1,0:T(8,128)(2,1)}, u32[]{:S(2)}) copy-start(bf16[16,64,1024]{2,1,0:T(8,128)(2,1)} %z_high.1) | copy-start | bytes 6291460
  2.2 17.1 %copy-start.3 = (f32[3,8]{1,0:T(4,128)S(1)}, f32[3,8]{1,0:T(4,128)}, u32[]{:S(2)}) copy-start(f32[3,8]{1,0:T(4,128)} %colour_ref.1) | copy-start | bytes 292
  2.2 17.1 %copy-start.4 = (s32[8]{0:T(128)S(1)}, s32[8]{0:T(128)}, u32[]{:S(2)}) copy-start(s32[8]{0:T(128)} %knots_ref.1) | copy-start | bytes 100
  2.2 17.1 %copy-start.5 = (f32[8]{0:T(128)S(1)}, f32[8]{0:T(128)}, u32[]{:S(2)}) copy-start(f32[8]{0:T(128)} %density_ref.1) | copy-start | bytes 100
  2.6 19.9 %collective-permute-start.4 = (bf16[64,1024]{1,0:T(8,128)(2,1)S(1)}, bf16[64,1024]{1,0:T(8,128)(2,1)S(1)}, u32[]{:S(2)}, u32[]{:S(2)}) collective-permute-start(bf16[64,1024]{1,0:T(8,128)(2,1)S(1)} %get-tuple-element.21), channel_id=1, source_target_pairs={{0,1},{1,2},{2,3},{3,4},{4,5},{5,6},{6,7},{7,8},{8,9},{9,10},{10,1... | collective-permute-start | bytes 393224 | tf_op jit(solution)/shard_map/ppermute | solution.py:360
  6.5 15.9 %collective-permute-start.5 = (bf16[64,1024]{1,0:T(8,128)(2,1)S(1)}, bf16[64,1024]{1,0:T(8,128)(2,1)S(1)}, u32[]{:S(2)}, u32[]{:S(2)}) collective-permute-start(bf16[64,1024]{1,0:T(8,128)(2,1)S(1)} %get-tuple-element.22), channel_id=1, source_target_pairs={{1,0},{2,1},{3,2},{4,3},{5,4},{6,5},{7,6},{8,7},{9,8},{10,9},{11,1... | collective-permute-start | bytes 393224 | tf_op jit(solution)/shard_map/ppermute | solution.py:360
  7.8 8.0 %collective-permute-start = (bf16[16,1024]{1,0:T(8,128)(2,1)S(1)}, bf16[16,1024]{1,0:T(8,128)(2,1)S(1)}, u32[]{:S(2)}, u32[]{:S(2)}) collective-permute-start(bf16[16,1024]{1,0:T(8,128)(2,1)S(1)} %get-tuple-element.18), channel_id=1, source_target_pairs={{0,64},{64,128},{128,192},{192,256},{256,320},{320,384},{384,448},... | collective-permute-start | bytes 98312 | tf_op jit(solution)/shard_map/ppermute | solution.py:360
  9.7 12.6 %collective-permute-start.1 = (bf16[16,1024]{1,0:T(8,128)(2,1)S(1)}, bf16[16,1024]{1,0:T(8,128)(2,1)S(1)}, u32[]{:S(2)}, u32[]{:S(2)}) collective-permute-start(bf16[16,1024]{1,0:T(8,128)(2,1)S(1)} %get-tuple-element.19), channel_id=1, source_target_pairs={{64,0},{128,64},{192,128},{256,192},{320,256},{384,320},{448,384},... | collective-permute-start | bytes 98312 | tf_op jit(solution)/shard_map/ppermute | solution.py:360
  13.4 9.0 %collective-permute-start.3 = (f32[64,128]{1,0:T(8,128)S(1)}, f32[64,128]{1,0:T(8,128)S(1)}, u32[]{:S(2)}, u32[]{:S(2)}) collective-permute-start(f32[64,128]{1,0:T(8,128)S(1)} %get-tuple-element.20), channel_id=1, source_target_pairs={{16,0},{32,16},{48,32},{17,1},{33,17},{49,33},{18,2},{34,18},{50,3... | collective-permute-start | bytes 98312 | tf_op jit(solution)/shard_map/ppermute | solution.py:360
  15.9 6.5 %collective-permute-start.2 = (f32[64,128]{1,0:T(8,128)S(1)}, f32[64,128]{1,0:T(8,128)S(1)}, u32[]{:S(2)}, u32[]{:S(2)}) collective-permute-start(f32[64,128]{1,0:T(8,128)S(1)} %get-tuple-element.20), channel_id=1, source_target_pairs={{0,16},{16,32},{32,48},{1,17},{17,33},{33,49},{2,18},{18,34},{34,5... | collective-permute-start | bytes 98312 | tf_op jit(solution)/shard_map/ppermute | solution.py:360
  22.4 10.3 %copy-start.2 = (f32[41,8,128]{2,1,0:T(8,128)}, f32[41,8,128]{2,1,0:T(8,128)S(1)}, u32[]{:S(2)}) copy-start(f32[41,8,128]{2,1,0:T(8,128)S(1)} %get-tuple-element.15.consts) | copy-start | bytes 503812
  28.1 10.1 %collective-permute-start.6 = (s32[8,8,8,128]{3,2,1,0:T(8,128)S(1)}, s32[8,8,8,128]{3,2,1,0:T(8,128)S(1)}, u32[]{:S(2)}, u32[]{:S(2)}) collective-permute-start(s32[8,8,8,128]{3,2,1,0:T(8,128)S(1)} %get-tuple-element.27), channel_id=1, source_target_pairs={{0,1},{1,0},{2,3},{3,2},{4,5},{5,4},{6,7},{7,6},{8,9},{9,8},{10,11... | collective-permute-start | bytes 786440 | tf_op jit(solution)/shard_map/ppermute | solution.py:434

commit v6 on v5

--- a/solution.py
+++ b/solution.py
@@ -13,6 +13,7 @@
 KNOTS = 8
 SEGMENTS = KNOTS - 1
 AMBIENT = 0.2
+DIFFUSE = (1.0 - AMBIENT) / 3.0
 LANES = 128
 SUB = 8
 GROUPS = 8
@@ -60,16 +61,21 @@
     return lax.broadcasted_iota(jnp.int32, (SUB, LANES), 1)
 
 
-def edges_kernel(x_low, x_high, y_low, y_high, z_low, z_high, top, bottom, y_out, front, rear, rows_x):
+def is_even(axis):
+    return lax.rem(lax.axis_index(axis), 2) == 0
+
+
+def edges_kernel(x_low, x_high, y_low, y_high, z_low, z_high, x_first, x_second, y_out, z_first, z_second, rows_x):
     depth = x_low.shape[0]
-    cols = x_low.shape[2]
+    even_x, even_z = is_even("gx"), is_even("gz")
     for z in range(depth):
         low = x_low[z].astype(jnp.float32)
         high = x_high[z].astype(jnp.float32)
         rows_x[0, z:z + 1, :] = low[:1]
         rows_x[1, z:z + 1, :] = high[15:]
-    top[...] = rows_x[0].astype(top.dtype)
-    bottom[...] = rows_x[1].astype(bottom.dtype)
+    top, bottom = rows_x[0], rows_x[1]
+    x_first[...] = jnp.where(even_x, bottom, top).astype(x_first.dtype)
+    x_second[...] = jnp.where(even_x, top, bottom).astype(x_second.dtype)
     lane = lane_index()
     for i in range(y_low.shape[1] // 16):
         sides = [jnp.zeros((SUB, LANES), jnp.float32)] * 2
@@ -82,8 +88,16 @@
                 sides[part] = jnp.where(lane == depth + z, high[at, LANES - 1:], sides[part])
         for part in range(2):
             y_out[pl.ds(2 * i + part, SUB, stride=GROUPS), :] = sides[part]
-    front[...] = z_low[0]
-    rear[...] = z_high[0]
+
+    @pl.when(even_z)
+    def _():
+        z_first[...] = z_high[0]
+        z_second[...] = z_low[0]
+
+    @pl.when(jnp.logical_not(even_z))
+    def _():
+        z_first[...] = z_low[0]
+        z_second[...] = z_high[0]
 
 
 def slots_of(i):
@@ -120,25 +134,26 @@
 
 def prepare(consts, knots_ref, colour_ref, density_ref, depth_total):
     top = BINS - 1.0
-    spans = []
+    slants = []
     for k in range(SEGMENTS):
         low = full(knots_ref[k].astype(jnp.float32))
         high = full(knots_ref[k + 1].astype(jnp.float32))
-        spans.append((high - low) * (1.0 / top))
+        slants.append(top / (high - low))
         if k:
-            consts[k - 1] = low / top
+            consts[k - 1] = low * (1.0 / top)
     unit = opacity_terms(10.0 / depth_total)[0] / depth_total
     consts[6] = full(density_ref[0]) * unit
     for k in range(SEGMENTS):
         step = full(density_ref[k + 1]) - full(density_ref[k])
-        consts[7 + k] = step * unit / spans[k]
+        consts[7 + k] = step * unit * slants[k]
     for c in range(3):
         scale = full(colour_scale(colour_ref, c))
         consts[SCALES + c] = scale
-        consts[14 + 8 * c] = full(colour_ref[c, 0]) / scale
+        unscale = DIFFUSE / scale
+        consts[14 + 8 * c] = full(colour_ref[c, 0]) * unscale
         for k in range(SEGMENTS):
             step = full(colour_ref[c, k + 1]) - full(colour_ref[c, k])
-            consts[15 + 8 * c + k] = step / scale / spans[k]
+            consts[15 + 8 * c + k] = step * unscale * slants[k]
 
 
 def composite(consts, cell, grad_x, grad_y, depth, depth_total):
@@ -155,9 +170,7 @@
         gx, gy, gz = grad_x(z), grad_y(z), later - earlier
         across = gy + gz
         facing = jnp.abs(gx + (across + across))
-        shading = AMBIENT + facing * (
-            ((1.0 - AMBIENT) / 3.0) * lax.rsqrt(gx * gx + gy * gy + (gz * gz + 1.0))
-        )
+        shading = AMBIENT / DIFFUSE + facing * lax.rsqrt(gx * gx + gy * gy + (gz * gz + 1.0))
         capped = [jnp.minimum(now, p) for p in points] + [now]
         ramps = [capped[0]] + [capped[k + 1] - capped[k] for k in range(6)]
         y = first
@@ -191,10 +204,12 @@
                 sides[side, t, slots_of(2 * c + part), :] = plane[8 * part:8 * part + 8, lanes_of(t)]
 
 
-def place_edges(cells, grads, bx_ref, ax_ref, by_ref, ay_ref, parity):
+def place_edges(cells, grads, x_first, x_second, y_first, y_second, parity):
     tiles, depth = cells.shape[:2]
     slot = jnp.where(parity == 0, ABOVE, BELOW)
-    edge = jnp.where(parity == 0, bx_ref[...].astype(jnp.float32), ax_ref[...].astype(jnp.float32))
+    even_x, even_y = is_even("gx"), is_even("gy")
+    second = (parity == 0) == even_x
+    edge = jnp.where(second, x_second[...].astype(jnp.float32), x_first[...].astype(jnp.float32))
     for z in range(depth):
         for t in range(tiles):
             cells[t, z, pl.ds(slot, 1), :] = edge[z:z + 1, lanes_of(t)]
@@ -204,7 +219,8 @@
         r = 4 * parity + j
         rows = pl.ds(pl.multiple_of(SUB * r, SUB), SUB)
         at = pl.ds(PITCH * r, SUB)
-        before, after = by_ref[rows, :], ay_ref[rows, :]
+        before = jnp.where(even_y, y_second[rows, :], y_first[rows, :])
+        after = jnp.where(even_y, y_first[rows, :], y_second[rows, :])
         for z in range(depth):
             first = jnp.where(lane == 0, before[:, depth + z:depth + z + 1], 0.0)
             last = jnp.where(lane == LANES - 1, after[:, z:z + 1], 0.0)
@@ -265,13 +281,14 @@
 
 
 def theirs_kernel(
-    consts, cells_in, grads_in, bx_ref, ax_ref, by_ref, ay_ref, bz_ref, az_ref,
+    consts, cells_in, grads_in, x_first, x_second, y_first, y_second, z_first, z_second,
     out_ref, cells, grads, sides, *, depth_total,
 ):
     parity = 1 - my_parity()
-    spread_side(bz_ref, sides, 0)
-    spread_side(az_ref, sides, 1)
-    place_edges(cells, grads, bx_ref, ax_ref, by_ref, ay_ref, parity)
+    before = jnp.where(is_even("gz"), 1, 0)
+    spread_side(z_first, sides, before)
+    spread_side(z_second, sides, 1 - before)
+    place_edges(cells, grads, x_first, x_second, y_first, y_second, parity)
 
     def store(t, j, values):
         first, second = pack(values)
@@ -282,11 +299,11 @@
 
 
 def ours_kernel(
-    consts, cells_in, grads_in, bx_ref, ax_ref, by_ref, ay_ref, sides,
+    consts, cells_in, grads_in, x_first, x_second, y_first, y_second, sides,
     out_ref, cells, grads, *, depth_total,
 ):
     parity = my_parity()
-    place_edges(cells, grads, bx_ref, ax_ref, by_ref, ay_ref, parity)
+    place_edges(cells, grads, x_first, x_second, y_first, y_second, parity)
 
     def store(t, j, values):
         for c in range(4):
@@ -353,11 +370,14 @@
         coverage_ref[:, lanes_of(t)] = high[4:]
 
 
-def neighbours(last, initial, axis):
+def meet(first, second, axis):
     count = lax.axis_size(axis)
-    up = [(i, i + 1) for i in range(count - 1)]
-    down = [(j, i) for i, j in up]
-    return lax.ppermute(last, axis, up), lax.ppermute(initial, axis, down)
+
+    def swap(edge, start):
+        pairs = [(i, i + 1) for i in range(start, count - 1, 2)]
+        return lax.ppermute(edge, axis, pairs + [(j, i) for i, j in pairs])
+
+    return swap(first, 0), swap(second, 1)
 
 
 def cost(flops, moved):
@@ -377,7 +397,7 @@
     def whole(*shape):
         return pl.BlockSpec(shape, lambda n: (0,) * len(shape))
 
-    top, bottom, y_edges, front, rear = pl.pallas_call(
+    x_first, x_second, y_edges, z_first, z_second = pl.pallas_call(
         edges_kernel,
         grid=(1,),
         out_shape=(
@@ -401,9 +421,9 @@
         cost_estimate=cost(1 << 20, 2 << 20),
         name="edges",
     )(*[volume] * 6)
-    bz, az = neighbours(rear, front, "gz")
-    by, ay = neighbours(y_edges, y_edges, "gy")
-    bx, ax = neighbours(bottom, top, "gx")
+    z_got = meet(z_first, z_second, "gz")
+    y_got = meet(y_edges, y_edges, "gy")
+    x_got = meet(x_first, x_second, "gx")
     spread_shape = jax.ShapeDtypeStruct((tiles, depth, PITCH * GROUPS, LANES), f32)
     consts_shape = jax.ShapeDtypeStruct((SCALES + 3, SUB, LANES), f32)
     cells, grads, consts = pl.pallas_call(
@@ -430,7 +450,7 @@
         compiler_params=params,
         cost_estimate=work,
         name="theirs",
-    )(consts, cells, grads, bx, ax, by, ay, bz, az)
+    )(consts, cells, grads, *x_got, *y_got, *z_got)
     arrived = lax.ppermute(theirs, "gz", [(i, i ^ 1) for i in range(count)])
     ours, _, _ = pl.pallas_call(
         functools.partial(ours_kernel, depth_total=depth_total),
@@ -441,7 +461,7 @@
         compiler_params=params,
         cost_estimate=work,
         name="ours",
-    )(consts, cells, grads, bx, ax, by, ay, sides)
+    )(consts, cells, grads, *x_got, *y_got, sides)
     half = count // 2
     codes = pl.pallas_call(
         pair_kernel,

time: 76.9 us -> 76.6 us (level)
  the two profiles are of different devices: /device:TPU:18 before, /device:TPU:10 now
where the time goes in v6:
time: 76.6 us; the launch traced here: 76.3 us
  blocking collectives  33.7 us (44%)
  starting transfers between devices  22.3 us (29%)
  Pallas kernels  16.7 us (22%)
  local copies, waits for them, and re-layouts  1.6 us (2%)
  waiting for transfers between devices  1.19 us (2%)
  between operations  0.82 us (1%)
    all_to_all x1, blocking collectives, on_device(): lax.all_to_all(codes.reshape(half, tiles * SUB, LANES), 'gz', split_axis=...  33.7 us
    ppermute x6, starting transfers between devices, swap(): return lax.ppermute(edge, axis, pairs + [(j, i) for i, j in pairs])  15.6 us
    ppermute x1, starting transfers between devices, on_device(): arrived = lax.ppermute(theirs, 'gz', [(i, i ^ 1) for i in range(count)])  6.68 us
    pallas_call x1, Pallas kernels, on_device(): pl.pallas_call(functools.partial(theirs_kernel, depth_total=depth_total),...  5.63 us
    pallas_call x1, Pallas kernels, on_device(): pl.pallas_call(functools.partial(ours_kernel, depth_total=depth_total), o...  5.26 us
    pallas_call x1, Pallas kernels, on_device(): pl.pallas_call(functools.partial(spread_kernel, depth_total=depth_total),...  3.06 us
    pallas_call x1, Pallas kernels, on_device(): pl.pallas_call(compose_kernel, out_shape=(jax.ShapeDtypeStruct((3, band,...  1.85 us
    unnamed x12, local copies, waits for them, and re-layouts  1.6 us
  transfers between devices with their start and end apart: 7, of which 1 were waited for; matrix products, arithmetic and copies ran while one was open for 0% of the time, Pallas kernels for 11%

profile of v6, /device:TPU:10, one launch (start us, length us, event | category | flops | bytes accessed | tf_op | source)
XLA Modules:
  0.0 76.3 jit_solution(12782283939597687925)
XLA Ops:
  0.6 0.0 copy-start
  0.6 1.6 %copy-done = bf16[16,64,1024]{2,1,0:T(8,128)(2,1)S(1)} copy-done((bf16[16,64,1024]{2,1,0:T(8,128)(2,1)S(1)}, bf16[16,64,1024]{2,1,0:T(8,128)(2,1)}, u32[]{:S(2)}) %copy-start) | copy-done | bytes 2097176
  2.2 0.3 edges.1
  2.6 4.0 %collective-permute-start.4 = (bf16[64,1024]{1,0:T(8,128)(2,1)S(1)}, bf16[64,1024]{1,0:T(8,128)(2,1)S(1)}, u32[]{:S(2)}, u32[]{:S(2)}) collective-permute-start(bf16[64,1024]{1,0:T(8,128)(2,1)S(1)} %get-tuple-element.21), channel_id=1, source_target_pairs={{0,1},{2,3},{4,5},{6,7},{8,9},{10,11},{12,13},{14,15},{1,0},{3,2},... | collective-permute-start | bytes 393224 | tf_op jit(solution)/shard_map/ppermute | solution.py:378
  6.5 0.7 collective-permute-start.5
  7.2 1.9 %collective-permute-start = (bf16[16,1024]{1,0:T(8,128)(2,1)S(1)}, bf16[16,1024]{1,0:T(8,128)(2,1)S(1)}, u32[]{:S(2)}, u32[]{:S(2)}) collective-permute-start(bf16[16,1024]{1,0:T(8,128)(2,1)S(1)} %get-tuple-element.18), channel_id=1, source_target_pairs={{0,64},{128,192},{256,320},{384,448},{64,0},{192,128},{320,256},{4... | collective-permute-start | bytes 98312 | tf_op jit(solution)/shard_map/ppermute | solution.py:378
  9.1 2.5 %collective-permute-start.1 = (bf16[16,1024]{1,0:T(8,128)(2,1)S(1)}, bf16[16,1024]{1,0:T(8,128)(2,1)S(1)}, u32[]{:S(2)}, u32[]{:S(2)}) collective-permute-start(bf16[16,1024]{1,0:T(8,128)(2,1)S(1)} %get-tuple-element.19), channel_id=1, source_target_pairs={{64,128},{192,256},{320,384},{128,64},{256,192},{384,320},{65,129}... | collective-permute-start | bytes 98312 | tf_op jit(solution)/shard_map/ppermute | solution.py:378
  11.6 3.4 %collective-permute-start.3 = (f32[64,128]{1,0:T(8,128)S(1)}, f32[64,128]{1,0:T(8,128)S(1)}, u32[]{:S(2)}, u32[]{:S(2)}) collective-permute-start(f32[64,128]{1,0:T(8,128)S(1)} %get-tuple-element.20), channel_id=1, source_target_pairs={{16,32},{32,16},{17,33},{33,17},{18,34},{34,18},{19,35},{35,19},{2... | collective-permute-start | bytes 98312 | tf_op jit(solution)/shard_map/ppermute | solution.py:378
  15.0 0.0 collective-permute-done.x_first
  15.0 3.2 %collective-permute-start.2 = (f32[64,128]{1,0:T(8,128)S(1)}, f32[64,128]{1,0:T(8,128)S(1)}, u32[]{:S(2)}, u32[]{:S(2)}) collective-permute-start(f32[64,128]{1,0:T(8,128)S(1)} %get-tuple-element.20), channel_id=1, source_target_pairs={{0,16},{32,48},{16,0},{48,32},{1,17},{33,49},{17,1},{49,33},{2,18}... | collective-permute-start | bytes 98312 | tf_op jit(solution)/shard_map/ppermute | solution.py:378
  18.3 3.1 %spread.1 = (f32[8,16,72,128]{3,2,1,0:T(8,128)S(1)}, f32[8,16,72,128]{3,2,1,0:T(8,128)S(1)}, f32[41,8,128]{2,1,0:T(8,128)S(1)}) custom-call(s32[8]{0:T(128)S(1)} %copy-done.4, f32[3,8]{1,0:T(4,128)S(1)} %copy-done.3, f32[8]{0:T(128)S(1)} %copy-done.5, bf16[16,64,1024]{2,1,0:T(8,128)(2,1)S(1)} %copy-done.1), custom_call_target="tpu_custom_call" | custom-call | flops 8388608 | bytes 2097152 | tf_op jit(solution)/shard_map/spread/pallas_call | solution.py:429
  21.3 0.0 copy-start.2
  21.3 0.0 collective-permute-done.1.x_second
  21.3 0.0 collective-permute-done.3.y_second
  21.3 0.0 collective-permute-done.2.y_first
  21.4 0.0 collective-permute-done.4.z_first
  21.4 0.0 collective-permute-done.5.z_second
  21.4 5.6 %theirs.1 = (s32[8,8,8,128]{3,2,1,0:T(8,128)S(1)}, f32[8,16,72,128]{3,2,1,0:T(8,128)S(1)}, f32[8,16,72,128]{3,2,1,0:T(8,128)S(1)}, f32[2,8,72,128]{3,2,1,0:T(8,128)S(1)}) custom-call(f32[41,8,128]{2,1,0:T(8,128)S(1)} %get-tuple-element.15.consts, f32[8,16,72,128]{3,2,1,0:T(8,128)S(1)} %get-tuple-element.16.cells_in, ...), custom_call_target="tpu_custom_call", output_to_operand_aliasing={{1}: (1, {}), {2}: (2, {})} | custom-call | flops 67108864 | bytes 8388608 | tf_op jit(solution)/shard_map/theirs/pallas_call | solution.py:439
  27.0 6.7 %collective-permute-start.6 = (s32[8,8,8,128]{3,2,1,0:T(8,128)S(1)}, s32[8,8,8,128]{3,2,1,0:T(8,128)S(1)}, u32[]{:S(2)}, u32[]{:S(2)}) collective-permute-start(s32[8,8,8,128]{3,2,1,0:T(8,128)S(1)} %get-tuple-element.27), channel_id=1, source_target_pairs={{0,1},{1,0},{2,3},{3,2},{4,5},{5,4},{6,7},{7,6},{8,9},{9,8},{10,11... | collective-permute-start | bytes 786440 | tf_op jit(solution)/shard_map/ppermute | solution.py:454
  33.7 5.3 %ours.1 = (f32[16,8,8,128]{3,2,1,0:T(8,128)S(1)}, f32[8,16,72,128]{3,2,1,0:T(8,128)S(1)}, f32[8,16,72,128]{3,2,1,0:T(8,128)S(1)}) custom-call(f32[41,8,128]{2,1,0:T(8,128)S(1)} %get-tuple-element.15.consts, f32[8,16,72,128]{3,2,1,0:T(8,128)S(1)} %get-tuple-element.23.cells_in, ...), custom_call_target="tpu_custom_call", output_to_operand_aliasing={{1}: (1, {}), {2}: (2, {})} | custom-call | flops 67108864 | bytes 8388608 | tf_op jit(solution)/shard_map/ours/pallas_call | solution.py:455
  39.0 1.2 %collective-permute-done.6.theirs_ref = s32[8,8,8,128]{3,2,1,0:T(8,128)S(1)} collective-permute-done((s32[8,8,8,128]{3,2,1,0:T(8,128)S(1)}, s32[8,8,8,128]{3,2,1,0:T(8,128)S(1)}, u32[]{:S(2)}, u32[]{:S(2)}) %collective-permute-start.6) | collective-permute-done | bytes 262176 | tf_op jit(solution)/shard_map/ppermute | solution.py:454
  40.2 0.6 pair.1
  40.7 33.7 %all_to_all.5.pieces_ref = s32[8,64,128]{2,1,0:T(8,128)} all-to-all(s32[8,64,128]{2,1,0:T(8,128)S(1)} %bitcast.1), channel_id=1, replica_groups={{0,2,4,6,8,10,12,14},{1,3,5,7,9,11,13,15},{16,18,20,22,24,26,28,30},{17..., dimensions={0} | all-to-all | bytes 524288 | tf_op jit(solution)/shard_map/all_to_all | solution.py:474
  74.4 1.8 %compose.1 = (f32[3,4,1024]{2,1,0:T(4,128)}, f32[4,1024]{1,0:T(4,128)}) custom-call(f32[41,8,128]{2,1,0:T(8,128)} %copy-done.2, s32[8,64,128]{2,1,0:T(8,128)} %all_to_all.5.pieces_ref), custom_call_target="tpu_custom_call" | custom-call | tf_op jit(solution)/shard_map/compose/pallas_call | solution.py:483
  (9 shorter events, 0.0 us)
Async XLA Ops:
  0.6 1.6 %copy-start = (bf16[16,64,1024]{2,1,0:T(8,128)(2,1)S(1)}, bf16[16,64,1024]{2,1,0:T(8,128)(2,1)}, u32[]{:S(2)}) copy-start(bf16[16,64,1024]{2,1,0:T(8,128)(2,1)} %z_high.1) | copy-start | bytes 6291460
  2.2 16.0 %copy-start.1 = (bf16[16,64,1024]{2,1,0:T(8,128)(2,1)S(1)}, bf16[16,64,1024]{2,1,0:T(8,128)(2,1)}, u32[]{:S(2)}) copy-start(bf16[16,64,1024]{2,1,0:T(8,128)(2,1)} %z_high.1) | copy-start | bytes 6291460
  2.2 16.0 %copy-start.3 = (f32[3,8]{1,0:T(4,128)S(1)}, f32[3,8]{1,0:T(4,128)}, u32[]{:S(2)}) copy-start(f32[3,8]{1,0:T(4,128)} %colour_ref.1) | copy-start | bytes 292
  2.2 16.0 %copy-start.4 = (s32[8]{0:T(128)S(1)}, s32[8]{0:T(128)}, u32[]{:S(2)}) copy-start(s32[8]{0:T(128)} %knots_ref.1) | copy-start | bytes 100
  2.2 16.0 %copy-start.5 = (f32[8]{0:T(128)S(1)}, f32[8]{0:T(128)}, u32[]{:S(2)}) copy-start(f32[8]{0:T(128)} %density_ref.1) | copy-start | bytes 100
  2.6 18.8 %collective-permute-start.4 = (bf16[64,1024]{1,0:T(8,128)(2,1)S(1)}, bf16[64,1024]{1,0:T(8,128)(2,1)S(1)}, u32[]{:S(2)}, u32[]{:S(2)}) collective-permute-start(bf16[64,1024]{1,0:T(8,128)(2,1)S(1)} %get-tuple-element.21), channel_id=1, source_target_pairs={{0,1},{2,3},{4,5},{6,7},{8,9},{10,11},{12,13},{14,15},{1,0},{3,2},... | collective-permute-start | bytes 393224 | tf_op jit(solution)/shard_map/ppermute | solution.py:378
  6.5 14.8 %collective-permute-start.5 = (bf16[64,1024]{1,0:T(8,128)(2,1)S(1)}, bf16[64,1024]{1,0:T(8,128)(2,1)S(1)}, u32[]{:S(2)}, u32[]{:S(2)}) collective-permute-start(bf16[64,1024]{1,0:T(8,128)(2,1)S(1)} %get-tuple-element.22), channel_id=1, source_target_pairs={{1,2},{3,4},{5,6},{7,8},{9,10},{11,12},{13,14},{2,1},{4,3},{6,5},{... | collective-permute-start | bytes 393224 | tf_op jit(solution)/shard_map/ppermute | solution.py:378
  7.2 7.8 %collective-permute-start = (bf16[16,1024]{1,0:T(8,128)(2,1)S(1)}, bf16[16,1024]{1,0:T(8,128)(2,1)S(1)}, u32[]{:S(2)}, u32[]{:S(2)}) collective-permute-start(bf16[16,1024]{1,0:T(8,128)(2,1)S(1)} %get-tuple-element.18), channel_id=1, source_target_pairs={{0,64},{128,192},{256,320},{384,448},{64,0},{192,128},{320,256},{4... | collective-permute-start | bytes 98312 | tf_op jit(solution)/shard_map/ppermute | solution.py:378
  9.1 12.2 %collective-permute-start.1 = (bf16[16,1024]{1,0:T(8,128)(2,1)S(1)}, bf16[16,1024]{1,0:T(8,128)(2,1)S(1)}, u32[]{:S(2)}, u32[]{:S(2)}) collective-permute-start(bf16[16,1024]{1,0:T(8,128)(2,1)S(1)} %get-tuple-element.19), channel_id=1, source_target_pairs={{64,128},{192,256},{320,384},{128,64},{256,192},{384,320},{65,129}... | collective-permute-start | bytes 98312 | tf_op jit(solution)/shard_map/ppermute | solution.py:378
  11.6 9.7 %collective-permute-start.3 = (f32[64,128]{1,0:T(8,128)S(1)}, f32[64,128]{1,0:T(8,128)S(1)}, u32[]{:S(2)}, u32[]{:S(2)}) collective-permute-start(f32[64,128]{1,0:T(8,128)S(1)} %get-tuple-element.20), channel_id=1, source_target_pairs={{16,32},{32,16},{17,33},{33,17},{18,34},{34,18},{19,35},{35,19},{2... | collective-permute-start | bytes 98312 | tf_op jit(solution)/shard_map/ppermute | solution.py:378
  15.0 6.3 %collective-permute-start.2 = (f32[64,128]{1,0:T(8,128)S(1)}, f32[64,128]{1,0:T(8,128)S(1)}, u32[]{:S(2)}, u32[]{:S(2)}) collective-permute-start(f32[64,128]{1,0:T(8,128)S(1)} %get-tuple-element.20), channel_id=1, source_target_pairs={{0,16},{32,48},{16,0},{48,32},{1,17},{33,49},{17,1},{49,33},{2,18}... | collective-permute-start | bytes 98312 | tf_op jit(solution)/shard_map/ppermute | solution.py:378
  21.3 12.4 %copy-start.2 = (f32[41,8,128]{2,1,0:T(8,128)}, f32[41,8,128]{2,1,0:T(8,128)S(1)}, u32[]{:S(2)}) copy-start(f32[41,8,128]{2,1,0:T(8,128)S(1)} %get-tuple-element.15.consts) | copy-start | bytes 503812
  27.0 13.1 %collective-permute-start.6 = (s32[8,8,8,128]{3,2,1,0:T(8,128)S(1)}, s32[8,8,8,128]{3,2,1,0:T(8,128)S(1)}, u32[]{:S(2)}, u32[]{:S(2)}) collective-permute-start(s32[8,8,8,128]{3,2,1,0:T(8,128)S(1)} %get-tuple-element.27), channel_id=1, source_target_pairs={{0,1},{1,0},{2,3},{3,2},{4,5},{5,4},{6,7},{7,6},{8,9},{9,8},{10,11... | collective-permute-start | bytes 786440 | tf_op jit(solution)/shard_map/ppermute | solution.py:454

commit v7 on v6

--- a/solution.py
+++ b/solution.py
@@ -281,7 +281,7 @@
 
 
 def theirs_kernel(
-    consts, cells_in, grads_in, x_first, x_second, y_first, y_second, z_first, z_second,
+    consts, cells_in, grads_in, y_second, y_first, x_first, x_second, z_first, z_second,
     out_ref, cells, grads, sides, *, depth_total,
 ):
     parity = 1 - my_parity()
@@ -299,7 +299,7 @@
 
 
 def ours_kernel(
-    consts, cells_in, grads_in, x_first, x_second, y_first, y_second, sides,
+    consts, cells_in, grads_in, y_second, y_first, x_first, x_second, sides,
     out_ref, cells, grads, *, depth_total,
 ):
     parity = my_parity()
@@ -450,7 +450,7 @@
         compiler_params=params,
         cost_estimate=work,
         name="theirs",
-    )(consts, cells, grads, *x_got, *y_got, *z_got)
+    )(consts, cells, grads, *y_got[::-1], *x_got, *z_got)
     arrived = lax.ppermute(theirs, "gz", [(i, i ^ 1) for i in range(count)])
     ours, _, _ = pl.pallas_call(
         functools.partial(ours_kernel, depth_total=depth_total),
@@ -461,7 +461,7 @@
         compiler_params=params,
         cost_estimate=work,
         name="ours",
-    )(consts, cells, grads, *x_got, *y_got, sides)
+    )(consts, cells, grads, *y_got[::-1], *x_got, sides)
     half = count // 2
     codes = pl.pallas_call(
         pair_kernel,

time: 76.6 us -> 76.3 us (level)
  the two profiles are of different devices: /device:TPU:10 before, /device:TPU:12 now
where the time goes in v7:
time: 76.3 us; the launch traced here: 76 us
  blocking collectives  33.7 us (44%)
  starting transfers between devices  22.5 us (29%)
  Pallas kernels  16.7 us (22%)
  local copies, waits for them, and re-layouts  1.6 us (2%)
  between operations  0.82 us (1%)
    all_to_all x1, blocking collectives, on_device(): lax.all_to_all(codes.reshape(half, tiles * SUB, LANES), 'gz', split_axis=...  33.7 us
    ppermute x6, starting transfers between devices, swap(): return lax.ppermute(edge, axis, pairs + [(j, i) for i, j in pairs])  17.4 us
    pallas_call x1, Pallas kernels, on_device(): pl.pallas_call(functools.partial(theirs_kernel, depth_total=depth_total),...  5.63 us
    pallas_call x1, Pallas kernels, on_device(): pl.pallas_call(functools.partial(ours_kernel, depth_total=depth_total), o...  5.26 us
    ppermute x1, starting transfers between devices, on_device(): arrived = lax.ppermute(theirs, 'gz', [(i, i ^ 1) for i in range(count)])  5.16 us
    pallas_call x1, Pallas kernels, on_device(): pl.pallas_call(functools.partial(spread_kernel, depth_total=depth_total),...  3.06 us
    pallas_call x1, Pallas kernels, on_device(): pl.pallas_call(compose_kernel, out_shape=(jax.ShapeDtypeStruct((3, band,...  1.85 us
    unnamed x12, local copies, waits for them, and re-layouts  1.6 us
  transfers between devices with their start and end apart: 7, of which 1 were waited for; matrix products, arithmetic and copies ran while one was open for 0% of the time, Pallas kernels for 11%

profile of v7, /device:TPU:12, one launch (start us, length us, event | category | flops | bytes accessed | tf_op | source)
XLA Modules:
  0.0 76.0 jit_solution(16257390630136153077)
XLA Ops:
  0.6 1.6 %copy-done = bf16[16,64,1024]{2,1,0:T(8,128)(2,1)S(1)} copy-done((bf16[16,64,1024]{2,1,0:T(8,128)(2,1)S(1)}, bf16[16,64,1024]{2,1,0:T(8,128)(2,1)}, u32[]{:S(2)}) %copy-start) | copy-done | bytes 2097176
  2.2 0.3 edges.1
  2.6 4.0 %collective-permute-start.4 = (bf16[64,1024]{1,0:T(8,128)(2,1)S(1)}, bf16[64,1024]{1,0:T(8,128)(2,1)S(1)}, u32[]{:S(2)}, u32[]{:S(2)}) collective-permute-start(bf16[64,1024]{1,0:T(8,128)(2,1)S(1)} %get-tuple-element.21), channel_id=1, source_target_pairs={{0,1},{2,3},{4,5},{6,7},{8,9},{10,11},{12,13},{14,15},{1,0},{3,2},... | collective-permute-start | bytes 393224 | tf_op jit(solution)/shard_map/ppermute | solution.py:378
  6.5 0.7 collective-permute-start.5
  7.2 1.9 %collective-permute-start.2 = (bf16[16,1024]{1,0:T(8,128)(2,1)S(1)}, bf16[16,1024]{1,0:T(8,128)(2,1)S(1)}, u32[]{:S(2)}, u32[]{:S(2)}) collective-permute-start(bf16[16,1024]{1,0:T(8,128)(2,1)S(1)} %get-tuple-element.19), channel_id=1, source_target_pairs={{0,64},{128,192},{256,320},{384,448},{64,0},{192,128},{320,256},{4... | collective-permute-start | bytes 98312 | tf_op jit(solution)/shard_map/ppermute | solution.py:378
  9.1 2.5 %collective-permute-start.3 = (bf16[16,1024]{1,0:T(8,128)(2,1)S(1)}, bf16[16,1024]{1,0:T(8,128)(2,1)S(1)}, u32[]{:S(2)}, u32[]{:S(2)}) collective-permute-start(bf16[16,1024]{1,0:T(8,128)(2,1)S(1)} %get-tuple-element.20), channel_id=1, source_target_pairs={{64,128},{192,256},{320,384},{128,64},{256,192},{384,320},{65,129}... | collective-permute-start | bytes 98312 | tf_op jit(solution)/shard_map/ppermute | solution.py:378
  11.6 3.1 %collective-permute-start.1 = (f32[64,128]{1,0:T(8,128)S(1)}, f32[64,128]{1,0:T(8,128)S(1)}, u32[]{:S(2)}, u32[]{:S(2)}) collective-permute-start(f32[64,128]{1,0:T(8,128)S(1)} %get-tuple-element.18), channel_id=1, source_target_pairs={{0,16},{32,48},{16,0},{48,32},{1,17},{33,49},{17,1},{49,33},{2,18}... | collective-permute-start | bytes 98312 | tf_op jit(solution)/shard_map/ppermute | solution.py:378
  14.7 0.0 collective-permute-done.2.x_first
  14.7 5.2 %collective-permute-start = (f32[64,128]{1,0:T(8,128)S(1)}, f32[64,128]{1,0:T(8,128)S(1)}, u32[]{:S(2)}, u32[]{:S(2)}) collective-permute-start(f32[64,128]{1,0:T(8,128)S(1)} %get-tuple-element.18), channel_id=1, source_target_pairs={{16,32},{32,16},{17,33},{33,17},{18,34},{34,18},{19,35},{35,19},{2... | collective-permute-start | bytes 98312 | tf_op jit(solution)/shard_map/ppermute | solution.py:378
  20.0 0.0 copy-done.1
  20.0 0.0 copy-done.3
  20.0 3.1 %spread.1 = (f32[8,16,72,128]{3,2,1,0:T(8,128)S(1)}, f32[8,16,72,128]{3,2,1,0:T(8,128)S(1)}, f32[41,8,128]{2,1,0:T(8,128)S(1)}) custom-call(s32[8]{0:T(128)S(1)} %copy-done.4, f32[3,8]{1,0:T(4,128)S(1)} %copy-done.3, f32[8]{0:T(128)S(1)} %copy-done.5, bf16[16,64,1024]{2,1,0:T(8,128)(2,1)S(1)} %copy-done.1), custom_call_target="tpu_custom_call" | custom-call | flops 8388608 | bytes 2097152 | tf_op jit(solution)/shard_map/spread/pallas_call | solution.py:429
  23.1 0.0 collective-permute-done.3.x_second
  23.1 0.0 collective-permute-done.1.y_first
  23.1 0.0 collective-permute-done.y_second
  23.1 0.0 collective-permute-done.4.z_first
  23.1 0.0 collective-permute-done.5.z_second
  23.2 5.6 %theirs.1 = (s32[8,8,8,128]{3,2,1,0:T(8,128)S(1)}, f32[8,16,72,128]{3,2,1,0:T(8,128)S(1)}, f32[8,16,72,128]{3,2,1,0:T(8,128)S(1)}, f32[2,8,72,128]{3,2,1,0:T(8,128)S(1)}) custom-call(f32[41,8,128]{2,1,0:T(8,128)S(1)} %get-tuple-element.15.consts, f32[8,16,72,128]{3,2,1,0:T(8,128)S(1)} %get-tuple-element.16.cells_in, ...), custom_call_target="tpu_custom_call", output_to_operand_aliasing={{1}: (1, {}), {2}: (2, {})} | custom-call | flops 67108864 | bytes 8388608 | tf_op jit(solution)/shard_map/theirs/pallas_call | solution.py:439
  28.8 5.2 %collective-permute-start.6 = (s32[8,8,8,128]{3,2,1,0:T(8,128)S(1)}, s32[8,8,8,128]{3,2,1,0:T(8,128)S(1)}, u32[]{:S(2)}, u32[]{:S(2)}) collective-permute-start(s32[8,8,8,128]{3,2,1,0:T(8,128)S(1)} %get-tuple-element.27), channel_id=1, source_target_pairs={{0,1},{1,0},{2,3},{3,2},{4,5},{5,4},{6,7},{7,6},{8,9},{9,8},{10,11... | collective-permute-start | bytes 786440 | tf_op jit(solution)/shard_map/ppermute | solution.py:454
  34.0 5.3 %ours.1 = (f32[16,8,8,128]{3,2,1,0:T(8,128)S(1)}, f32[8,16,72,128]{3,2,1,0:T(8,128)S(1)}, f32[8,16,72,128]{3,2,1,0:T(8,128)S(1)}) custom-call(f32[41,8,128]{2,1,0:T(8,128)S(1)} %get-tuple-element.15.consts, f32[8,16,72,128]{3,2,1,0:T(8,128)S(1)} %get-tuple-element.23.cells_in, ...), custom_call_target="tpu_custom_call", output_to_operand_aliasing={{1}: (1, {}), {2}: (2, {})} | custom-call | flops 67108864 | bytes 8388608 | tf_op jit(solution)/shard_map/ours/pallas_call | solution.py:455
  39.2 0.6 collective-permute-done.6.theirs_ref
  39.9 0.6 pair.1
  40.5 33.7 %all_to_all.5.pieces_ref = s32[8,64,128]{2,1,0:T(8,128)} all-to-all(s32[8,64,128]{2,1,0:T(8,128)S(1)} %bitcast.1), channel_id=1, replica_groups={{0,2,4,6,8,10,12,14},{1,3,5,7,9,11,13,15},{16,18,20,22,24,26,28,30},{17..., dimensions={0} | all-to-all | bytes 524288 | tf_op jit(solution)/shard_map/all_to_all | solution.py:474
  74.1 1.8 %compose.1 = (f32[3,4,1024]{2,1,0:T(4,128)}, f32[4,1024]{1,0:T(4,128)}) custom-call(f32[41,8,128]{2,1,0:T(8,128)} %copy-done.2, s32[8,64,128]{2,1,0:T(8,128)} %all_to_all.5.pieces_ref), custom_call_target="tpu_custom_call" | custom-call | tf_op jit(solution)/shard_map/compose/pallas_call | solution.py:483
  (9 shorter events, 0.0 us)
Async XLA Ops:
  0.6 1.6 %copy-start = (bf16[16,64,1024]{2,1,0:T(8,128)(2,1)S(1)}, bf16[16,64,1024]{2,1,0:T(8,128)(2,1)}, u32[]{:S(2)}) copy-start(bf16[16,64,1024]{2,1,0:T(8,128)(2,1)} %z_high.1) | copy-start | bytes 6291460
  2.2 17.8 %copy-start.1 = (bf16[16,64,1024]{2,1,0:T(8,128)(2,1)S(1)}, bf16[16,64,1024]{2,1,0:T(8,128)(2,1)}, u32[]{:S(2)}) copy-start(bf16[16,64,1024]{2,1,0:T(8,128)(2,1)} %z_high.1) | copy-start | bytes 6291460
  2.2 17.8 %copy-start.3 = (f32[3,8]{1,0:T(4,128)S(1)}, f32[3,8]{1,0:T(4,128)}, u32[]{:S(2)}) copy-start(f32[3,8]{1,0:T(4,128)} %colour_ref.1) | copy-start | bytes 292
  2.2 17.8 %copy-start.4 = (s32[8]{0:T(128)S(1)}, s32[8]{0:T(128)}, u32[]{:S(2)}) copy-start(s32[8]{0:T(128)} %knots_ref.1) | copy-start | bytes 100
  2.2 17.8 %copy-start.5 = (f32[8]{0:T(128)S(1)}, f32[8]{0:T(128)}, u32[]{:S(2)}) copy-start(f32[8]{0:T(128)} %density_ref.1) | copy-start | bytes 100
  2.6 20.6 %collective-permute-start.4 = (bf16[64,1024]{1,0:T(8,128)(2,1)S(1)}, bf16[64,1024]{1,0:T(8,128)(2,1)S(1)}, u32[]{:S(2)}, u32[]{:S(2)}) collective-permute-start(bf16[64,1024]{1,0:T(8,128)(2,1)S(1)} %get-tuple-element.21), channel_id=1, source_target_pairs={{0,1},{2,3},{4,5},{6,7},{8,9},{10,11},{12,13},{14,15},{1,0},{3,2},... | collective-permute-start | bytes 393224 | tf_op jit(solution)/shard_map/ppermute | solution.py:378
  6.5 16.6 %collective-permute-start.5 = (bf16[64,1024]{1,0:T(8,128)(2,1)S(1)}, bf16[64,1024]{1,0:T(8,128)(2,1)S(1)}, u32[]{:S(2)}, u32[]{:S(2)}) collective-permute-start(bf16[64,1024]{1,0:T(8,128)(2,1)S(1)} %get-tuple-element.22), channel_id=1, source_target_pairs={{1,2},{3,4},{5,6},{7,8},{9,10},{11,12},{13,14},{2,1},{4,3},{6,5},{... | collective-permute-start | bytes 393224 | tf_op jit(solution)/shard_map/ppermute | solution.py:378
  7.2 7.5 %collective-permute-start.2 = (bf16[16,1024]{1,0:T(8,128)(2,1)S(1)}, bf16[16,1024]{1,0:T(8,128)(2,1)S(1)}, u32[]{:S(2)}, u32[]{:S(2)}) collective-permute-start(bf16[16,1024]{1,0:T(8,128)(2,1)S(1)} %get-tuple-element.19), channel_id=1, source_target_pairs={{0,64},{128,192},{256,320},{384,448},{64,0},{192,128},{320,256},{4... | collective-permute-start | bytes 98312 | tf_op jit(solution)/shard_map/ppermute | solution.py:378
  9.1 14.0 %collective-permute-start.3 = (bf16[16,1024]{1,0:T(8,128)(2,1)S(1)}, bf16[16,1024]{1,0:T(8,128)(2,1)S(1)}, u32[]{:S(2)}, u32[]{:S(2)}) collective-permute-start(bf16[16,1024]{1,0:T(8,128)(2,1)S(1)} %get-tuple-element.20), channel_id=1, source_target_pairs={{64,128},{192,256},{320,384},{128,64},{256,192},{384,320},{65,129}... | collective-permute-start | bytes 98312 | tf_op jit(solution)/shard_map/ppermute | solution.py:378
  11.6 11.5 %collective-permute-start.1 = (f32[64,128]{1,0:T(8,128)S(1)}, f32[64,128]{1,0:T(8,128)S(1)}, u32[]{:S(2)}, u32[]{:S(2)}) collective-permute-start(f32[64,128]{1,0:T(8,128)S(1)} %get-tuple-element.18), channel_id=1, source_target_pairs={{0,16},{32,48},{16,0},{48,32},{1,17},{33,49},{17,1},{49,33},{2,18}... | collective-permute-start | bytes 98312 | tf_op jit(solution)/shard_map/ppermute | solution.py:378
  14.7 8.4 %collective-permute-start = (f32[64,128]{1,0:T(8,128)S(1)}, f32[64,128]{1,0:T(8,128)S(1)}, u32[]{:S(2)}, u32[]{:S(2)}) collective-permute-start(f32[64,128]{1,0:T(8,128)S(1)} %get-tuple-element.18), channel_id=1, source_target_pairs={{16,32},{32,16},{17,33},{33,17},{18,34},{34,18},{19,35},{35,19},{2... | collective-permute-start | bytes 98312 | tf_op jit(solution)/shard_map/ppermute | solution.py:378
  23.1 10.9 %copy-start.2 = (f32[41,8,128]{2,1,0:T(8,128)}, f32[41,8,128]{2,1,0:T(8,128)S(1)}, u32[]{:S(2)}) copy-start(f32[41,8,128]{2,1,0:T(8,128)S(1)} %get-tuple-element.15.consts) | copy-start | bytes 503812
  28.8 11.1 %collective-permute-start.6 = (s32[8,8,8,128]{3,2,1,0:T(8,128)S(1)}, s32[8,8,8,128]{3,2,1,0:T(8,128)S(1)}, u32[]{:S(2)}, u32[]{:S(2)}) collective-permute-start(s32[8,8,8,128]{3,2,1,0:T(8,128)S(1)} %get-tuple-element.27), channel_id=1, source_target_pairs={{0,1},{1,0},{2,3},{3,2},{4,5},{5,4},{6,7},{7,6},{8,9},{9,8},{10,11... | collective-permute-start | bytes 786440 | tf_op jit(solution)/shard_map/ppermute | solution.py:454

commit v8 on v6

--- a/solution.py
+++ b/solution.py
@@ -204,11 +204,10 @@
                 sides[side, t, slots_of(2 * c + part), :] = plane[8 * part:8 * part + 8, lanes_of(t)]
 
 
-def place_edges(cells, grads, x_first, x_second, y_first, y_second, parity):
+def place_edges(cells, grads, x_first, x_second, y_before, y_after, parity):
     tiles, depth = cells.shape[:2]
     slot = jnp.where(parity == 0, ABOVE, BELOW)
-    even_x, even_y = is_even("gx"), is_even("gy")
-    second = (parity == 0) == even_x
+    second = (parity == 0) == is_even("gx")
     edge = jnp.where(second, x_second[...].astype(jnp.float32), x_first[...].astype(jnp.float32))
     for z in range(depth):
         for t in range(tiles):
@@ -219,8 +218,7 @@
         r = 4 * parity + j
         rows = pl.ds(pl.multiple_of(SUB * r, SUB), SUB)
         at = pl.ds(PITCH * r, SUB)
-        before = jnp.where(even_y, y_second[rows, :], y_first[rows, :])
-        after = jnp.where(even_y, y_first[rows, :], y_second[rows, :])
+        before, after = y_before[rows, :], y_after[rows, :]
         for z in range(depth):
             first = jnp.where(lane == 0, before[:, depth + z:depth + z + 1], 0.0)
             last = jnp.where(lane == LANES - 1, after[:, z:z + 1], 0.0)
@@ -281,14 +279,14 @@
 
 
 def theirs_kernel(
-    consts, cells_in, grads_in, x_first, x_second, y_first, y_second, z_first, z_second,
+    consts, cells_in, grads_in, x_first, x_second, y_before, y_after, z_first, z_second,
     out_ref, cells, grads, sides, *, depth_total,
 ):
     parity = 1 - my_parity()
     before = jnp.where(is_even("gz"), 1, 0)
     spread_side(z_first, sides, before)
     spread_side(z_second, sides, 1 - before)
-    place_edges(cells, grads, x_first, x_second, y_first, y_second, parity)
+    place_edges(cells, grads, x_first, x_second, y_before, y_after, parity)
 
     def store(t, j, values):
         first, second = pack(values)
@@ -299,11 +297,11 @@
 
 
 def ours_kernel(
-    consts, cells_in, grads_in, x_first, x_second, y_first, y_second, sides,
+    consts, cells_in, grads_in, x_first, x_second, y_before, y_after, sides,
     out_ref, cells, grads, *, depth_total,
 ):
     parity = my_parity()
-    place_edges(cells, grads, x_first, x_second, y_first, y_second, parity)
+    place_edges(cells, grads, x_first, x_second, y_before, y_after, parity)
 
     def store(t, j, values):
         for c in range(4):
@@ -378,6 +376,13 @@
         return lax.ppermute(edge, axis, pairs + [(j, i) for i, j in pairs])
 
     return swap(first, 0), swap(second, 1)
+
+
+def shift_both(edges, axis):
+    count = lax.axis_size(axis)
+    up = [(i, i + 1) for i in range(count - 1)]
+    down = [(j, i) for i, j in up]
+    return lax.ppermute(edges, axis, up), lax.ppermute(edges, axis, down)
 
 
 def cost(flops, moved):
@@ -422,7 +427,7 @@
         name="edges",
     )(*[volume] * 6)
     z_got = meet(z_first, z_second, "gz")
-    y_got = meet(y_edges, y_edges, "gy")
+    y_got = shift_both(y_edges, "gy")
     x_got = meet(x_first, x_second, "gx")
     spread_shape = jax.ShapeDtypeStruct((tiles, depth, PITCH * GROUPS, LANES), f32)
     consts_shape = jax.ShapeDtypeStruct((SCALES + 3, SUB, LANES), f32)

time: 76.6 us -> 75.9 us (level)
  the two profiles are of different devices: /device:TPU:10 before, /device:TPU:14 now
where the time goes in v8:
time: 75.9 us; the launch traced here: 75.6 us
  blocking collectives  33.7 us (44%)
  starting transfers between devices  20 us (26%)
  Pallas kernels  16.7 us (22%)
  waiting for transfers between devices  2.82 us (4%)
  local copies, waits for them, and re-layouts  1.6 us (2%)
  between operations  0.8 us (1%)
    all_to_all x1, blocking collectives, on_device(): lax.all_to_all(codes.reshape(half, tiles * SUB, LANES), 'gz', split_axis=...  33.7 us
    ppermute x4, starting transfers between devices, swap(): return lax.ppermute(edge, axis, pairs + [(j, i) for i, j in pairs])  9.01 us
    ppermute x1, starting transfers between devices, on_device(): arrived = lax.ppermute(theirs, 'gz', [(i, i ^ 1) for i in range(count)])  6.97 us
    pallas_call x1, Pallas kernels, on_device(): pl.pallas_call(functools.partial(theirs_kernel, depth_total=depth_total),...  5.62 us
    pallas_call x1, Pallas kernels, on_device(): pl.pallas_call(functools.partial(ours_kernel, depth_total=depth_total), o...  5.25 us
    ppermute x2, starting transfers between devices, shift_both(): return (lax.ppermute(edges, axis, up), lax.ppermute(edges, axis, down))  4.03 us
    pallas_call x1, Pallas kernels, on_device(): pl.pallas_call(functools.partial(spread_kernel, depth_total=depth_total),...  3.06 us
    pallas_call x1, Pallas kernels, on_device(): pl.pallas_call(compose_kernel, out_shape=(jax.ShapeDtypeStruct((3, band,...  1.85 us
  transfers between devices with their start and end apart: 7, of which 2 were waited for; matrix products, arithmetic and copies ran while one was open for 0% of the time, Pallas kernels for 11%

profile of v8, /device:TPU:14, one launch (start us, length us, event | category | flops | bytes accessed | tf_op | source)
XLA Modules:
  0.0 75.6 jit_solution(16643929428428060359)
XLA Ops:
  0.6 0.0 copy-start
  0.6 1.6 %copy-done = bf16[16,64,1024]{2,1,0:T(8,128)(2,1)S(1)} copy-done((bf16[16,64,1024]{2,1,0:T(8,128)(2,1)S(1)}, bf16[16,64,1024]{2,1,0:T(8,128)(2,1)}, u32[]{:S(2)}) %copy-start) | copy-done | bytes 2097176
  2.2 0.3 edges.1
  2.6 4.0 %collective-permute-start.4 = (bf16[64,1024]{1,0:T(8,128)(2,1)S(1)}, bf16[64,1024]{1,0:T(8,128)(2,1)S(1)}, u32[]{:S(2)}, u32[]{:S(2)}) collective-permute-start(bf16[64,1024]{1,0:T(8,128)(2,1)S(1)} %get-tuple-element.21), channel_id=1, source_target_pairs={{0,1},{2,3},{4,5},{6,7},{8,9},{10,11},{12,13},{14,15},{1,0},{3,2},... | collective-permute-start | bytes 393224 | tf_op jit(solution)/shard_map/ppermute | solution.py:376
  6.5 0.7 collective-permute-start.5
  7.2 1.9 %collective-permute-start = (bf16[16,1024]{1,0:T(8,128)(2,1)S(1)}, bf16[16,1024]{1,0:T(8,128)(2,1)S(1)}, u32[]{:S(2)}, u32[]{:S(2)}) collective-permute-start(bf16[16,1024]{1,0:T(8,128)(2,1)S(1)} %get-tuple-element.18), channel_id=1, source_target_pairs={{0,64},{128,192},{256,320},{384,448},{64,0},{192,128},{320,256},{4... | collective-permute-start | bytes 98312 | tf_op jit(solution)/shard_map/ppermute | solution.py:376
  9.1 2.5 %collective-permute-start.1 = (bf16[16,1024]{1,0:T(8,128)(2,1)S(1)}, bf16[16,1024]{1,0:T(8,128)(2,1)S(1)}, u32[]{:S(2)}, u32[]{:S(2)}) collective-permute-start(bf16[16,1024]{1,0:T(8,128)(2,1)S(1)} %get-tuple-element.19), channel_id=1, source_target_pairs={{64,128},{192,256},{320,384},{128,64},{256,192},{384,320},{65,129}... | collective-permute-start | bytes 98312 | tf_op jit(solution)/shard_map/ppermute | solution.py:376
  11.6 2.7 %collective-permute-start.3 = (f32[64,128]{1,0:T(8,128)S(1)}, f32[64,128]{1,0:T(8,128)S(1)}, u32[]{:S(2)}, u32[]{:S(2)}) collective-permute-start(f32[64,128]{1,0:T(8,128)S(1)} %get-tuple-element.20), channel_id=1, source_target_pairs={{16,0},{32,16},{48,32},{17,1},{33,17},{49,33},{18,2},{34,18},{50,3... | collective-permute-start | bytes 98312 | tf_op jit(solution)/shard_map/ppermute | solution.py:385
  14.4 0.0 collective-permute-done.x_first
  14.4 1.3 %collective-permute-start.2 = (f32[64,128]{1,0:T(8,128)S(1)}, f32[64,128]{1,0:T(8,128)S(1)}, u32[]{:S(2)}, u32[]{:S(2)}) collective-permute-start(f32[64,128]{1,0:T(8,128)S(1)} %get-tuple-element.20), channel_id=1, source_target_pairs={{0,16},{16,32},{32,48},{1,17},{17,33},{33,49},{2,18},{18,34},{34,5... | collective-permute-start | bytes 98312 | tf_op jit(solution)/shard_map/ppermute | solution.py:385
  15.7 0.0 copy-done.1
  15.7 3.1 %spread.1 = (f32[8,16,72,128]{3,2,1,0:T(8,128)S(1)}, f32[8,16,72,128]{3,2,1,0:T(8,128)S(1)}, f32[41,8,128]{2,1,0:T(8,128)S(1)}) custom-call(s32[8]{0:T(128)S(1)} %copy-done.4, f32[3,8]{1,0:T(4,128)S(1)} %copy-done.3, f32[8]{0:T(128)S(1)} %copy-done.5, bf16[16,64,1024]{2,1,0:T(8,128)(2,1)S(1)} %copy-done.1), custom_call_target="tpu_custom_call" | custom-call | flops 8388608 | bytes 2097152 | tf_op jit(solution)/shard_map/spread/pallas_call | solution.py:434
  18.8 0.0 collective-permute-done.1.x_second
  18.8 0.0 collective-permute-done.3.y_after
  18.8 1.6 %collective-permute-done.2.y_before = f32[64,128]{1,0:T(8,128)S(1)} collective-permute-done((f32[64,128]{1,0:T(8,128)S(1)}, f32[64,128]{1,0:T(8,128)S(1)}, u32[]{:S(2)}, u32[]{:S(2)}) %collective-permute-start.2) | collective-permute-done | bytes 32800 | tf_op jit(solution)/shard_map/ppermute | solution.py:385
  20.4 0.0 collective-permute-done.4.z_first
  20.4 0.0 collective-permute-done.5.z_second
  20.4 5.6 %theirs.1 = (s32[8,8,8,128]{3,2,1,0:T(8,128)S(1)}, f32[8,16,72,128]{3,2,1,0:T(8,128)S(1)}, f32[8,16,72,128]{3,2,1,0:T(8,128)S(1)}, f32[2,8,72,128]{3,2,1,0:T(8,128)S(1)}) custom-call(f32[41,8,128]{2,1,0:T(8,128)S(1)} %get-tuple-element.15.consts, f32[8,16,72,128]{3,2,1,0:T(8,128)S(1)} %get-tuple-element.16.cells_in, ...), custom_call_target="tpu_custom_call", output_to_operand_aliasing={{1}: (1, {}), {2}: (2, {})} | custom-call | flops 67108864 | bytes 8388608 | tf_op jit(solution)/shard_map/theirs/pallas_call | solution.py:444
  26.1 7.0 %collective-permute-start.6 = (s32[8,8,8,128]{3,2,1,0:T(8,128)S(1)}, s32[8,8,8,128]{3,2,1,0:T(8,128)S(1)}, u32[]{:S(2)}, u32[]{:S(2)}) collective-permute-start(s32[8,8,8,128]{3,2,1,0:T(8,128)S(1)} %get-tuple-element.27), channel_id=1, source_target_pairs={{0,1},{1,0},{2,3},{3,2},{4,5},{5,4},{6,7},{7,6},{8,9},{9,8},{10,11... | collective-permute-start | bytes 786440 | tf_op jit(solution)/shard_map/ppermute | solution.py:459
  33.0 5.3 %ours.1 = (f32[16,8,8,128]{3,2,1,0:T(8,128)S(1)}, f32[8,16,72,128]{3,2,1,0:T(8,128)S(1)}, f32[8,16,72,128]{3,2,1,0:T(8,128)S(1)}) custom-call(f32[41,8,128]{2,1,0:T(8,128)S(1)} %get-tuple-element.15.consts, f32[8,16,72,128]{3,2,1,0:T(8,128)S(1)} %get-tuple-element.23.cells_in, ...), custom_call_target="tpu_custom_call", output_to_operand_aliasing={{1}: (1, {}), {2}: (2, {})} | custom-call | flops 67108864 | bytes 8388608 | tf_op jit(solution)/shard_map/ours/pallas_call | solution.py:460
  38.3 1.2 %collective-permute-done.6.theirs_ref = s32[8,8,8,128]{3,2,1,0:T(8,128)S(1)} collective-permute-done((s32[8,8,8,128]{3,2,1,0:T(8,128)S(1)}, s32[8,8,8,128]{3,2,1,0:T(8,128)S(1)}, u32[]{:S(2)}, u32[]{:S(2)}) %collective-permute-start.6) | collective-permute-done | bytes 262176 | tf_op jit(solution)/shard_map/ppermute | solution.py:459
  39.5 0.6 pair.1
  40.1 33.7 %all_to_all.5.pieces_ref = s32[8,64,128]{2,1,0:T(8,128)} all-to-all(s32[8,64,128]{2,1,0:T(8,128)S(1)} %bitcast.1), channel_id=1, replica_groups={{0,2,4,6,8,10,12,14},{1,3,5,7,9,11,13,15},{16,18,20,22,24,26,28,30},{17..., dimensions={0} | all-to-all | bytes 524288 | tf_op jit(solution)/shard_map/all_to_all | solution.py:479
  73.7 1.8 %compose.1 = (f32[3,4,1024]{2,1,0:T(4,128)}, f32[4,1024]{1,0:T(4,128)}) custom-call(f32[41,8,128]{2,1,0:T(8,128)} %copy-done.2, s32[8,64,128]{2,1,0:T(8,128)} %all_to_all.5.pieces_ref), custom_call_target="tpu_custom_call" | custom-call | tf_op jit(solution)/shard_map/compose/pallas_call | solution.py:488
  (9 shorter events, 0.0 us)
Async XLA Ops:
  0.6 1.6 %copy-start = (bf16[16,64,1024]{2,1,0:T(8,128)(2,1)S(1)}, bf16[16,64,1024]{2,1,0:T(8,128)(2,1)}, u32[]{:S(2)}) copy-start(bf16[16,64,1024]{2,1,0:T(8,128)(2,1)} %z_high.1) | copy-start | bytes 6291460
  2.2 13.4 %copy-start.1 = (bf16[16,64,1024]{2,1,0:T(8,128)(2,1)S(1)}, bf16[16,64,1024]{2,1,0:T(8,128)(2,1)}, u32[]{:S(2)}) copy-start(bf16[16,64,1024]{2,1,0:T(8,128)(2,1)} %z_high.1) | copy-start | bytes 6291460
  2.2 13.5 %copy-start.3 = (f32[3,8]{1,0:T(4,128)S(1)}, f32[3,8]{1,0:T(4,128)}, u32[]{:S(2)}) copy-start(f32[3,8]{1,0:T(4,128)} %colour_ref.1) | copy-start | bytes 292
  2.2 13.5 %copy-start.4 = (s32[8]{0:T(128)S(1)}, s32[8]{0:T(128)}, u32[]{:S(2)}) copy-start(s32[8]{0:T(128)} %knots_ref.1) | copy-start | bytes 100
  2.2 13.5 %copy-start.5 = (f32[8]{0:T(128)S(1)}, f32[8]{0:T(128)}, u32[]{:S(2)}) copy-start(f32[8]{0:T(128)} %density_ref.1) | copy-start | bytes 100
  2.6 17.9 %collective-permute-start.4 = (bf16[64,1024]{1,0:T(8,128)(2,1)S(1)}, bf16[64,1024]{1,0:T(8,128)(2,1)S(1)}, u32[]{:S(2)}, u32[]{:S(2)}) collective-permute-start(bf16[64,1024]{1,0:T(8,128)(2,1)S(1)} %get-tuple-element.21), channel_id=1, source_target_pairs={{0,1},{2,3},{4,5},{6,7},{8,9},{10,11},{12,13},{14,15},{1,0},{3,2},... | collective-permute-start | bytes 393224 | tf_op jit(solution)/shard_map/ppermute | solution.py:376
  6.5 13.9 %collective-permute-start.5 = (bf16[64,1024]{1,0:T(8,128)(2,1)S(1)}, bf16[64,1024]{1,0:T(8,128)(2,1)S(1)}, u32[]{:S(2)}, u32[]{:S(2)}) collective-permute-start(bf16[64,1024]{1,0:T(8,128)(2,1)S(1)} %get-tuple-element.22), channel_id=1, source_target_pairs={{1,2},{3,4},{5,6},{7,8},{9,10},{11,12},{13,14},{2,1},{4,3},{6,5},{... | collective-permute-start | bytes 393224 | tf_op jit(solution)/shard_map/ppermute | solution.py:376
  7.2 7.1 %collective-permute-start = (bf16[16,1024]{1,0:T(8,128)(2,1)S(1)}, bf16[16,1024]{1,0:T(8,128)(2,1)S(1)}, u32[]{:S(2)}, u32[]{:S(2)}) collective-permute-start(bf16[16,1024]{1,0:T(8,128)(2,1)S(1)} %get-tuple-element.18), channel_id=1, source_target_pairs={{0,64},{128,192},{256,320},{384,448},{64,0},{192,128},{320,256},{4... | collective-permute-start | bytes 98312 | tf_op jit(solution)/shard_map/ppermute | solution.py:376
  9.1 9.6 %collective-permute-start.1 = (bf16[16,1024]{1,0:T(8,128)(2,1)S(1)}, bf16[16,1024]{1,0:T(8,128)(2,1)S(1)}, u32[]{:S(2)}, u32[]{:S(2)}) collective-permute-start(bf16[16,1024]{1,0:T(8,128)(2,1)S(1)} %get-tuple-element.19), channel_id=1, source_target_pairs={{64,128},{192,256},{320,384},{128,64},{256,192},{384,320},{65,129}... | collective-permute-start | bytes 98312 | tf_op jit(solution)/shard_map/ppermute | solution.py:376
  11.6 7.2 %collective-permute-start.3 = (f32[64,128]{1,0:T(8,128)S(1)}, f32[64,128]{1,0:T(8,128)S(1)}, u32[]{:S(2)}, u32[]{:S(2)}) collective-permute-start(f32[64,128]{1,0:T(8,128)S(1)} %get-tuple-element.20), channel_id=1, source_target_pairs={{16,0},{32,16},{48,32},{17,1},{33,17},{49,33},{18,2},{34,18},{50,3... | collective-permute-start | bytes 98312 | tf_op jit(solution)/shard_map/ppermute | solution.py:385
  14.4 6.0 %collective-permute-start.2 = (f32[64,128]{1,0:T(8,128)S(1)}, f32[64,128]{1,0:T(8,128)S(1)}, u32[]{:S(2)}, u32[]{:S(2)}) collective-permute-start(f32[64,128]{1,0:T(8,128)S(1)} %get-tuple-element.20), channel_id=1, source_target_pairs={{0,16},{16,32},{32,48},{1,17},{17,33},{33,49},{2,18},{18,34},{34,5... | collective-permute-start | bytes 98312 | tf_op jit(solution)/shard_map/ppermute | solution.py:385
  18.8 14.3 %copy-start.2 = (f32[41,8,128]{2,1,0:T(8,128)}, f32[41,8,128]{2,1,0:T(8,128)S(1)}, u32[]{:S(2)}) copy-start(f32[41,8,128]{2,1,0:T(8,128)S(1)} %get-tuple-element.15.consts) | copy-start | bytes 503812
  26.1 13.4 %collective-permute-start.6 = (s32[8,8,8,128]{3,2,1,0:T(8,128)S(1)}, s32[8,8,8,128]{3,2,1,0:T(8,128)S(1)}, u32[]{:S(2)}, u32[]{:S(2)}) collective-permute-start(s32[8,8,8,128]{3,2,1,0:T(8,128)S(1)} %get-tuple-element.27), channel_id=1, source_target_pairs={{0,1},{1,0},{2,3},{3,2},{4,5},{5,4},{6,7},{7,6},{8,9},{9,8},{10,11... | collective-permute-start | bytes 786440 | tf_op jit(solution)/shard_map/ppermute | solution.py:459

commit v9 on v8

--- a/solution.py
+++ b/solution.py
@@ -65,7 +65,7 @@
     return lax.rem(lax.axis_index(axis), 2) == 0
 
 
-def edges_kernel(x_low, x_high, y_low, y_high, z_low, z_high, x_first, x_second, y_out, z_first, z_second, rows_x):
+def edges_kernel(x_low, x_high, y_low, y_high, z_low, z_high, x_first, x_second, y_out, z_first, z_second, rows_x, cols_y):
     depth = x_low.shape[0]
     even_x, even_z = is_even("gx"), is_even("gz")
     for z in range(depth):
@@ -87,7 +87,8 @@
                 sides[part] = jnp.where(lane == z, low[at, :1], sides[part])
                 sides[part] = jnp.where(lane == depth + z, high[at, LANES - 1:], sides[part])
         for part in range(2):
-            y_out[pl.ds(2 * i + part, SUB, stride=GROUPS), :] = sides[part]
+            cols_y[pl.ds(2 * i + part, SUB, stride=GROUPS), :] = sides[part]
+    y_out[...] = cols_y[...].astype(y_out.dtype)
 
     @pl.when(even_z)
     def _():
@@ -204,9 +205,11 @@
                 sides[side, t, slots_of(2 * c + part), :] = plane[8 * part:8 * part + 8, lanes_of(t)]
 
 
-def place_edges(cells, grads, x_first, x_second, y_before, y_after, parity):
+def place_edges(cells, grads, x_first, x_second, y_before, y_after, columns, parity):
     tiles, depth = cells.shape[:2]
     slot = jnp.where(parity == 0, ABOVE, BELOW)
+    columns[0] = y_before[...].astype(jnp.float32)
+    columns[1] = y_after[...].astype(jnp.float32)
     second = (parity == 0) == is_even("gx")
     edge = jnp.where(second, x_second[...].astype(jnp.float32), x_first[...].astype(jnp.float32))
     for z in range(depth):
@@ -218,7 +221,7 @@
         r = 4 * parity + j
         rows = pl.ds(pl.multiple_of(SUB * r, SUB), SUB)
         at = pl.ds(PITCH * r, SUB)
-        before, after = y_before[rows, :], y_after[rows, :]
+        before, after = columns[0, rows, :], columns[1, rows, :]
         for z in range(depth):
             first = jnp.where(lane == 0, before[:, depth + z:depth + z + 1], 0.0)
             last = jnp.where(lane == LANES - 1, after[:, z:z + 1], 0.0)
@@ -280,13 +283,13 @@
 
 def theirs_kernel(
     consts, cells_in, grads_in, x_first, x_second, y_before, y_after, z_first, z_second,
-    out_ref, cells, grads, sides, *, depth_total,
+    out_ref, cells, grads, sides, columns, *, depth_total,
 ):
     parity = 1 - my_parity()
     before = jnp.where(is_even("gz"), 1, 0)
     spread_side(z_first, sides, before)
     spread_side(z_second, sides, 1 - before)
-    place_edges(cells, grads, x_first, x_second, y_before, y_after, parity)
+    place_edges(cells, grads, x_first, x_second, y_before, y_after, columns, parity)
 
     def store(t, j, values):
         first, second = pack(values)
@@ -298,10 +301,10 @@
 
 def ours_kernel(
     consts, cells_in, grads_in, x_first, x_second, y_before, y_after, sides,
-    out_ref, cells, grads, *, depth_total,
+    out_ref, cells, grads, columns, *, depth_total,
 ):
     parity = my_parity()
-    place_edges(cells, grads, x_first, x_second, y_before, y_after, parity)
+    place_edges(cells, grads, x_first, x_second, y_before, y_after, columns, parity)
 
     def store(t, j, values):
         for c in range(4):
@@ -408,7 +411,7 @@
         out_shape=(
             jax.ShapeDtypeStruct((depth, cols), volume.dtype),
             jax.ShapeDtypeStruct((depth, cols), volume.dtype),
-            jax.ShapeDtypeStruct((rows, LANES), f32),
+            jax.ShapeDtypeStruct((rows, LANES), volume.dtype),
             jax.ShapeDtypeStruct((rows, cols), volume.dtype),
             jax.ShapeDtypeStruct((rows, cols), volume.dtype),
         ),
@@ -421,7 +424,7 @@
             pl.BlockSpec((1, rows, cols), lambda n: (depth - 1, 0, 0)),
         ],
         out_specs=(whole(depth, cols), whole(depth, cols), whole(rows, LANES), whole(rows, cols), whole(rows, cols)),
-        scratch_shapes=[pltpu.VMEM((2, depth, cols), f32)],
+        scratch_shapes=[pltpu.VMEM((2, depth, cols), f32), pltpu.VMEM((rows, LANES), f32)],
         compiler_params=params,
         cost_estimate=cost(1 << 20, 2 << 20),
         name="edges",
@@ -452,6 +455,7 @@
         in_specs=[vmem] * 9,
         out_specs=(vmem,) * 4,
         input_output_aliases={1: 1, 2: 2},
+        scratch_shapes=[pltpu.VMEM((2, rows, LANES), f32)],
         compiler_params=params,
         cost_estimate=work,
         name="theirs",
@@ -463,6 +467,7 @@
         in_specs=[vmem] * 8,
         out_specs=(vmem,) * 3,
         input_output_aliases={1: 1, 2: 2},
+        scratch_shapes=[pltpu.VMEM((2, rows, LANES), f32)],
         compiler_params=params,
         cost_estimate=work,
         name="ours",

time: 75.9 us -> 75.8 us (level)
  the two profiles are of different devices: /device:TPU:14 before, /device:TPU:42 now
where the time goes in v9:
time: 75.8 us; the launch traced here: 75.4 us
  blocking collectives  32.6 us (43%)
  starting transfers between devices  20.1 us (27%)
  Pallas kernels  16.7 us (22%)
  waiting for transfers between devices  3.64 us (5%)
  local copies, waits for them, and re-layouts  1.6 us (2%)
  between operations  0.79 us (1%)
    all_to_all x1, blocking collectives, on_device(): lax.all_to_all(codes.reshape(half, tiles * SUB, LANES), 'gz', split_axis=...  32.6 us
    ppermute x4, starting transfers between devices, swap(): return lax.ppermute(edge, axis, pairs + [(j, i) for i, j in pairs])  13.8 us
    pallas_call x1, Pallas kernels, on_device(): pl.pallas_call(functools.partial(theirs_kernel, depth_total=depth_total),...  5.61 us
    pallas_call x1, Pallas kernels, on_device(): pl.pallas_call(functools.partial(ours_kernel, depth_total=depth_total), o...  5.25 us
    ppermute x2, starting transfers between devices, shift_both(): return (lax.ppermute(edges, axis, up), lax.ppermute(edges, axis, down))  4.36 us
    pallas_call x1, Pallas kernels, on_device(): pl.pallas_call(functools.partial(spread_kernel, depth_total=depth_total),...  3.06 us
    ppermute x1, waiting for transfers between devices, on_device(): arrived = lax.ppermute(theirs, 'gz', [(i, i ^ 1) for i in range(count)])  3.04 us
    ppermute x1, starting transfers between devices, on_device(): arrived = lax.ppermute(theirs, 'gz', [(i, i ^ 1) for i in range(count)])  1.92 us
  transfers between devices with their start and end apart: 7, of which 2 were waited for; matrix products, arithmetic and copies ran while one was open for 0% of the time, Pallas kernels for 11%

profile of v9, /device:TPU:42, one launch (start us, length us, event | category | flops | bytes accessed | tf_op | source)
XLA Modules:
  0.0 75.4 jit_solution(12764994060221714615)
XLA Ops:
  0.6 0.0 copy-start
  0.6 1.6 %copy-done = bf16[16,64,1024]{2,1,0:T(8,128)(2,1)S(1)} copy-done((bf16[16,64,1024]{2,1,0:T(8,128)(2,1)S(1)}, bf16[16,64,1024]{2,1,0:T(8,128)(2,1)}, u32[]{:S(2)}) %copy-start) | copy-done | bytes 2097176
  2.2 0.3 edges.1
  2.6 2.1 %collective-permute-start.4 = (bf16[64,1024]{1,0:T(8,128)(2,1)S(1)}, bf16[64,1024]{1,0:T(8,128)(2,1)S(1)}, u32[]{:S(2)}, u32[]{:S(2)}) collective-permute-start(bf16[64,1024]{1,0:T(8,128)(2,1)S(1)} %get-tuple-element.21), channel_id=1, source_target_pairs={{0,1},{2,3},{4,5},{6,7},{8,9},{10,11},{12,13},{14,15},{1,0},{3,2},... | collective-permute-start | bytes 393224 | tf_op jit(solution)/shard_map/ppermute | solution.py:379
  4.7 5.6 %collective-permute-start.5 = (bf16[64,1024]{1,0:T(8,128)(2,1)S(1)}, bf16[64,1024]{1,0:T(8,128)(2,1)S(1)}, u32[]{:S(2)}, u32[]{:S(2)}) collective-permute-start(bf16[64,1024]{1,0:T(8,128)(2,1)S(1)} %get-tuple-element.22), channel_id=1, source_target_pairs={{1,2},{3,4},{5,6},{7,8},{9,10},{11,12},{13,14},{2,1},{4,3},{6,5},{... | collective-permute-start | bytes 393224 | tf_op jit(solution)/shard_map/ppermute | solution.py:379
  10.4 2.4 %collective-permute-start.3 = (bf16[64,128]{1,0:T(8,128)(2,1)S(1)}, bf16[64,128]{1,0:T(8,128)(2,1)S(1)}, u32[]{:S(2)}, u32[]{:S(2)}) collective-permute-start(bf16[64,128]{1,0:T(8,128)(2,1)S(1)} %get-tuple-element.20), channel_id=1, source_target_pairs={{16,0},{32,16},{48,32},{17,1},{33,17},{49,33},{18,2},{34,18},{50,3... | collective-permute-start | bytes 49160 | tf_op jit(solution)/shard_map/ppermute | solution.py:388
  12.8 1.9 %collective-permute-start = (bf16[16,1024]{1,0:T(8,128)(2,1)S(1)}, bf16[16,1024]{1,0:T(8,128)(2,1)S(1)}, u32[]{:S(2)}, u32[]{:S(2)}) collective-permute-start(bf16[16,1024]{1,0:T(8,128)(2,1)S(1)} %get-tuple-element.18), channel_id=1, source_target_pairs={{0,64},{128,192},{256,320},{384,448},{64,0},{192,128},{320,256},{4... | collective-permute-start | bytes 98312 | tf_op jit(solution)/shard_map/ppermute | solution.py:379
  14.8 4.1 %collective-permute-start.1 = (bf16[16,1024]{1,0:T(8,128)(2,1)S(1)}, bf16[16,1024]{1,0:T(8,128)(2,1)S(1)}, u32[]{:S(2)}, u32[]{:S(2)}) collective-permute-start(bf16[16,1024]{1,0:T(8,128)(2,1)S(1)} %get-tuple-element.19), channel_id=1, source_target_pairs={{64,128},{192,256},{320,384},{128,64},{256,192},{384,320},{65,129}... | collective-permute-start | bytes 98312 | tf_op jit(solution)/shard_map/ppermute | solution.py:379
  18.9 0.0 collective-permute-done.3.y_after
  18.9 1.9 %collective-permute-start.2 = (bf16[64,128]{1,0:T(8,128)(2,1)S(1)}, bf16[64,128]{1,0:T(8,128)(2,1)S(1)}, u32[]{:S(2)}, u32[]{:S(2)}) collective-permute-start(bf16[64,128]{1,0:T(8,128)(2,1)S(1)} %get-tuple-element.20), channel_id=1, source_target_pairs={{0,16},{16,32},{32,48},{1,17},{17,33},{33,49},{2,18},{18,34},{34,5... | collective-permute-start | bytes 49160 | tf_op jit(solution)/shard_map/ppermute | solution.py:388
  20.8 0.0 copy-done.1
  20.9 3.1 %spread.1 = (f32[8,16,72,128]{3,2,1,0:T(8,128)S(1)}, f32[8,16,72,128]{3,2,1,0:T(8,128)S(1)}, f32[41,8,128]{2,1,0:T(8,128)S(1)}) custom-call(s32[8]{0:T(128)S(1)} %copy-done.4, f32[3,8]{1,0:T(4,128)S(1)} %copy-done.3, f32[8]{0:T(128)S(1)} %copy-done.5, bf16[16,64,1024]{2,1,0:T(8,128)(2,1)S(1)} %copy-done.1), custom_call_target="tpu_custom_call" | custom-call | flops 8388608 | bytes 2097152 | tf_op jit(solution)/shard_map/spread/pallas_call | solution.py:437
  23.9 0.6 collective-permute-done.2.y_before
  24.5 0.0 collective-permute-done.x_first
  24.5 0.0 collective-permute-done.1.x_second
  24.5 0.0 collective-permute-done.4.z_first
  24.5 0.0 collective-permute-done.5.z_second
  24.5 5.6 %theirs.1 = (s32[8,8,8,128]{3,2,1,0:T(8,128)S(1)}, f32[8,16,72,128]{3,2,1,0:T(8,128)S(1)}, f32[8,16,72,128]{3,2,1,0:T(8,128)S(1)}, f32[2,8,72,128]{3,2,1,0:T(8,128)S(1)}) custom-call(f32[41,8,128]{2,1,0:T(8,128)S(1)} %get-tuple-element.15.consts, f32[8,16,72,128]{3,2,1,0:T(8,128)S(1)} %get-tuple-element.16.cells_in, ...), custom_call_target="tpu_custom_call", output_to_operand_aliasing={{1}: (1, {}), {2}: (2, {})} | custom-call | flops 67108864 | bytes 8388608 | tf_op jit(solution)/shard_map/theirs/pallas_call | solution.py:447
  30.2 1.9 %collective-permute-start.6 = (s32[8,8,8,128]{3,2,1,0:T(8,128)S(1)}, s32[8,8,8,128]{3,2,1,0:T(8,128)S(1)}, u32[]{:S(2)}, u32[]{:S(2)}) collective-permute-start(s32[8,8,8,128]{3,2,1,0:T(8,128)S(1)} %get-tuple-element.27), channel_id=1, source_target_pairs={{0,1},{1,0},{2,3},{3,2},{4,5},{5,4},{6,7},{7,6},{8,9},{9,8},{10,11... | collective-permute-start | bytes 786440 | tf_op jit(solution)/shard_map/ppermute | solution.py:463
  32.1 5.3 %ours.1 = (f32[16,8,8,128]{3,2,1,0:T(8,128)S(1)}, f32[8,16,72,128]{3,2,1,0:T(8,128)S(1)}, f32[8,16,72,128]{3,2,1,0:T(8,128)S(1)}) custom-call(f32[41,8,128]{2,1,0:T(8,128)S(1)} %get-tuple-element.15.consts, f32[8,16,72,128]{3,2,1,0:T(8,128)S(1)} %get-tuple-element.23.cells_in, ...), custom_call_target="tpu_custom_call", output_to_operand_aliasing={{1}: (1, {}), {2}: (2, {})} | custom-call | flops 67108864 | bytes 8388608 | tf_op jit(solution)/shard_map/ours/pallas_call | solution.py:464
  37.4 3.0 %collective-permute-done.6.theirs_ref = s32[8,8,8,128]{3,2,1,0:T(8,128)S(1)} collective-permute-done((s32[8,8,8,128]{3,2,1,0:T(8,128)S(1)}, s32[8,8,8,128]{3,2,1,0:T(8,128)S(1)}, u32[]{:S(2)}, u32[]{:S(2)}) %collective-permute-start.6) | collective-permute-done | bytes 262176 | tf_op jit(solution)/shard_map/ppermute | solution.py:463
  40.4 0.6 pair.1
  41.0 32.6 %all_to_all.5.pieces_ref = s32[8,64,128]{2,1,0:T(8,128)} all-to-all(s32[8,64,128]{2,1,0:T(8,128)S(1)} %bitcast.1), channel_id=1, replica_groups={{0,2,4,6,8,10,12,14},{1,3,5,7,9,11,13,15},{16,18,20,22,24,26,28,30},{17..., dimensions={0} | all-to-all | bytes 524288 | tf_op jit(solution)/shard_map/all_to_all | solution.py:484
  73.6 1.8 %compose.1 = (f32[3,4,1024]{2,1,0:T(4,128)}, f32[4,1024]{1,0:T(4,128)}) custom-call(f32[41,8,128]{2,1,0:T(8,128)} %copy-done.2, s32[8,64,128]{2,1,0:T(8,128)} %all_to_all.5.pieces_ref), custom_call_target="tpu_custom_call" | custom-call | tf_op jit(solution)/shard_map/compose/pallas_call | solution.py:493
  (9 shorter events, 0.0 us)
Async XLA Ops:
  0.6 1.6 %copy-start = (bf16[16,64,1024]{2,1,0:T(8,128)(2,1)S(1)}, bf16[16,64,1024]{2,1,0:T(8,128)(2,1)}, u32[]{:S(2)}) copy-start(bf16[16,64,1024]{2,1,0:T(8,128)(2,1)} %z_high.1) | copy-start | bytes 6291460
  2.2 18.6 %copy-start.1 = (bf16[16,64,1024]{2,1,0:T(8,128)(2,1)S(1)}, bf16[16,64,1024]{2,1,0:T(8,128)(2,1)}, u32[]{:S(2)}) copy-start(bf16[16,64,1024]{2,1,0:T(8,128)(2,1)} %z_high.1) | copy-start | bytes 6291460
  2.2 18.6 %copy-start.3 = (f32[3,8]{1,0:T(4,128)S(1)}, f32[3,8]{1,0:T(4,128)}, u32[]{:S(2)}) copy-start(f32[3,8]{1,0:T(4,128)} %colour_ref.1) | copy-start | bytes 292
  2.2 18.6 %copy-start.4 = (s32[8]{0:T(128)S(1)}, s32[8]{0:T(128)}, u32[]{:S(2)}) copy-start(s32[8]{0:T(128)} %knots_ref.1) | copy-start | bytes 100
  2.2 18.6 %copy-start.5 = (f32[8]{0:T(128)S(1)}, f32[8]{0:T(128)}, u32[]{:S(2)}) copy-start(f32[8]{0:T(128)} %density_ref.1) | copy-start | bytes 100
  2.6 21.9 %collective-permute-start.4 = (bf16[64,1024]{1,0:T(8,128)(2,1)S(1)}, bf16[64,1024]{1,0:T(8,128)(2,1)S(1)}, u32[]{:S(2)}, u32[]{:S(2)}) collective-permute-start(bf16[64,1024]{1,0:T(8,128)(2,1)S(1)} %get-tuple-element.21), channel_id=1, source_target_pairs={{0,1},{2,3},{4,5},{6,7},{8,9},{10,11},{12,13},{14,15},{1,0},{3,2},... | collective-permute-start | bytes 393224 | tf_op jit(solution)/shard_map/ppermute | solution.py:379
  4.7 19.8 %collective-permute-start.5 = (bf16[64,1024]{1,0:T(8,128)(2,1)S(1)}, bf16[64,1024]{1,0:T(8,128)(2,1)S(1)}, u32[]{:S(2)}, u32[]{:S(2)}) collective-permute-start(bf16[64,1024]{1,0:T(8,128)(2,1)S(1)} %get-tuple-element.22), channel_id=1, source_target_pairs={{1,2},{3,4},{5,6},{7,8},{9,10},{11,12},{13,14},{2,1},{4,3},{6,5},{... | collective-permute-start | bytes 393224 | tf_op jit(solution)/shard_map/ppermute | solution.py:379
  10.4 8.5 %collective-permute-start.3 = (bf16[64,128]{1,0:T(8,128)(2,1)S(1)}, bf16[64,128]{1,0:T(8,128)(2,1)S(1)}, u32[]{:S(2)}, u32[]{:S(2)}) collective-permute-start(bf16[64,128]{1,0:T(8,128)(2,1)S(1)} %get-tuple-element.20), channel_id=1, source_target_pairs={{16,0},{32,16},{48,32},{17,1},{33,17},{49,33},{18,2},{34,18},{50,3... | collective-permute-start | bytes 49160 | tf_op jit(solution)/shard_map/ppermute | solution.py:388
  12.8 11.7 %collective-permute-start = (bf16[16,1024]{1,0:T(8,128)(2,1)S(1)}, bf16[16,1024]{1,0:T(8,128)(2,1)S(1)}, u32[]{:S(2)}, u32[]{:S(2)}) collective-permute-start(bf16[16,1024]{1,0:T(8,128)(2,1)S(1)} %get-tuple-element.18), channel_id=1, source_target_pairs={{0,64},{128,192},{256,320},{384,448},{64,0},{192,128},{320,256},{4... | collective-permute-start | bytes 98312 | tf_op jit(solution)/shard_map/ppermute | solution.py:379
  14.8 9.8 %collective-permute-start.1 = (bf16[16,1024]{1,0:T(8,128)(2,1)S(1)}, bf16[16,1024]{1,0:T(8,128)(2,1)S(1)}, u32[]{:S(2)}, u32[]{:S(2)}) collective-permute-start(bf16[16,1024]{1,0:T(8,128)(2,1)S(1)} %get-tuple-element.19), channel_id=1, source_target_pairs={{64,128},{192,256},{320,384},{128,64},{256,192},{384,320},{65,129}... | collective-permute-start | bytes 98312 | tf_op jit(solution)/shard_map/ppermute | solution.py:379
  18.9 5.6 %collective-permute-start.2 = (bf16[64,128]{1,0:T(8,128)(2,1)S(1)}, bf16[64,128]{1,0:T(8,128)(2,1)S(1)}, u32[]{:S(2)}, u32[]{:S(2)}) collective-permute-start(bf16[64,128]{1,0:T(8,128)(2,1)S(1)} %get-tuple-element.20), channel_id=1, source_target_pairs={{0,16},{16,32},{32,48},{1,17},{17,33},{33,49},{2,18},{18,34},{34,5... | collective-permute-start | bytes 49160 | tf_op jit(solution)/shard_map/ppermute | solution.py:388
  23.9 8.2 %copy-start.2 = (f32[41,8,128]{2,1,0:T(8,128)}, f32[41,8,128]{2,1,0:T(8,128)S(1)}, u32[]{:S(2)}) copy-start(f32[41,8,128]{2,1,0:T(8,128)S(1)} %get-tuple-element.15.consts) | copy-start | bytes 503812
  30.2 10.2 %collective-permute-start.6 = (s32[8,8,8,128]{3,2,1,0:T(8,128)S(1)}, s32[8,8,8,128]{3,2,1,0:T(8,128)S(1)}, u32[]{:S(2)}, u32[]{:S(2)}) collective-permute-start(s32[8,8,8,128]{3,2,1,0:T(8,128)S(1)} %get-tuple-element.27), channel_id=1, source_target_pairs={{0,1},{1,0},{2,3},{3,2},{4,5},{5,4},{6,7},{7,6},{8,9},{9,8},{10,11... | collective-permute-start | bytes 786440 | tf_op jit(solution)/shard_map/ppermute | solution.py:463
